TPU v7x, 128 devices: a whole 4x4x4 slice. The times are simulated.
128 devices in a mesh: grp: 4 (over y), inner: 32 (over z, x, core).
Axes of the slice: x: 4, y: 4, z: 4, core: 2. Of those that a mesh axis runs over, the one named last changes fastest.
Arguments:
- amplitude: float32 [1024, 16384], P(('grp', 'inner')), may hold values from -6 to 6
- integrals: float32 [16384, 128, 128], P(('grp', 'inner')), may hold values from -0.09375 to 0.09375
- tile_owner: int32 [16384, 1], P(('grp', 'inner')), may hold values from 0 to 127; in each aligned block of 128 rows (0 to 127, 128 to 255, ...) at most 2 rows name the same one
- tile_row: int32 [16384], P(('grp', 'inner')), may hold values from 0 to 3
- tile_col: int32 [16384], P(('grp', 'inner')), may hold values from 0 to 127
Outputs:
- ladder: float32 [1024, 16384], P(('grp', 'inner'))
Inputs may be any that keep to these rules, and one draw needn't show every extreme that they name: `tile_owner`: among the 128 tiles of one device no owner is named more than 2 times, a bound that some block reaches.
All inputs are finite; a program needn't handle non-finite values.
Results may differ from a plain program's by a relative error of at most 0.0001.
Values sent between devices are 32-bit elements; how exact they have to be, the bound alone decides.
No kernel may reach another device: no remote copies, remote signals or barrier semaphores. Data moves between devices by JAX's collectives and lax.ppermute only.
A program may use at most 192 MiB of HBM per device.

v0:
```python
import functools

import jax
import jax.numpy as jnp
from jax import lax
from jax.experimental import pallas as pl
from jax.experimental.pallas import tpu as pltpu
from jax.sharding import PartitionSpec as P

TILE = 128
SLOTS = 40
FIRST = 30
VMEM = 24 * 1024 * 1024
AXES = ("grp", "inner")


def slow_part(amplitude, integrals, tile_owner, tile_row, tile_col):
    n_grp, n_inner = lax.axis_size("grp"), lax.axis_size("inner")
    devices = n_grp * n_inner
    count, size = integrals.shape[:2]
    blocks = amplitude.shape[1] // size
    per_dev = blocks // n_inner
    capacity = max(2, 2 * count // devices)
    owners = tile_owner[:, 0]
    order = jnp.arange(count, dtype=jnp.int32)
    same = (owners[:, None] == owners[None, :]) & (order[None, :] < order[:, None])
    slot = owners * capacity + jnp.sum(same.astype(jnp.int32), axis=1)
    position = (tile_row * blocks + tile_col).astype(jnp.float32)
    tiles = jnp.zeros((devices * capacity, size, size), jnp.float32).at[slot].set(integrals)
    place = jnp.zeros((devices * capacity,), jnp.float32).at[slot].set(position)
    tiles, place = (
        lax.all_to_all(tiles, AXES, split_axis=0, concat_axis=0, tiled=True),
        lax.all_to_all(place, AXES, split_axis=0, concat_axis=0, tiled=True),
    )
    dense = jnp.zeros((per_dev * blocks, size, size), jnp.float32).at[place.astype(jnp.int32)].add(tiles)
    dense = dense.reshape(per_dev, blocks, size, size).transpose(0, 2, 1, 3).reshape(per_dev * size, blocks * size)
    slab = lax.all_to_all(amplitude, "inner", split_axis=1, concat_axis=0, tiled=True)
    return lax.psum_scatter(
        jnp.dot(slab, dense, precision=lax.Precision.HIGHEST, preferred_element_type=jnp.float32),
        "inner",
        scatter_dimension=0,
        tiled=True,
    )


def pack_kernel(spans, total, index, tiles, *refs):
    outs, sems = refs[: len(spans)], refs[-1]
    for at, (which, lo, hi) in enumerate(spans):

        def issue(k, _):
            pltpu.make_async_copy(tiles.at[index[which * total + lo + k]], outs[at].at[k], sems.at[at]).start()
            return 0

        lax.fori_loop(0, hi - lo, issue, 0)
    for at, (_, lo, hi) in enumerate(spans):
        pltpu.make_async_copy(tiles.at[pl.ds(0, hi - lo)], outs[at], sems.at[at]).wait()


def pack(integrals, index, spans, total):
    return pl.pallas_call(
        functools.partial(pack_kernel, spans, total),
        out_shape=[jax.ShapeDtypeStruct((hi - lo, TILE, TILE), jnp.float32) for _, lo, hi in spans],
        in_specs=[pl.BlockSpec(memory_space=pltpu.SMEM), pl.BlockSpec(memory_space=pl.ANY)],
        out_specs=[pl.BlockSpec(memory_space=pltpu.VMEM)] * len(spans),
        scratch_shapes=[pltpu.SemaphoreType.DMA((len(spans),))],
        compiler_params=pltpu.CompilerParams(vmem_limit_bytes=16 * 2**20),
        cost_estimate=pl.CostEstimate(flops=0, bytes_accessed=1000, transcendentals=0),
    )(index, integrals)


def add_kernel(one, two, out):
    out[...] = one[...] + two[...]


def add(one, two):
    return pl.pallas_call(add_kernel, out_shape=jax.ShapeDtypeStruct(one.shape, one.dtype))(one, two)


def gate_kernel(*refs):
    pass


def gate(value, *after):
    any_spec = pl.BlockSpec(memory_space=pl.ANY)
    return pl.pallas_call(
        gate_kernel,
        out_shape=jax.ShapeDtypeStruct(value.shape, value.dtype),
        in_specs=[any_spec] * (1 + len(after)),
        out_specs=any_spec,
        input_output_aliases={0: 0},
        compiler_params=pltpu.CompilerParams(vmem_limit_bytes=2**17),
    )(value, *after)


def split(value):
    high = value.astype(jnp.bfloat16)
    return high, (value - high.astype(jnp.float32)).astype(jnp.bfloat16)


def arrange_kernel(where, amp, out, sem):
    z, x = where[0], where[1]
    for sx in range(4):
        for sz in range(4):
            source = lax.rem(z + sz, 4) * 4 + lax.rem(x + sx, 4)
            pltpu.make_async_copy(amp.at[source], out.at[sx * 4 + sz], sem).start()
    pltpu.make_async_copy(amp, out, sem).wait()


def arrange(where, amp):
    return pl.pallas_call(
        arrange_kernel,
        out_shape=pltpu.VMEM(amp.shape, amp.dtype),
        in_specs=[pl.BlockSpec(memory_space=pltpu.SMEM), pl.BlockSpec(memory_space=pl.ANY)],
        out_specs=pl.BlockSpec(memory_space=pltpu.VMEM),
        scratch_shapes=[pltpu.SemaphoreType.DMA],
        compiler_params=pltpu.CompilerParams(vmem_limit_bytes=2**20),
        cost_estimate=pl.CostEstimate(flops=0, bytes_accessed=1000, transcendentals=0),
    )(where, amp)


def ladder_kernel(counts, blocks, first, last, *refs):
    refs, lists = list(refs), len(counts)
    code, amp_v = refs[:2]
    del refs[:2]
    acc_v = None if first else refs.pop(0)
    tiles = refs[:lists]
    del refs[:lists]
    if last:
        parts = [refs.pop(0) for _ in range(10)]
    else:
        acc_v = refs.pop(0)
        token = refs.pop(0)
        token[...] = jnp.zeros_like(token)
    tile_v = refs[:lists]
    tile_sem, out_sem = refs[lists:]

    copies = [pltpu.make_async_copy(tiles[k], tile_v[k], tile_sem.at[k]) for k in range(lists)]
    for copy in copies:
        copy.start()
    if first:
        acc_v[...] = jnp.zeros_like(acc_v)

    for k in range(lists):
        copies[k].wait()
        base = sum(counts[:k])

        def pair(j, _):
            places = [code[base + 2 * j], code[base + 2 * j + 1]]

            @pl.when(jnp.maximum(*places) >= 0)
            def _():
                terms = []
                for half, place in enumerate(places):
                    held = jnp.maximum(place, 0)
                    row = pl.multiple_of((held // blocks) * TILE, TILE)
                    col = pl.multiple_of(lax.rem(held, blocks) * TILE, TILE)
                    a_hi, a_lo = split(amp_v[:, :, pl.ds(row, TILE)].reshape(16 * 8, TILE))
                    t_hi, t_lo = split(jnp.where(place >= 0, tile_v[k][2 * j + half], 0.0))
                    left = jnp.concatenate([a_hi, a_lo], axis=1)
                    right = jnp.concatenate([t_hi, t_lo], axis=1)
                    both = jnp.dot(left, jnp.concatenate([right, right], axis=0), preferred_element_type=jnp.float32)
                    terms.append((col, (both[:, :TILE] + both[:, TILE:]).reshape(4, 4, 8, TILE)))
                for col, term in terms:
                    acc_v[:, :, :, pl.ds(col, TILE)] += term

            return 0

        lax.fori_loop(0, counts[k] // 2, pair, 0)

    if last:
        half = blocks * TILE // 2
        one, two = pl.ds(0, half), pl.ds(half, half)
        sources = [acc_v.at[2, pl.ds(0, 2), :, one], acc_v.at[2, pl.ds(2, 2), :, one]]
        sources += [acc_v.at[pl.ds(0, 2), 2, :, two], acc_v.at[pl.ds(2, 2), 2, :, two]]
        sources += [acc_v.at[s, :, :, one] for s in (1, 3, 0)] + [acc_v.at[:, s, :, two] for s in (1, 3, 0)]
        done = [pltpu.make_async_copy(source, part, out_sem.at[i]) for i, (source, part) in enumerate(zip(sources, parts))]
        for copy in done:
            copy.start()
        for copy in done:
            copy.wait()


def keep(value):
    return pltpu.with_memory_space_constraint(value, pltpu.VMEM)


def ladder(code, amp, acc, tiles, last, blocks):
    counts = tuple(t.shape[0] for t in tiles)
    any_spec, smem, vmem = [pl.BlockSpec(memory_space=m) for m in (pl.ANY, pltpu.SMEM, pltpu.VMEM)]
    held = [] if acc is None else [acc]
    if last:
        shapes = [pltpu.HBM((n, 8, blocks * TILE // 2), jnp.float32) for n in (2,) * 4 + (4,) * 6]
    else:
        shapes = [pltpu.VMEM((4, 4, 8, blocks * TILE), jnp.float32), jax.ShapeDtypeStruct((8, TILE), jnp.float32)]
    return pl.pallas_call(
        functools.partial(ladder_kernel, counts, blocks, acc is None, last),
        out_shape=shapes,
        in_specs=[smem, vmem] + [vmem] * len(held) + [any_spec] * len(tiles),
        out_specs=[any_spec] * len(shapes) if last else [vmem, vmem],
        scratch_shapes=[
            *[pltpu.VMEM((n, TILE, TILE), jnp.float32) for n in counts],
            pltpu.SemaphoreType.DMA((len(tiles),)),
            pltpu.SemaphoreType.DMA((10,)),
        ],
        input_output_aliases={2: 0} if held and not last else {},
        compiler_params=pltpu.CompilerParams(vmem_limit_bytes=VMEM),
        cost_estimate=pl.CostEstimate(flops=0, bytes_accessed=1000, transcendentals=0),
    )(code, keep(amp), *[keep(h) for h in held], *tiles)


def per_device(amplitude, integrals, tile_owner, tile_row, tile_col):
    n_grp, n_inner = lax.axis_size("grp"), lax.axis_size("inner")
    devices = n_grp * n_inner
    rows, width = amplitude.shape
    count = integrals.shape[0]
    blocks = width // TILE
    per_dev = blocks // n_inner
    total = SLOTS
    grp, inner = lax.axis_index("grp"), lax.axis_index("inner")
    z, x, core = inner // 8, (inner // 2) % 4, inner % 2

    def at(z, x, core):
        return (z % 4) * 8 + (x % 4) * 2 + core

    every = [(a, b, c) for a in range(4) for b in range(4) for c in range(2)]
    along_x = {s: [(at(a, b, c), at(a, b + s, c)) for a, b, c in every] for s in (1, 2, 3)}
    along_z = {s: [(at(a, b, c), at(a + s, b, c)) for a, b, c in every] for s in (1, 2, 3)}
    along_y = {s: [(i, (i + s) % n_grp) for i in range(n_grp)] for s in (1, 2, 3)}
    across = [(i, i ^ 1) for i in range(n_inner)]
    same_core = [[at(a, b, c) for a in range(4) for b in range(4)] for c in range(2)]

    amp = lax.all_gather(amplitude, "inner", axis=0, axis_index_groups=same_core)

    owners = tile_owner[:, 0]
    slab = owners // n_inner
    step = (slab - grp + n_grp) % n_grp
    order = jnp.arange(count, dtype=jnp.int32)
    key = tile_col * count + order
    ahead = (slab[:, None] == slab[None, :]) & (key[None, :] < key[:, None])
    rank = jnp.sum(ahead.astype(jnp.int32), axis=1)
    fits = rank < total
    code = ((owners % n_inner) * per_dev + tile_row) * blocks + tile_col
    slots = jnp.arange(n_grp * total, dtype=jnp.int32)[:, None]
    mine = jnp.where(fits, step * total + rank, -1)[None, :] == slots
    index = jnp.sum(jnp.where(mine, order[None, :], 0), axis=1)
    theirs = jnp.where(fits, slab * total + rank, -1)[None, :] == slots
    codes = jnp.sum(jnp.where(theirs, code[None, :] + 1, 0), axis=1) - 1
    left_over = jnp.sum((~fits).astype(jnp.int32))

    where = jnp.stack([z, x]).astype(jnp.int32)

    def finish(parts):
        x_up, x_down, z_up, z_down = parts[:4]
        got_xu, got_xd = lax.ppermute(x_up, "inner", along_x[1]), lax.ppermute(x_down, "inner", along_x[3])
        got_zu, got_zd = lax.ppermute(z_up, "inner", along_z[1]), lax.ppermute(z_down, "inner", along_z[3])

        def onward(near_up, near_down, got_up, got_down):
            up = jnp.concatenate([near_up[:2] + got_up, near_up[2:]], axis=0)
            down = jnp.concatenate([near_down[:2], near_down[2:] + got_down], axis=0)
            return up, down

        x_up, x_down = onward(parts[4], parts[5], got_xu, got_xd)
        z_up, z_down = onward(parts[7], parts[8], got_zu, got_zd)
        got_xu, got_xd = lax.ppermute(x_up, "inner", along_x[1]), lax.ppermute(x_down, "inner", along_x[3])
        got_zu, got_zd = lax.ppermute(z_up, "inner", along_z[1]), lax.ppermute(z_down, "inner", along_z[3])
        s1 = [parts[6][q] + got_xu[q] + got_xd[q] for q in range(4)]
        s2 = [parts[9][q] + got_zu[q] + got_zd[q] for q in range(4)]
        f1 = [lax.ppermute(s1[s], "inner", along_z[s]) for s in (1, 3, 2)]
        f2 = [lax.ppermute(s2[s], "inner", along_x[s]) for s in (1, 3, 2)]
        return [s1[0] + f1[0] + f1[1] + f1[2], s2[0] + f2[0] + f2[1] + f2[2]]

    p1, p3 = pack(integrals, index, ((1, 0, total), (3, 0, total)), total)
    r1, r3 = lax.ppermute(p1, "grp", along_y[1]), lax.ppermute(p3, "grp", along_y[3])
    p2, p4, p0 = pack(integrals, index, ((2, 0, FIRST), (2, FIRST, total), (0, 0, total)), total)
    r2, r4 = lax.ppermute(p2, "grp", along_y[2]), lax.ppermute(p4, "grp", along_y[2])
    codes, _ = lax.optimization_barrier((codes, p4))
    note = jnp.concatenate(
        [
            jnp.broadcast_to(codes.reshape(n_grp, 1, total), (n_grp, n_inner, total)),
            jnp.broadcast_to(left_over, (n_grp, n_inner, 1)),
        ],
        axis=2,
    ).astype(jnp.float32)
    note = lax.all_to_all(note.reshape(devices, total + 1), AXES, split_axis=0, concat_axis=0, tiled=True)
    overflow = jnp.sum(note[:, total]) > 0.5
    note = note[:, :total].reshape(n_grp, n_inner // 2, 2, total)
    note = lax.dynamic_index_in_dim(note, inner // 2, axis=1, keepdims=False)
    note = jnp.stack([lax.dynamic_index_in_dim(note, (grp - s + n_grp) % n_grp, axis=0, keepdims=False) for s in range(4)])
    note = jnp.stack([lax.dynamic_index_in_dim(note, core, axis=1, keepdims=False), lax.dynamic_index_in_dim(note, 1 - core, axis=1, keepdims=False)])
    note = note.astype(jnp.int32)

    def codes_of(steps, lo, hi):
        return jnp.concatenate([note[side, s, lo:hi] for side in range(2) for s in steps])

    def with_other(tiles):
        return [*tiles, *[lax.ppermute(t, "inner", across) for t in tiles]]

    amp = arrange(where, amp)
    acc, token = ladder(codes_of((0, 1, 3), 0, total), amp, None, with_other([p0, gate(r1, note), gate(r3, note)]), False, blocks)
    acc, token = ladder(codes_of((2,), 0, FIRST), amp, acc, with_other([gate(r2, token)]), False, blocks)
    parts = ladder(codes_of((2,), FIRST, total), amp, acc, with_other([gate(r4, token)]), True, blocks)
    pieces = finish(parts)
    out = jnp.concatenate(pieces, axis=1)

    def with_rest(out):
        rest = jnp.where(fits[:, None, None], 0.0, integrals)
        return add(out, slow_part(amplitude, rest, tile_owner, tile_row, tile_col))

    return lax.cond(overflow, with_rest, lambda out: out, out)


def solution(mesh):
    placed = (P(AXES, None), P(AXES, None, None), P(AXES, None), P(AXES), P(AXES))
    return jax.shard_map(per_device, mesh=mesh, in_specs=placed, out_specs=P(AXES, None), check_vma=False)
```

profile of v0, /device:TPU:0, one launch (start us, length us, event | category | flops | bytes accessed | tf_op | source)
XLA Modules:
  0.0 229.7 jit_solution(16290951443999571724)
XLA Ops:
  6.5 0.7 all-gather.3.cloned.1.call-update
  7.3 0.8 fusion.36
  8.1 0.8 and_select_fusion.2
  8.9 0.2 convert_reduce_fusion.2
  9.1 0.6 fusion.33
  9.7 0.1 select_reduce_fusion
  9.9 6.0 %shard_map.59 = (f32[40,128,128]{2,1,0:T(8,128)}, f32[40,128,128]{2,1,0:T(8,128)}) custom-call(s32[160]{0:T(256)S(1)} %get-tuple-element.107.index, f32[128,128,128]{2,1,0:T(8,128)} %tiles.3), custom_call_target="tpu_custom_call" | custom-call | bytes 1000 | tf_op jit(solution)/shard_map/pallas_call | solution.py:60
  15.9 1.6 collective-permute-start
  17.5 1.7 collective-permute-start.1
  19.2 9.3 %shard_map.57 = (f32[30,128,128]{2,1,0:T(8,128)}, f32[10,128,128]{2,1,0:T(8,128)S(1)}, f32[40,128,128]{2,1,0:T(8,128)S(1)}) custom-call(s32[160]{0:T(256)S(1)} %get-tuple-element.107.index, f32[128,128,128]{2,1,0:T(8,128)S(1)} %copy-done.3), custom_call_target="tpu_custom_call" | custom-call | bytes 1000 | tf_op jit(solution)/shard_map/pallas_call | solution.py:60
  28.5 1.5 copy-done.1
  30.1 0.1 broadcast_in_dim.59
  30.2 1.2 pad_convert_fusion
  31.4 9.9 %all-to-all-start.3 = ((f32[128,1,41]{2,1,0:T(1,128)}), f32[128,1,41]{2,1,0:T(1,128)S(1)}, u32[]{:S(2)}, u32[]{:S(2)}) async-start(f32[128,1,41]{2,1,0:T(1,128)} %bitcast.13), calls=%async_computation.4 | async-start | bytes 131072 | tf_op jit(solution)/shard_map/all_to_all | solution.py:284
  41.3 0.1 collective-permute-start.2
  41.5 40.0 %all-to-all-done.3 = f32[128,1,41]{2,1,0:T(1,128)S(1)} async-done(((f32[128,1,41]{2,1,0:T(1,128)}), f32[128,1,41]{2,1,0:T(1,128)S(1)}, u32[]{:S(2)}, u32[]{:S(2)}) %all-to-all-start.3) | async-done | bytes 21024 | tf_op jit(solution)/shard_map/all_to_all | solution.py:284
  81.5 0.1 collective-permute-start.3
  81.7 0.5 collective-permute-start.4
  82.1 1.7 collective-permute-start.5
  83.8 0.1 pad_add_fusion.1.where
  83.9 0.1 concatenate.33.refs_0_
  84.0 3.4 %copy-done = f32[128,16384]{1,0:T(8,128)S(1)} copy-done((f32[128,16384]{1,0:T(8,128)S(1)}, f32[128,16384]{1,0:T(8,128)}, u32[]{:S(2)}) %copy-start) | copy-done | bytes 8388632
  87.4 1.2 shard_map.58.refs_1_
  88.6 0.9 collective-permute-done.3.refs_6_
  89.5 0.9 collective-permute-done.4.refs_7_
  90.4 25.9 %shard_map.62 = (f32[4,4,8,16384]{3,2,1,0:T(8,128)S(1)}, f32[8,128]{1,0:T(8,128)S(1)}) custom-call(s32[240]{0:T(256)S(1)} %concatenate.33.refs_0_, f32[16,8,16384]{2,1,0:T(8,128)S(1)} %shard_map.58.refs_1_, f32[40,128,128]{2,1,0:T(8,128)S(1)} %copy-done.2, f32[40,128,128]{2,1,0:T(8,128)} %shard_map.60.refs_3_, f32[40,128,128]{2,1,0:T(8,128)S(1)} %shard_map.61.refs_4_, ...), custom_call_target="tpu_custom_call" | custom-call | bytes 1000 | tf_op jit(solution)/shard_map/pallas_call | solution.py:195
  116.3 12.4 %collective-permute-done.5.refs_0_ = f32[30,128,128]{2,1,0:T(8,128)} collective-permute-done((f32[30,128,128]{2,1,0:T(8,128)}, f32[30,128,128]{2,1,0:T(8,128)}, u32[]{:S(2)}, u32[]{:S(2)}) %collective-permute-start.5) | collective-permute-done | bytes 1966112 | tf_op jit(solution)/shard_map/ppermute | solution.py:275
  128.8 1.7 collective-permute-start.7
  130.5 0.1 pad_add_fusion.2.refs_0_
  130.6 2.4 %collective-permute-done.6.refs_4_ = f32[30,128,128]{2,1,0:T(8,128)S(1)} collective-permute-done((f32[30,128,128]{2,1,0:T(8,128)}, f32[30,128,128]{2,1,0:T(8,128)S(1)}, u32[]{:S(2)}, u32[]{:S(2)}) %collective-permute-start.6) | collective-permute-done | bytes 1966112 | tf_op jit(solution)/shard_map/ppermute | solution.py:296
  133.0 8.8 %shard_map.64 = (f32[4,4,8,16384]{3,2,1,0:T(8,128)S(1)}, f32[8,128]{1,0:T(8,128)S(1)}) custom-call(s32[60]{0:T(128)S(1)} %pad_add_fusion.2.refs_0_, f32[16,8,16384]{2,1,0:T(8,128)S(1)} %shard_map.58.refs_1_, f32[4,4,8,16384]{3,2,1,0:T(8,128)S(1)} %get-tuple-element.55.refs_2_, f32[30,128,128]{2,1,0:T(8,128)} %shard_map.63.refs_3_, ...), custom_call_target="tpu_custom_call", output_to_operand_aliasing={{0}: (2, {})} | custom-call | bytes 1000 | tf_op jit(solution)/shard_map/pallas_call | solution.py:195
  141.8 5.6 %collective-permute-done.7.refs_0_ = f32[10,128,128]{2,1,0:T(8,128)S(1)} collective-permute-done((f32[10,128,128]{2,1,0:T(8,128)S(1)}, f32[10,128,128]{2,1,0:T(8,128)S(1)}, u32[]{:S(2)}, u32[]{:S(2)}) %collective-permute-start.7) | collective-permute-done | bytes 655392 | tf_op jit(solution)/shard_map/ppermute | solution.py:275
  147.5 0.1 pad_add_fusion.refs_0_
  147.6 1.9 collective-permute-done.8.refs_4_
  149.5 6.0 %shard_map.66 = (f32[2,8,8192]{2,1,0:T(8,128)}, f32[2,8,8192]{2,1,0:T(8,128)}, f32[2,8,8192]{2,1,0:T(8,128)}, f32[2,8,8192]{2,1,0:T(8,128)}, f32[4,8,8192]{2,1,0...) custom-call(s32[20]{0:T(128)S(1)} %pad_add_fusion.refs_0_, ...), custom_call_target="tpu_custom_call" | custom-call | bytes 1000 | tf_op jit(solution)/shard_map/pallas_call | solution.py:195
  155.5 1.0 collective-permute-start.9
  156.5 0.7 slice_reduce_fusion
  157.9 2.4 %collective-permute-start.11 = (f32[2,8,8192]{2,1,0:T(8,128)}, f32[2,8,8192]{2,1,0:T(8,128)S(1)}, u32[]{:S(2)}, u32[]{:S(2)}) collective-permute-start(f32[2,8,8192]{2,1,0:T(8,128)} %get-tuple-element.64), channel_id=1, source_target_pairs={{0,6},{1,7},{2,0},{3,1},{4,2},{5,3},{6,4},{7,5},{8,14},{9,15},{10,... | collective-permute-start | bytes 1572872 | tf_op jit(solution)/shard_map/ppermute | solution.py:254
  160.3 0.5 collective-permute-start.16
  160.8 2.7 %collective-permute-start.18 = (f32[2,8,8192]{2,1,0:T(8,128)}, f32[2,8,8192]{2,1,0:T(8,128)S(1)}, u32[]{:S(2)}, u32[]{:S(2)}) collective-permute-start(f32[2,8,8192]{2,1,0:T(8,128)} %get-tuple-element.69), channel_id=1, source_target_pairs={{0,24},{1,25},{2,26},{3,27},{4,28},{5,29},{6,30},{7,31},{8,0},{9,1... | collective-permute-start | bytes 1572872 | tf_op jit(solution)/shard_map/ppermute | solution.py:255
  163.5 7.5 %collective-permute-done.9 = f32[2,8,8192]{2,1,0:T(8,128)S(1)} collective-permute-done((f32[2,8,8192]{2,1,0:T(8,128)}, f32[2,8,8192]{2,1,0:T(8,128)S(1)}, u32[]{:S(2)}, u32[]{:S(2)}) %collective-permute-start.9) | collective-permute-done | bytes 524320 | tf_op jit(solution)/shard_map/ppermute | solution.py:254
  171.0 1.3 slice_add_fusion.3
  172.4 0.1 collective-permute-start.10
  172.5 1.4 fusion.37
  174.0 3.3 %collective-permute-start.12 = (f32[4,8,8192]{2,1,0:T(8,128)S(1)}, f32[4,8,8192]{2,1,0:T(8,128)S(1)}, u32[]{:S(2)}, u32[]{:S(2)}) collective-permute-start(f32[4,8,8192]{2,1,0:T(8,128)S(1)} %pad_maximum_fusion.1), channel_id=1, source_target_pairs={{0,6},{1,7},{2,0},{3,1},{4,2},{5,3},{6,4},{7,5},{8,14},{9,15},{10,... | collective-permute-start | bytes 3145736 | tf_op jit(solution)/shard_map/ppermute | solution.py:264
  177.2 0.1 slice_add_fusion.1
  177.4 0.6 collective-permute-start.17
  178.0 0.1 fusion.38
  178.2 2.8 %collective-permute-start.19 = (f32[4,8,8192]{2,1,0:T(8,128)S(1)}, f32[4,8,8192]{2,1,0:T(8,128)S(1)}, u32[]{:S(2)}, u32[]{:S(2)}) collective-permute-start(f32[4,8,8192]{2,1,0:T(8,128)S(1)} %pad_maximum_fusion.3), channel_id=1, source_target_pairs={{0,24},{1,25},{2,26},{3,27},{4,28},{5,29},{6,30},{7,31},{8,0},{9,1... | collective-permute-start | bytes 3145736 | tf_op jit(solution)/shard_map/ppermute | solution.py:265
  181.0 17.1 %collective-permute-done.10 = f32[4,8,8192]{2,1,0:T(8,128)S(1)} collective-permute-done((f32[4,8,8192]{2,1,0:T(8,128)S(1)}, f32[4,8,8192]{2,1,0:T(8,128)S(1)}, u32[]{:S(2)}, u32[]{:S(2)}) %collective-permute-start.10) | collective-permute-done | bytes 1048608 | tf_op jit(solution)/shard_map/ppermute | solution.py:264
  198.0 0.8 collective-permute-done.12
  198.8 0.1 fusion.20
  198.9 0.6 collective-permute-start.13
  199.5 2.7 %collective-permute-start.14 = (f32[8,8192]{1,0:T(8,128)S(1)}, f32[8,8192]{1,0:T(8,128)S(1)}, u32[]{:S(2)}, u32[]{:S(2)}) collective-permute-start(f32[8,8192]{1,0:T(8,128)S(1)} %get-tuple-element.73), channel_id=1, source_target_pairs={{0,24},{1,25},{2,26},{3,27},{4,28},{5,29},{6,30},{7,31},{8,0},{9,1... | collective-permute-start | bytes 786440 | tf_op jit(solution)/shard_map/ppermute | solution.py:268
  202.3 1.8 collective-permute-done.17
  204.1 0.1 fusion.13
  204.2 0.4 collective-permute-start.20
  204.5 3.2 %collective-permute-start.21 = (f32[8,8192]{1,0:T(8,128)S(1)}, f32[8,8192]{1,0:T(8,128)S(1)}, u32[]{:S(2)}, u32[]{:S(2)}) collective-permute-start(f32[8,8192]{1,0:T(8,128)S(1)} %get-tuple-element.76), channel_id=1, source_target_pairs={{0,6},{1,7},{2,0},{3,1},{4,2},{5,3},{6,4},{7,5},{8,14},{9,15},{10,... | collective-permute-start | bytes 786440 | tf_op jit(solution)/shard_map/ppermute | solution.py:269
  207.8 6.0 %collective-permute-done.13 = f32[8,8192]{1,0:T(8,128)S(1)} collective-permute-done((f32[8,8192]{1,0:T(8,128)S(1)}, f32[8,8192]{1,0:T(8,128)S(1)}, u32[]{:S(2)}, u32[]{:S(2)}) %collective-permute-start.13) | collective-permute-done | bytes 262176 | tf_op jit(solution)/shard_map/ppermute | solution.py:268
  213.8 0.9 collective-permute-start.22
  214.7 0.1 fusion.24
  214.8 6.9 %collective-permute-done.22 = f32[8,8192]{1,0:T(8,128)S(1)} collective-permute-done((f32[8,8192]{1,0:T(8,128)S(1)}, f32[8,8192]{1,0:T(8,128)S(1)}, u32[]{:S(2)}, u32[]{:S(2)}) %collective-permute-start.22) | collective-permute-done | bytes 262176 | tf_op jit(solution)/shard_map/ppermute | solution.py:269
  221.8 0.2 conditional.1
  222.0 0.8 copy-done.4
  (57 shorter events, 0.6 us)
Async XLA Ops:
  6.5 77.5 %all-gather.3.cloned.1.call-start = ((), (), s32[]{:S(2)}) async-start(), calls=%async_computation.6 | async-start | bytes 8912896 | tf_op jit(solution)/shard_map/all_gather | solution.py:232
  7.3 11.9 %copy-start.3 = (f32[128,128,128]{2,1,0:T(8,128)S(1)}, f32[128,128,128]{2,1,0:T(8,128)}, u32[]{:S(2)}) copy-start(f32[128,128,128]{2,1,0:T(8,128)} %tiles.3) | copy-start | bytes 25165828
  15.9 65.7 %collective-permute-start = (f32[40,128,128]{2,1,0:T(8,128)}, f32[40,128,128]{2,1,0:T(8,128)}, u32[]{:S(2)}, u32[]{:S(2)}) collective-permute-start(f32[40,128,128]{2,1,0:T(8,128)} %get-tuple-element.53), channel_id=1, source_target_pairs={{0,32},{32,64},{64,96},{96,0},{1,33},{33,65},{65,97},{97,1},{2,34}... | collective-permute-start | bytes 7864328 | tf_op jit(solution)/shard_map/ppermute | solution.py:273
  17.5 64.2 %collective-permute-start.1 = (f32[40,128,128]{2,1,0:T(8,128)}, f32[40,128,128]{2,1,0:T(8,128)S(1)}, u32[]{:S(2)}, u32[]{:S(2)}) collective-permute-start(f32[40,128,128]{2,1,0:T(8,128)} %get-tuple-element.54), channel_id=1, source_target_pairs={{0,96},{32,0},{64,32},{96,64},{1,97},{33,1},{65,33},{97,65},{2,98}... | collective-permute-start | bytes 7864328 | tf_op jit(solution)/shard_map/ppermute | solution.py:273
  28.5 1.5 copy-start.1
  31.4 50.1 %all-to-all-start.3 = ((f32[128,1,41]{2,1,0:T(1,128)}), f32[128,1,41]{2,1,0:T(1,128)S(1)}, u32[]{:S(2)}, u32[]{:S(2)}) async-start(f32[128,1,41]{2,1,0:T(1,128)} %bitcast.13), calls=%async_computation.4 | async-start | bytes 131072 | tf_op jit(solution)/shard_map/all_to_all | solution.py:284
  41.3 47.3 %collective-permute-start.2 = (f32[40,128,128]{2,1,0:T(8,128)}, f32[40,128,128]{2,1,0:T(8,128)}, u32[]{:S(2)}, u32[]{:S(2)}) collective-permute-start(f32[40,128,128]{2,1,0:T(8,128)} %copy-done.1), channel_id=1, source_target_pairs={{0,1},{1,0},{2,3},{3,2},{4,5},{5,4},{6,7},{7,6},{8,9},{9,8},{10,11... | collective-permute-start | bytes 7864328 | tf_op jit(solution)/shard_map/ppermute | solution.py:296
  81.5 7.9 %collective-permute-start.3 = (f32[40,128,128]{2,1,0:T(8,128)}, f32[40,128,128]{2,1,0:T(8,128)}, u32[]{:S(2)}, u32[]{:S(2)}) collective-permute-start(f32[40,128,128]{2,1,0:T(8,128)} %shard_map.60.refs_3_), channel_id=1, source_target_pairs={{0,1},{1,0},{2,3},{3,2},{4,5},{5,4},{6,7},{7,6},{8,9},{9,8},{10,11... | collective-permute-start | bytes 7864328 | tf_op jit(solution)/shard_map/ppermute | solution.py:296
  81.7 8.8 %collective-permute-start.4 = (f32[40,128,128]{2,1,0:T(8,128)S(1)}, f32[40,128,128]{2,1,0:T(8,128)}, u32[]{:S(2)}, u32[]{:S(2)}) collective-permute-start(f32[40,128,128]{2,1,0:T(8,128)S(1)} %shard_map.61.refs_4_), channel_id=1, source_target_pairs={{0,1},{1,0},{2,3},{3,2},{4,5},{5,4},{6,7},{7,6},{8,9},{9,8},{10,11... | collective-permute-start | bytes 7864328 | tf_op jit(solution)/shard_map/ppermute | solution.py:296
  82.1 46.7 %collective-permute-start.5 = (f32[30,128,128]{2,1,0:T(8,128)}, f32[30,128,128]{2,1,0:T(8,128)}, u32[]{:S(2)}, u32[]{:S(2)}) collective-permute-start(f32[30,128,128]{2,1,0:T(8,128)} %get-tuple-element.56), channel_id=1, source_target_pairs={{0,64},{32,96},{64,0},{96,32},{1,65},{33,97},{65,1},{97,33},{2,66}... | collective-permute-start | bytes 5898248 | tf_op jit(solution)/shard_map/ppermute | solution.py:275
  84.0 3.4 %copy-start = (f32[128,16384]{1,0:T(8,128)S(1)}, f32[128,16384]{1,0:T(8,128)}, u32[]{:S(2)}) copy-start(f32[128,16384]{1,0:T(8,128)} %all-gather.3.cloned.1.call-done) | copy-start | bytes 25165828
  87.4 3.0 %copy-start.2 = (f32[40,128,128]{2,1,0:T(8,128)S(1)}, f32[40,128,128]{2,1,0:T(8,128)}, u32[]{:S(2)}) copy-start(f32[40,128,128]{2,1,0:T(8,128)} %copy-done.1) | copy-start | bytes 7864324
  128.8 4.2 %collective-permute-start.6 = (f32[30,128,128]{2,1,0:T(8,128)}, f32[30,128,128]{2,1,0:T(8,128)S(1)}, u32[]{:S(2)}, u32[]{:S(2)}) collective-permute-start(f32[30,128,128]{2,1,0:T(8,128)} %shard_map.63.refs_3_), channel_id=1, source_target_pairs={{0,1},{1,0},{2,3},{3,2},{4,5},{5,4},{6,7},{7,6},{8,9},{9,8},{10,11... | collective-permute-start | bytes 5898248 | tf_op jit(solution)/shard_map/ppermute | solution.py:296
  128.8 18.6 %collective-permute-start.7 = (f32[10,128,128]{2,1,0:T(8,128)S(1)}, f32[10,128,128]{2,1,0:T(8,128)S(1)}, u32[]{:S(2)}, u32[]{:S(2)}) collective-permute-start(f32[10,128,128]{2,1,0:T(8,128)S(1)} %get-tuple-element.50), channel_id=1, source_target_pairs={{0,64},{32,96},{64,0},{96,32},{1,65},{33,97},{65,1},{97,33},{2,66}... | collective-permute-start | bytes 1966088 | tf_op jit(solution)/shard_map/ppermute | solution.py:275
  147.4 2.1 collective-permute-start.8
  155.5 21.7 %copy-start.8 = (f32[4,8,8192]{2,1,0:T(8,128)S(1)}, f32[4,8,8192]{2,1,0:T(8,128)}, u32[]{:S(2)}) copy-start(f32[4,8,8192]{2,1,0:T(8,128)} %get-tuple-element.66) | copy-start | bytes 3145732
  155.5 22.5 %copy-start.7 = (f32[4,8,8192]{2,1,0:T(8,128)S(1)}, f32[4,8,8192]{2,1,0:T(8,128)}, u32[]{:S(2)}) copy-start(f32[4,8,8192]{2,1,0:T(8,128)} %get-tuple-element.68) | copy-start | bytes 3145732
  155.5 15.5 %collective-permute-start.9 = (f32[2,8,8192]{2,1,0:T(8,128)}, f32[2,8,8192]{2,1,0:T(8,128)S(1)}, u32[]{:S(2)}, u32[]{:S(2)}) collective-permute-start(f32[2,8,8192]{2,1,0:T(8,128)} %get-tuple-element.62), channel_id=1, source_target_pairs={{0,2},{1,3},{2,4},{3,5},{4,6},{5,7},{6,0},{7,1},{8,10},{9,11},{10,... | collective-permute-start | bytes 1572872 | tf_op jit(solution)/shard_map/ppermute | solution.py:254
  157.9 14.6 %collective-permute-start.11 = (f32[2,8,8192]{2,1,0:T(8,128)}, f32[2,8,8192]{2,1,0:T(8,128)S(1)}, u32[]{:S(2)}, u32[]{:S(2)}) collective-permute-start(f32[2,8,8192]{2,1,0:T(8,128)} %get-tuple-element.64), channel_id=1, source_target_pairs={{0,6},{1,7},{2,0},{3,1},{4,2},{5,3},{6,4},{7,5},{8,14},{9,15},{10,... | collective-permute-start | bytes 1572872 | tf_op jit(solution)/shard_map/ppermute | solution.py:254
  160.3 16.9 %collective-permute-start.16 = (f32[2,8,8192]{2,1,0:T(8,128)}, f32[2,8,8192]{2,1,0:T(8,128)S(1)}, u32[]{:S(2)}, u32[]{:S(2)}) collective-permute-start(f32[2,8,8192]{2,1,0:T(8,128)} %get-tuple-element.67), channel_id=1, source_target_pairs={{0,8},{1,9},{2,10},{3,11},{4,12},{5,13},{6,14},{7,15},{8,16},{9,17... | collective-permute-start | bytes 1572872 | tf_op jit(solution)/shard_map/ppermute | solution.py:255
  160.8 17.2 %collective-permute-start.18 = (f32[2,8,8192]{2,1,0:T(8,128)}, f32[2,8,8192]{2,1,0:T(8,128)S(1)}, u32[]{:S(2)}, u32[]{:S(2)}) collective-permute-start(f32[2,8,8192]{2,1,0:T(8,128)} %get-tuple-element.69), channel_id=1, source_target_pairs={{0,24},{1,25},{2,26},{3,27},{4,28},{5,29},{6,30},{7,31},{8,0},{9,1... | collective-permute-start | bytes 1572872 | tf_op jit(solution)/shard_map/ppermute | solution.py:255
  172.3 26.5 %copy-start.6 = (f32[4,8,8192]{2,1,0:T(8,128)S(1)}, f32[4,8,8192]{2,1,0:T(8,128)}, u32[]{:S(2)}) copy-start(f32[4,8,8192]{2,1,0:T(8,128)} %get-tuple-element.60) | copy-start | bytes 3145732
  172.4 25.7 %collective-permute-start.10 = (f32[4,8,8192]{2,1,0:T(8,128)S(1)}, f32[4,8,8192]{2,1,0:T(8,128)S(1)}, u32[]{:S(2)}, u32[]{:S(2)}) collective-permute-start(f32[4,8,8192]{2,1,0:T(8,128)S(1)} %pad_maximum_fusion), channel_id=1, source_target_pairs={{0,2},{1,3},{2,4},{3,5},{4,6},{5,7},{6,0},{7,1},{8,10},{9,11},{10,... | collective-permute-start | bytes 3145736 | tf_op jit(solution)/shard_map/ppermute | solution.py:264
  172.5 31.6 %copy-start.5 = (f32[4,8,8192]{2,1,0:T(8,128)S(1)}, f32[4,8,8192]{2,1,0:T(8,128)}, u32[]{:S(2)}) copy-start(f32[4,8,8192]{2,1,0:T(8,128)} %get-tuple-element.65) | copy-start | bytes 3145732
  174.0 24.9 %collective-permute-start.12 = (f32[4,8,8192]{2,1,0:T(8,128)S(1)}, f32[4,8,8192]{2,1,0:T(8,128)S(1)}, u32[]{:S(2)}, u32[]{:S(2)}) collective-permute-start(f32[4,8,8192]{2,1,0:T(8,128)S(1)} %pad_maximum_fusion.1), channel_id=1, source_target_pairs={{0,6},{1,7},{2,0},{3,1},{4,2},{5,3},{6,4},{7,5},{8,14},{9,15},{10,... | collective-permute-start | bytes 3145736 | tf_op jit(solution)/shard_map/ppermute | solution.py:264
  177.4 44.4 %copy-start.9 = (s32[128,1]{0,1:T(1,128)S(1)}, s32[128,1]{0,1:T(1,128)}, u32[]{:S(2)}) copy-start(s32[128,1]{0,1:T(1,128)} %param.9) | copy-start | bytes 1540
  177.4 44.4 %copy-start.10 = (s32[128]{0:T(128)S(1)}, s32[128]{0:T(128)}, u32[]{:S(2)}) copy-start(s32[128]{0:T(128)} %param.11) | copy-start | bytes 1540
  177.4 44.4 %copy-start.11 = (s32[128]{0:T(128)S(1)}, s32[128]{0:T(128)}, u32[]{:S(2)}) copy-start(s32[128]{0:T(128)} %param.10) | copy-start | bytes 1540
  177.4 26.6 %collective-permute-start.17 = (f32[4,8,8192]{2,1,0:T(8,128)S(1)}, f32[4,8,8192]{2,1,0:T(8,128)S(1)}, u32[]{:S(2)}, u32[]{:S(2)}) collective-permute-start(f32[4,8,8192]{2,1,0:T(8,128)S(1)} %pad_maximum_fusion.2), channel_id=1, source_target_pairs={{0,8},{1,9},{2,10},{3,11},{4,12},{5,13},{6,14},{7,15},{8,16},{9,17... | collective-permute-start | bytes 3145736 | tf_op jit(solution)/shard_map/ppermute | solution.py:265
  178.2 25.9 %collective-permute-start.19 = (f32[4,8,8192]{2,1,0:T(8,128)S(1)}, f32[4,8,8192]{2,1,0:T(8,128)S(1)}, u32[]{:S(2)}, u32[]{:S(2)}) collective-permute-start(f32[4,8,8192]{2,1,0:T(8,128)S(1)} %pad_maximum_fusion.3), channel_id=1, source_target_pairs={{0,24},{1,25},{2,26},{3,27},{4,28},{5,29},{6,30},{7,31},{8,0},{9,1... | collective-permute-start | bytes 3145736 | tf_op jit(solution)/shard_map/ppermute | solution.py:265
  198.9 14.8 %collective-permute-start.13 = (f32[8,8192]{1,0:T(8,128)S(1)}, f32[8,8192]{1,0:T(8,128)S(1)}, u32[]{:S(2)}, u32[]{:S(2)}) collective-permute-start(f32[8,8192]{1,0:T(8,128)S(1)} %get-tuple-element.71), channel_id=1, source_target_pairs={{0,8},{1,9},{2,10},{3,11},{4,12},{5,13},{6,14},{7,15},{8,16},{9,17... | collective-permute-start | bytes 786440 | tf_op jit(solution)/shard_map/ppermute | solution.py:268
  199.5 15.1 %collective-permute-start.14 = (f32[8,8192]{1,0:T(8,128)S(1)}, f32[8,8192]{1,0:T(8,128)S(1)}, u32[]{:S(2)}, u32[]{:S(2)}) collective-permute-start(f32[8,8192]{1,0:T(8,128)S(1)} %get-tuple-element.73), channel_id=1, source_target_pairs={{0,24},{1,25},{2,26},{3,27},{4,28},{5,29},{6,30},{7,31},{8,0},{9,1... | collective-permute-start | bytes 786440 | tf_op jit(solution)/shard_map/ppermute | solution.py:268
  202.3 12.4 %collective-permute-start.15 = (f32[8,8192]{1,0:T(8,128)S(1)}, f32[8,8192]{1,0:T(8,128)S(1)}, u32[]{:S(2)}, u32[]{:S(2)}) collective-permute-start(f32[8,8192]{1,0:T(8,128)S(1)} %get-tuple-element.72), channel_id=1, source_target_pairs={{0,16},{1,17},{2,18},{3,19},{4,20},{5,21},{6,22},{7,23},{8,24},{9,... | collective-permute-start | bytes 786440 | tf_op jit(solution)/shard_map/ppermute | solution.py:268
  204.2 10.6 %collective-permute-start.20 = (f32[8,8192]{1,0:T(8,128)S(1)}, f32[8,8192]{1,0:T(8,128)S(1)}, u32[]{:S(2)}, u32[]{:S(2)}) collective-permute-start(f32[8,8192]{1,0:T(8,128)S(1)} %get-tuple-element.74), channel_id=1, source_target_pairs={{0,2},{1,3},{2,4},{3,5},{4,6},{5,7},{6,0},{7,1},{8,10},{9,11},{10,... | collective-permute-start | bytes 786440 | tf_op jit(solution)/shard_map/ppermute | solution.py:269
  204.5 10.2 %collective-permute-start.21 = (f32[8,8192]{1,0:T(8,128)S(1)}, f32[8,8192]{1,0:T(8,128)S(1)}, u32[]{:S(2)}, u32[]{:S(2)}) collective-permute-start(f32[8,8192]{1,0:T(8,128)S(1)} %get-tuple-element.76), channel_id=1, source_target_pairs={{0,6},{1,7},{2,0},{3,1},{4,2},{5,3},{6,4},{7,5},{8,14},{9,15},{10,... | collective-permute-start | bytes 786440 | tf_op jit(solution)/shard_map/ppermute | solution.py:269
  213.8 7.9 %collective-permute-start.22 = (f32[8,8192]{1,0:T(8,128)S(1)}, f32[8,8192]{1,0:T(8,128)S(1)}, u32[]{:S(2)}, u32[]{:S(2)}) collective-permute-start(f32[8,8192]{1,0:T(8,128)S(1)} %get-tuple-element.75), channel_id=1, source_target_pairs={{0,4},{1,5},{2,6},{3,7},{4,0},{5,1},{6,2},{7,3},{8,12},{9,13},{10,... | collective-permute-start | bytes 786440 | tf_op jit(solution)/shard_map/ppermute | solution.py:269
  222.0 0.8 copy-start.4
Sparse Core Ops, SparseCore 0:
  9.5 73.6 all-gather.2
where the time goes:
time: 229 us; the launch traced here: 230 us
  waiting for transfers between devices  105 us (46%)
  Pallas kernels  57.2 us (25%)
  starting transfers between devices  38.4 us (17%)
  between operations  14.5 us (6%)
  other arithmetic  8.32 us (4%)
  local copies, waits for them, and re-layouts  6.02 us (3%)
    pallas_call x3, Pallas kernels, ladder(): pl.pallas_call(functools.partial(ladder_kernel, counts, blocks, acc is No...  40.7 us
    all_to_all x1, waiting for transfers between devices, per_device(): lax.all_to_all(note.reshape(devices, total + 1), AXES, split_axis=0, conc...  40 us
    ppermute x2, waiting for transfers between devices, finish(): lax.ppermute(x_up, 'inner', along_x[1])  24.5 us
    pallas_call x2, Pallas kernels, pack(): pl.pallas_call(functools.partial(pack_kernel, spans, total), out_shape=[j...  15.3 us
    ppermute x1, waiting for transfers between devices, per_device(): lax.ppermute(p2, 'grp', along_y[2])  12.4 us
    all_to_all x1, starting transfers between devices, per_device(): lax.all_to_all(note.reshape(devices, total + 1), AXES, split_axis=0, conc...  9.89 us
    ppermute x3, waiting for transfers between devices, finish(): f2 = [lax.ppermute(s2[s], 'inner', along_x[s]) for s in (1, 3, 2)]  6.89 us
    ppermute x5, waiting for transfers between devices, with_other(): return [*tiles, *[lax.ppermute(t, 'inner', across) for t in tiles]]  6.17 us
  transfers between devices with their start and end apart: 25, of which 13 were waited for; matrix products, arithmetic and copies ran while one was open for 4% of the time, Pallas kernels for 22%

commit v1 on v0

--- a/solution.py
+++ b/solution.py
@@ -10,7 +10,8 @@
 TILE = 128
 SLOTS = 40
 FIRST = 30
-VMEM = 24 * 1024 * 1024
+LOW = 64
+GUESS = (80 * 10**6, 35 * 10**6, 20 * 10**6)
 AXES = ("grp", "inner")
 
 
@@ -72,8 +73,19 @@
     out[...] = one[...] + two[...]
 
 
-def add(one, two):
-    return pl.pallas_call(add_kernel, out_shape=jax.ShapeDtypeStruct(one.shape, one.dtype))(one, two)
+def total_kernel(*refs):
+    out, width = refs[-1], refs[0].shape[1]
+    for piece in range(len(refs) // 4):
+        group = refs[piece * 4 : piece * 4 + 4]
+        out[:, pl.ds(piece * width, width)] = (group[0][...] + group[1][...]) + (group[2][...] + group[3][...])
+
+
+def small(kernel, shape, *values):
+    return pl.pallas_call(
+        kernel,
+        out_shape=jax.ShapeDtypeStruct(shape, jnp.float32),
+        compiler_params=pltpu.CompilerParams(vmem_limit_bytes=6 * 2**20),
+    )(*values)
 
 
 def gate_kernel(*refs):
@@ -97,12 +109,16 @@
     return high, (value - high.astype(jnp.float32)).astype(jnp.bfloat16)
 
 
-def arrange_kernel(where, amp, out, sem):
+def start_arranged(where, amp, out, sem):
     z, x = where[0], where[1]
     for sx in range(4):
         for sz in range(4):
             source = lax.rem(z + sz, 4) * 4 + lax.rem(x + sx, 4)
             pltpu.make_async_copy(amp.at[source], out.at[sx * 4 + sz], sem).start()
+
+
+def arrange_kernel(where, amp, out, sem):
+    start_arranged(where, amp, out, sem)
     pltpu.make_async_copy(amp, out, sem).wait()
 
 
@@ -118,30 +134,9 @@
     )(where, amp)
 
 
-def ladder_kernel(counts, blocks, first, last, *refs):
-    refs, lists = list(refs), len(counts)
-    code, amp_v = refs[:2]
-    del refs[:2]
-    acc_v = None if first else refs.pop(0)
-    tiles = refs[:lists]
-    del refs[:lists]
-    if last:
-        parts = [refs.pop(0) for _ in range(10)]
-    else:
-        acc_v = refs.pop(0)
-        token = refs.pop(0)
-        token[...] = jnp.zeros_like(token)
-    tile_v = refs[:lists]
-    tile_sem, out_sem = refs[lists:]
-
-    copies = [pltpu.make_async_copy(tiles[k], tile_v[k], tile_sem.at[k]) for k in range(lists)]
-    for copy in copies:
-        copy.start()
-    if first:
-        acc_v[...] = jnp.zeros_like(acc_v)
-
-    for k in range(lists):
-        copies[k].wait()
+def multiply(code, counts, tiles, tile_v, tile_sem, amp_v, acc_v, low, blocks):
+    for k, count in enumerate(counts):
+        pltpu.make_async_copy(tiles[k], tile_v[k], tile_sem.at[k]).wait()
         base = sum(counts[:k])
 
         def pair(j, _):
@@ -151,9 +146,9 @@
             def _():
                 terms = []
                 for half, place in enumerate(places):
-                    held = jnp.maximum(place, 0)
+                    held = jnp.maximum(place, low)
                     row = pl.multiple_of((held // blocks) * TILE, TILE)
-                    col = pl.multiple_of(lax.rem(held, blocks) * TILE, TILE)
+                    col = pl.multiple_of((lax.rem(held, blocks) - low) * TILE, TILE)
                     a_hi, a_lo = split(amp_v[:, :, pl.ds(row, TILE)].reshape(16 * 8, TILE))
                     t_hi, t_lo = split(jnp.where(place >= 0, tile_v[k][2 * j + half], 0.0))
                     left = jnp.concatenate([a_hi, a_lo], axis=1)
@@ -165,47 +160,94 @@
 
             return 0
 
-        lax.fori_loop(0, counts[k] // 2, pair, 0)
-
-    if last:
-        half = blocks * TILE // 2
-        one, two = pl.ds(0, half), pl.ds(half, half)
-        sources = [acc_v.at[2, pl.ds(0, 2), :, one], acc_v.at[2, pl.ds(2, 2), :, one]]
-        sources += [acc_v.at[pl.ds(0, 2), 2, :, two], acc_v.at[pl.ds(2, 2), 2, :, two]]
-        sources += [acc_v.at[s, :, :, one] for s in (1, 3, 0)] + [acc_v.at[:, s, :, two] for s in (1, 3, 0)]
-        done = [pltpu.make_async_copy(source, part, out_sem.at[i]) for i, (source, part) in enumerate(zip(sources, parts))]
-        for copy in done:
-            copy.start()
-        for copy in done:
-            copy.wait()
+        lax.fori_loop(0, count // 2, pair, 0)
+
+
+def part_copies(acc_v, width, parts, sem):
+    half = width // 2
+    one, two = pl.ds(0, half), pl.ds(half, half)
+    sources = [acc_v.at[2, pl.ds(0, 2), :, one], acc_v.at[2, pl.ds(2, 2), :, one]]
+    sources += [acc_v.at[pl.ds(0, 2), 2, :, two], acc_v.at[pl.ds(2, 2), 2, :, two]]
+    sources += [acc_v.at[s, :, :, one] for s in (1, 3, 0)] + [acc_v.at[:, s, :, two] for s in (1, 3, 0)]
+    return [pltpu.make_async_copy(source, part, sem.at[i]) for i, (source, part) in enumerate(zip(sources, parts))]
+
+
+def ladder_kernel(step, counts, low, *refs):
+    refs, lists = list(refs), len(counts)
+
+    def take(n):
+        taken = refs[:n]
+        del refs[:n]
+        return taken
+
+    code, amp = take(2)
+    where, acc_in = take(2) if step == 2 else (None, None)
+    (acc_v,) = take(1) if step == 1 else (None,)
+    tiles = take(lists)
+    parts = take(10) if step else []
+    (rest,) = take(1) if step == 1 else (None,)
+    if step == 0:
+        (acc_v,) = take(1)
+    if step < 2:
+        (token,) = take(1)
+        token[...] = jnp.zeros_like(token)
+    tile_v = take(lists)
+    tile_sem, out_sem = take(2)
+    for k in range(lists):
+        pltpu.make_async_copy(tiles[k], tile_v[k], tile_sem.at[k]).start()
+    amp_v = amp
+    if step == 0:
+        acc_v[...] = jnp.zeros_like(acc_v)
+    if step == 2:
+        amp_v, acc_v, held_sem = refs
+        start_arranged(where, amp, amp_v, held_sem.at[0])
+        acc_copy = pltpu.make_async_copy(acc_in, acc_v, held_sem.at[1])
+        acc_copy.start()
+        pltpu.make_async_copy(amp, amp_v, held_sem.at[0]).wait()
+        acc_copy.wait()
+    blocks = amp.shape[2] // TILE
+    multiply(code, counts, tiles, tile_v, tile_sem, amp_v, acc_v, low if step == 2 else 0, blocks)
+    done = part_copies(acc_v, acc_in.shape[3] if step == 2 else low * TILE, parts, out_sem) if step else []
+    if step == 1:
+        done.append(pltpu.make_async_copy(acc_v.at[:, :, :, pl.ds(low * TILE, (blocks - low) * TILE)], rest, out_sem.at[10]))
+    for copy in done:
+        copy.start()
+    for copy in done:
+        copy.wait()
 
 
 def keep(value):
     return pltpu.with_memory_space_constraint(value, pltpu.VMEM)
 
 
-def ladder(code, amp, acc, tiles, last, blocks):
+def ladder(step, code, amp, held, tiles, blocks, guess):
     counts = tuple(t.shape[0] for t in tiles)
     any_spec, smem, vmem = [pl.BlockSpec(memory_space=m) for m in (pl.ANY, pltpu.SMEM, pltpu.VMEM)]
-    held = [] if acc is None else [acc]
-    if last:
-        shapes = [pltpu.HBM((n, 8, blocks * TILE // 2), jnp.float32) for n in (2,) * 4 + (4,) * 6]
+    width = ((blocks, LOW, blocks - LOW)[step]) * TILE
+    token = jax.ShapeDtypeStruct((8, TILE), jnp.float32)
+    parts = [pltpu.HBM((n, 8, width // 2), jnp.float32) for n in (2,) * 4 + (4,) * 6]
+    if step == 0:
+        given, into, shapes, specs = [keep(amp)], [vmem], [pltpu.VMEM((4, 4, 8, width), jnp.float32), token], [vmem] * 2
+    elif step == 1:
+        given, into = [keep(amp), keep(held)], [vmem] * 2
+        shapes, specs = [*parts, pltpu.HBM((4, 4, 8, blocks * TILE - width), jnp.float32), token], [any_spec] * 11 + [vmem]
     else:
-        shapes = [pltpu.VMEM((4, 4, 8, blocks * TILE), jnp.float32), jax.ShapeDtypeStruct((8, TILE), jnp.float32)]
-    return pl.pallas_call(
-        functools.partial(ladder_kernel, counts, blocks, acc is None, last),
+        given, into, shapes, specs = [amp, *held], [any_spec, smem, any_spec], parts, [any_spec] * 10
+    scratch = [pltpu.VMEM((n, TILE, TILE), jnp.float32) for n in counts]
+    scratch += [pltpu.SemaphoreType.DMA((len(tiles),)), pltpu.SemaphoreType.DMA((11,))]
+    limit = 2**21 + sum(counts) * TILE * TILE * 4
+    if step == 2:
+        scratch += [pltpu.VMEM(amp.shape, jnp.float32), pltpu.VMEM((4, 4, 8, width), jnp.float32), pltpu.SemaphoreType.DMA((2,))]
+        limit += 12 * 2**20
+    return pl.pallas_call(
+        functools.partial(ladder_kernel, step, counts, LOW),
         out_shape=shapes,
-        in_specs=[smem, vmem] + [vmem] * len(held) + [any_spec] * len(tiles),
-        out_specs=[any_spec] * len(shapes) if last else [vmem, vmem],
-        scratch_shapes=[
-            *[pltpu.VMEM((n, TILE, TILE), jnp.float32) for n in counts],
-            pltpu.SemaphoreType.DMA((len(tiles),)),
-            pltpu.SemaphoreType.DMA((10,)),
-        ],
-        input_output_aliases={2: 0} if held and not last else {},
-        compiler_params=pltpu.CompilerParams(vmem_limit_bytes=VMEM),
-        cost_estimate=pl.CostEstimate(flops=0, bytes_accessed=1000, transcendentals=0),
-    )(code, keep(amp), *[keep(h) for h in held], *tiles)
+        in_specs=[smem] + into + [any_spec] * len(tiles),
+        out_specs=specs,
+        scratch_shapes=scratch,
+        compiler_params=pltpu.CompilerParams(vmem_limit_bytes=limit),
+        cost_estimate=pl.CostEstimate(flops=0, bytes_accessed=guess, transcendentals=0),
+    )(code, *given, *tiles)
 
 
 def per_device(amplitude, integrals, tile_owner, tile_row, tile_col):
@@ -238,7 +280,7 @@
     key = tile_col * count + order
     ahead = (slab[:, None] == slab[None, :]) & (key[None, :] < key[:, None])
     rank = jnp.sum(ahead.astype(jnp.int32), axis=1)
-    fits = rank < total
+    fits = rank < jnp.where(tile_col < LOW, FIRST, total)
     code = ((owners % n_inner) * per_dev + tile_row) * blocks + tile_col
     slots = jnp.arange(n_grp * total, dtype=jnp.int32)[:, None]
     mine = jnp.where(fits, step * total + rank, -1)[None, :] == slots
@@ -267,13 +309,14 @@
         s2 = [parts[9][q] + got_zu[q] + got_zd[q] for q in range(4)]
         f1 = [lax.ppermute(s1[s], "inner", along_z[s]) for s in (1, 3, 2)]
         f2 = [lax.ppermute(s2[s], "inner", along_x[s]) for s in (1, 3, 2)]
-        return [s1[0] + f1[0] + f1[1] + f1[2], s2[0] + f2[0] + f2[1] + f2[2]]
-
-    p1, p3 = pack(integrals, index, ((1, 0, total), (3, 0, total)), total)
+        return [s1[0], *f1, s2[0], *f2]
+
+    p1, p3 = pack(integrals, index, ((1, 0, FIRST), (3, 0, FIRST)), total)
     r1, r3 = lax.ppermute(p1, "grp", along_y[1]), lax.ppermute(p3, "grp", along_y[3])
-    p2, p4, p0 = pack(integrals, index, ((2, 0, FIRST), (2, FIRST, total), (0, 0, total)), total)
-    r2, r4 = lax.ppermute(p2, "grp", along_y[2]), lax.ppermute(p4, "grp", along_y[2])
-    codes, _ = lax.optimization_barrier((codes, p4))
+    p2, p4, p5, p6, p0 = pack(integrals, index, ((2, 0, FIRST), (1, FIRST, total), (2, FIRST, total), (3, FIRST, total), (0, 0, total)), total)
+    r2 = lax.ppermute(p2, "grp", along_y[2])
+    late = [lax.ppermute(p, "grp", along_y[s]) for p, s in ((p4, 1), (p6, 3), (p5, 2))]
+    codes, _ = lax.optimization_barrier((codes, p2))
     note = jnp.concatenate(
         [
             jnp.broadcast_to(codes.reshape(n_grp, 1, total), (n_grp, n_inner, total)),
@@ -289,22 +332,24 @@
     note = jnp.stack([lax.dynamic_index_in_dim(note, core, axis=1, keepdims=False), lax.dynamic_index_in_dim(note, 1 - core, axis=1, keepdims=False)])
     note = note.astype(jnp.int32)
 
-    def codes_of(steps, lo, hi):
-        return jnp.concatenate([note[side, s, lo:hi] for side in range(2) for s in steps])
+    def codes_of(*pieces):
+        return jnp.concatenate([note[side, s, lo:hi] for side in range(2) for s, lo, hi in pieces])
 
     def with_other(tiles):
         return [*tiles, *[lax.ppermute(t, "inner", across) for t in tiles]]
 
-    amp = arrange(where, amp)
-    acc, token = ladder(codes_of((0, 1, 3), 0, total), amp, None, with_other([p0, gate(r1, note), gate(r3, note)]), False, blocks)
-    acc, token = ladder(codes_of((2,), 0, FIRST), amp, acc, with_other([gate(r2, token)]), False, blocks)
-    parts = ladder(codes_of((2,), FIRST, total), amp, acc, with_other([gate(r4, token)]), True, blocks)
+    held = arrange(where, amp)
+    acc, token = ladder(0, codes_of((0, 0, total), (1, 0, FIRST), (3, 0, FIRST)), held, None, with_other([p0, gate(r1, note), gate(r3, note)]), blocks, GUESS[0])
+    *parts, acc, token = ladder(1, codes_of((2, 0, FIRST)), held, acc, with_other([gate(r2, token)]), blocks, GUESS[1])
     pieces = finish(parts)
-    out = jnp.concatenate(pieces, axis=1)
+    late = with_other([gate(r, token) for r in late])
+    parts = ladder(2, codes_of((1, FIRST, total), (3, FIRST, total), (2, FIRST, total)), amp, (where, acc), late, blocks, GUESS[2])
+    pieces += finish(parts)
+    out = small(total_kernel, (rows, width), *pieces)
 
     def with_rest(out):
         rest = jnp.where(fits[:, None, None], 0.0, integrals)
-        return add(out, slow_part(amplitude, rest, tile_owner, tile_row, tile_col))
+        return small(add_kernel, out.shape, out, slow_part(amplitude, rest, tile_owner, tile_row, tile_col))
 
     return lax.cond(overflow, with_rest, lambda out: out, out)
 

time: 229 us -> 242 us (1.057); the launches traced: 230 us -> 240 us
  starting transfers between devices: 38.4 us -> 60.4 us
  waiting for transfers between devices: 105 us -> 86.5 us
  other arithmetic: 8.32 us -> 12.9 us
  local copies, waits for them, and re-layouts: 6.02 us -> 9.23 us
    ppermute x2 -> x4, waiting for transfers between devices: 24.5 us -> 4.82 us  [finish(): lax.ppermute(x_up, 'inner', along_x[1])]
    all_to_all x1, waiting for transfers between devices: 40 us -> 23.3 us  [per_device(): lax.all_to_all(note.reshape(devices, total + 1), AXES, split_axis=0, conc...]
    all_gather x1, waiting for transfers between devices: 0.01 us -> 14.7 us  [per_device(): lax.all_gather(amplitude, 'inner', axis=0, axis_index_groups=same_core)]
    ppermute x3 -> x6, waiting for transfers between devices: 6.89 us -> 0.02 us  [finish(): f2 = [lax.ppermute(s2[s], 'inner', along_x[s]) for s in (1, 3, 2)]]
    ppermute x2 -> x4, waiting for transfers between devices: 1.8 us -> 8.46 us  [finish(): lax.ppermute(z_up, 'inner', along_z[1])]
    ppermute x2 -> x4, waiting for transfers between devices: 0.01 us -> 6.27 us  [finish(): lax.ppermute(z_down, 'inner', along_z[3])]
    ppermute x5 -> x7, waiting for transfers between devices: 6.17 us -> 0.41 us  [with_other(): return [*tiles, *[lax.ppermute(t, 'inner', across) for t in tiles]]]
    ppermute x2 -> x4, starting transfers between devices: 5.65 us -> 11.2 us  [finish(): lax.ppermute(x_down, 'inner', along_x[3])]
  transfers between devices with their start and end apart: 25 -> 43, of which waited for: 13 -> 13; matrix products, arithmetic and copies ran while one was open for 4% -> 6% of each run, Pallas kernels for 22% -> 23%
where the time goes in v1:
time: 242 us; the launch traced here: 240 us
  waiting for transfers between devices  86.5 us (36%)
  starting transfers between devices  60.4 us (25%)
  Pallas kernels  56 us (23%)
  between operations  14.7 us (6%)
  other arithmetic  12.9 us (5%)
  local copies, waits for them, and re-layouts  9.23 us (4%)
    pallas_call x3, Pallas kernels, ladder(): pl.pallas_call(functools.partial(ladder_kernel, step, counts, LOW), out_s...  38.6 us
    all_to_all x1, waiting for transfers between devices, per_device(): lax.all_to_all(note.reshape(devices, total + 1), AXES, split_axis=0, conc...  23.3 us
    ppermute x3, waiting for transfers between devices, per_device(): lax.ppermute(p, 'grp', along_y[s])  16.3 us
    pallas_call x2, Pallas kernels, pack(): pl.pallas_call(functools.partial(pack_kernel, spans, total), out_shape=[j...  16.1 us
    all_gather x1, waiting for transfers between devices, per_device(): lax.all_gather(amplitude, 'inner', axis=0, axis_index_groups=same_core)  14.7 us
    ppermute x4, starting transfers between devices, finish(): lax.ppermute(x_down, 'inner', along_x[3])  11.2 us
    all_to_all x1, starting transfers between devices, per_device(): lax.all_to_all(note.reshape(devices, total + 1), AXES, split_axis=0, conc...  10 us
    unnamed x30, local copies, waits for them, and re-layouts  8.88 us
  transfers between devices with their start and end apart: 43, of which 13 were waited for; matrix products, arithmetic and copies ran while one was open for 6% of the time, Pallas kernels for 23%

profile of v1, /device:TPU:0, one launch (start us, length us, event | category | flops | bytes accessed | tf_op | source)
XLA Modules:
  0.0 240.0 jit_solution(4913362246320397802)
XLA Ops:
  6.5 0.7 all-gather.3.cloned.1.call-update
  7.3 0.8 fusion.39
  8.1 0.8 and_select_fusion.2
  9.1 1.7 fusion.37
  10.9 4.0 %shard_map.59 = (f32[30,128,128]{2,1,0:T(8,128)}, f32[30,128,128]{2,1,0:T(8,128)S(1)}) custom-call(s32[160]{0:T(256)S(1)} %select_reduce_fusion.index, f32[128,128,128]{2,1,0:T(8,128)} %tiles.3), custom_call_target="tpu_custom_call" | custom-call | bytes 1000 | tf_op jit(solution)/shard_map/pallas_call | solution.py:61
  14.9 1.7 collective-permute-start
  16.6 1.6 collective-permute-start.1
  18.2 12.1 %shard_map.57 = (f32[30,128,128]{2,1,0:T(8,128)S(1)}, f32[10,128,128]{2,1,0:T(8,128)}, f32[10,128,128]{2,1,0:T(8,128)}, f32[10,128,128]{2,1,0:T(8,128)}, f32[40,128,128]{2,1,0:T(8,128)}) custom-call(s32[160]{0:T(256)S(1)} %select_reduce_fusion.index, f32[128,128,128]{2,1,0:T(8,128)S(1)} %copy-done.5), custom_call_target="tpu_custom_call" | custom-call | bytes 1000 | tf_op jit(solution)/shard_map/pallas_call | solution.py:61
  30.3 1.3 copy-done.4
  31.8 1.2 pad_convert_fusion
  33.0 10.0 %all-to-all-start.3 = ((f32[128,1,41]{2,1,0:T(1,128)}), f32[128,1,41]{2,1,0:T(1,128)S(1)}, u32[]{:S(2)}, u32[]{:S(2)}) async-start(f32[128,1,41]{2,1,0:T(1,128)} %bitcast.13), calls=%async_computation.4 | async-start | bytes 131072 | tf_op jit(solution)/shard_map/all_to_all | solution.py:327
  43.2 23.3 %all-to-all-done.3 = f32[128,1,41]{2,1,0:T(1,128)S(1)} async-done(((f32[128,1,41]{2,1,0:T(1,128)}), f32[128,1,41]{2,1,0:T(1,128)S(1)}, u32[]{:S(2)}, u32[]{:S(2)}) %all-to-all-start.3) | async-done | bytes 21024 | tf_op jit(solution)/shard_map/all_to_all | solution.py:327
  66.6 0.5 collective-permute-start.4
  67.1 1.5 collective-permute-start.5
  68.8 14.7 %all-gather.3.cloned.1.call-done = f32[128,16384]{1,0:T(8,128)} async-done(((f32[8,16384]{1,0:T(8,128)}), f32[128,16384]{1,0:T(8,128)}) %all-gather.3.cloned.1.call-update) | async-done | bytes 8388624 | tf_op jit(solution)/shard_map/all_gather | solution.py:274
  83.5 3.4 %copy-done = f32[128,16384]{1,0:T(8,128)S(1)} copy-done((f32[128,16384]{1,0:T(8,128)S(1)}, f32[128,16384]{1,0:T(8,128)}, u32[]{:S(2)}) %copy-start) | copy-done | bytes 8388632
  86.9 1.2 shard_map.58.refs_1_
  88.1 22.1 %shard_map.62 = (f32[4,4,8,16384]{3,2,1,0:T(8,128)S(1)}, f32[8,128]{1,0:T(8,128)S(1)}) custom-call(s32[200]{0:T(256)S(1)} %concatenate.38.refs_0_, f32[16,8,16384]{2,1,0:T(8,128)S(1)} %shard_map.58.refs_1_, f32[40,128,128]{2,1,0:T(8,128)} %get-tuple-element.64.refs_2_, f32[30,128,128]{2,1,0:T(8,128)} %shard_map.60.refs_3_, ...), custom_call_target="tpu_custom_call" | custom-call | bytes 80000000 | tf_op jit(solution)/shard_map/pallas_call | solution.py:242
  110.2 3.5 %collective-permute-done.5.refs_0_ = f32[30,128,128]{2,1,0:T(8,128)S(1)} collective-permute-done((f32[30,128,128]{2,1,0:T(8,128)}, f32[30,128,128]{2,1,0:T(8,128)S(1)}, u32[]{:S(2)}, u32[]{:S(2)}) %collective-permute-start.5) | collective-permute-done | bytes 1966112 | tf_op jit(solution)/shard_map/ppermute | solution.py:317
  113.7 0.9 collective-permute-start.21
  114.6 2.3 collective-permute-start.22
  117.2 0.4 collective-permute-done.6.refs_4_
  117.6 10.9 %shard_map.64 = (f32[2,8,4096]{2,1,0:T(8,128)}, f32[2,8,4096]{2,1,0:T(8,128)}, f32[2,8,4096]{2,1,0:T(8,128)}, f32[2,8,4096]{2,1,0:T(8,128)}, f32[4,8,4096]{2,1,0...) custom-call(s32[60]{0:T(128)S(1)} %pad_add_fusion.refs_0_, ...), custom_call_target="tpu_custom_call" | custom-call | bytes 35000000 | tf_op jit(solution)/shard_map/pallas_call | solution.py:242
  128.6 1.4 collective-permute-start.14
  130.1 16.3 %collective-permute-done.21.refs_0_ = f32[10,128,128]{2,1,0:T(8,128)} collective-permute-done((f32[10,128,128]{2,1,0:T(8,128)}, f32[10,128,128]{2,1,0:T(8,128)}, u32[]{:S(2)}, u32[]{:S(2)}) %collective-permute-start.21) | collective-permute-done | bytes 655392 | tf_op jit(solution)/shard_map/ppermute | solution.py:318
  146.4 0.5 collective-permute-start.25
  147.0 1.5 collective-permute-start.7
  148.5 1.1 slice_add_fusion.5
  149.6 6.3 %collective-permute-done.16 = f32[2,8,4096]{2,1,0:T(8,128)S(1)} collective-permute-done((f32[2,8,4096]{2,1,0:T(8,128)}, f32[2,8,4096]{2,1,0:T(8,128)S(1)}, u32[]{:S(2)}, u32[]{:S(2)}) %collective-permute-start.16) | collective-permute-done | bytes 262176 | tf_op jit(solution)/shard_map/ppermute | solution.py:297
  155.9 2.8 %collective-permute-start.9 = (f32[2,8,4096]{2,1,0:T(8,128)}, f32[2,8,4096]{2,1,0:T(8,128)S(1)}, u32[]{:S(2)}, u32[]{:S(2)}) collective-permute-start(f32[2,8,4096]{2,1,0:T(8,128)} %get-tuple-element.73), channel_id=1, source_target_pairs={{0,6},{1,7},{2,0},{3,1},{4,2},{5,3},{6,4},{7,5},{8,14},{9,15},{10,... | collective-permute-start | bytes 786440 | tf_op jit(solution)/shard_map/ppermute | solution.py:296
  158.6 1.1 fusion.43
  159.7 1.0 collective-permute-start.15
  160.7 1.1 slice_add_fusion.7
  161.8 2.5 %collective-permute-done.9 = f32[2,8,4096]{2,1,0:T(8,128)S(1)} collective-permute-done((f32[2,8,4096]{2,1,0:T(8,128)}, f32[2,8,4096]{2,1,0:T(8,128)S(1)}, u32[]{:S(2)}, u32[]{:S(2)}) %collective-permute-start.9) | collective-permute-done | bytes 262176 | tf_op jit(solution)/shard_map/ppermute | solution.py:296
  164.3 1.7 collective-permute-start.17
  166.1 1.2 collective-permute-start.8
  167.3 2.7 %collective-permute-start.10 = (f32[4,8,4096]{2,1,0:T(8,128)S(1)}, f32[4,8,4096]{2,1,0:T(8,128)S(1)}, u32[]{:S(2)}, u32[]{:S(2)}) collective-permute-start(f32[4,8,4096]{2,1,0:T(8,128)S(1)} %pad_maximum_fusion.1), channel_id=1, source_target_pairs={{0,6},{1,7},{2,0},{3,1},{4,2},{5,3},{6,4},{7,5},{8,14},{9,15},{10,... | collective-permute-start | bytes 1572872 | tf_op jit(solution)/shard_map/ppermute | solution.py:306
  170.1 3.4 %copy-done.1 = f32[128,16384]{1,0:T(8,128)S(1)} copy-done((f32[128,16384]{1,0:T(8,128)S(1)}, f32[128,16384]{1,0:T(8,128)}, u32[]{:S(2)}) %copy-start.1) | copy-done | bytes 8388632
  173.5 5.5 %shard_map.68 = (f32[2,8,4096]{2,1,0:T(8,128)}, f32[2,8,4096]{2,1,0:T(8,128)}, f32[2,8,4096]{2,1,0:T(8,128)}, f32[2,8,4096]{2,1,0:T(8,128)}, f32[4,8,4096]{2,1,0...) custom-call(s32[60]{0:T(128)S(1)} %concatenate.43.refs_0_, ...), custom_call_target="tpu_custom_call" | custom-call | bytes 20000000 | tf_op jit(solution)/shard_map/pallas_call | solution.py:242
  179.0 1.0 collective-permute-start.34
  180.1 2.3 collective-permute-start.36
  182.5 3.3 %collective-permute-start.29 = (f32[2,8,4096]{2,1,0:T(8,128)}, f32[2,8,4096]{2,1,0:T(8,128)S(1)}, u32[]{:S(2)}, u32[]{:S(2)}) collective-permute-start(f32[2,8,4096]{2,1,0:T(8,128)} %get-tuple-element.88), channel_id=1, source_target_pairs={{0,6},{1,7},{2,0},{3,1},{4,2},{5,3},{6,4},{7,5},{8,14},{9,15},{10,... | collective-permute-start | bytes 786440 | tf_op jit(solution)/shard_map/ppermute | solution.py:296
  185.9 1.3 collective-permute-done.34
  187.2 2.0 collective-permute-start.19
  189.2 1.1 slice_add_fusion.1
  190.4 1.1 fusion.41
  191.6 1.1 slice_add_fusion.3
  192.7 3.3 %collective-permute-start.37 = (f32[4,8,4096]{2,1,0:T(8,128)S(1)}, f32[4,8,4096]{2,1,0:T(8,128)S(1)}, u32[]{:S(2)}, u32[]{:S(2)}) collective-permute-start(f32[4,8,4096]{2,1,0:T(8,128)S(1)} %pad_maximum_fusion.7), channel_id=1, source_target_pairs={{0,24},{1,25},{2,26},{3,27},{4,28},{5,29},{6,30},{7,31},{8,0},{9,1... | collective-permute-start | bytes 1572872 | tf_op jit(solution)/shard_map/ppermute | solution.py:307
  196.2 7.2 %collective-permute-done.35 = f32[4,8,4096]{2,1,0:T(8,128)S(1)} collective-permute-done((f32[4,8,4096]{2,1,0:T(8,128)S(1)}, f32[4,8,4096]{2,1,0:T(8,128)S(1)}, u32[]{:S(2)}, u32[]{:S(2)}) %collective-permute-start.35) | collective-permute-done | bytes 524320 | tf_op jit(solution)/shard_map/ppermute | solution.py:307
  203.4 0.9 collective-permute-start.28
  204.2 2.4 %collective-permute-start.30 = (f32[4,8,4096]{2,1,0:T(8,128)S(1)}, f32[4,8,4096]{2,1,0:T(8,128)S(1)}, u32[]{:S(2)}, u32[]{:S(2)}) collective-permute-start(f32[4,8,4096]{2,1,0:T(8,128)S(1)} %pad_maximum_fusion.5), channel_id=1, source_target_pairs={{0,6},{1,7},{2,0},{3,1},{4,2},{5,3},{6,4},{7,5},{8,14},{9,15},{10,... | collective-permute-start | bytes 1572872 | tf_op jit(solution)/shard_map/ppermute | solution.py:306
  206.8 3.8 %collective-permute-start.12 = (f32[8,4096]{1,0:T(8,128)S(1)}, f32[8,4096]{1,0:T(8,128)S(1)}, u32[]{:S(2)}, u32[]{:S(2)}) collective-permute-start(f32[8,4096]{1,0:T(8,128)S(1)} %get-tuple-element.110), channel_id=1, source_target_pairs={{0,24},{1,25},{2,26},{3,27},{4,28},{5,29},{6,30},{7,31},{8,0},{9,1... | collective-permute-start | bytes 393224 | tf_op jit(solution)/shard_map/ppermute | solution.py:310
  210.6 4.8 %collective-permute-done.28 = f32[4,8,4096]{2,1,0:T(8,128)S(1)} collective-permute-done((f32[4,8,4096]{2,1,0:T(8,128)S(1)}, f32[4,8,4096]{2,1,0:T(8,128)S(1)}, u32[]{:S(2)}, u32[]{:S(2)}) %collective-permute-start.28) | collective-permute-done | bytes 524320 | tf_op jit(solution)/shard_map/ppermute | solution.py:306
  215.4 0.7 collective-permute-done.30
  216.2 0.8 collective-permute-start.38
  217.0 3.1 %collective-permute-start.39 = (f32[8,4096]{1,0:T(8,128)S(1)}, f32[8,4096]{1,0:T(8,128)S(1)}, u32[]{:S(2)}, u32[]{:S(2)}) collective-permute-start(f32[8,4096]{1,0:T(8,128)S(1)} %get-tuple-element.98), channel_id=1, source_target_pairs={{0,6},{1,7},{2,0},{3,1},{4,2},{5,3},{6,4},{7,5},{8,14},{9,15},{10,... | collective-permute-start | bytes 393224 | tf_op jit(solution)/shard_map/ppermute | solution.py:311
  220.2 1.6 collective-permute-start.40
  221.7 1.2 collective-permute-done.13.refs_3_
  222.9 2.5 %collective-permute-start.32 = (f32[8,4096]{1,0:T(8,128)S(1)}, f32[8,4096]{1,0:T(8,128)S(1)}, u32[]{:S(2)}, u32[]{:S(2)}) collective-permute-start(f32[8,4096]{1,0:T(8,128)S(1)} %get-tuple-element.102), channel_id=1, source_target_pairs={{0,24},{1,25},{2,26},{3,27},{4,28},{5,29},{6,30},{7,31},{8,0},{9,1... | collective-permute-start | bytes 393224 | tf_op jit(solution)/shard_map/ppermute | solution.py:310
  225.5 1.5 collective-permute-start.33
  227.0 0.7 slice_reduce_fusion
  228.4 3.6 %collective-permute-done.33.refs_11_ = f32[8,4096]{1,0:T(8,128)S(1)} collective-permute-done((f32[8,4096]{1,0:T(8,128)S(1)}, f32[8,4096]{1,0:T(8,128)S(1)}, u32[]{:S(2)}, u32[]{:S(2)}) %collective-permute-start.33) | collective-permute-done | bytes 131104 | tf_op jit(solution)/shard_map/ppermute | solution.py:310
  232.1 0.3 conditional.1
  232.4 0.8 copy-done.6
  (110 shorter events, 2.6 us)
Async XLA Ops:
  6.5 76.9 %all-gather.3.cloned.1.call-start = ((), (), s32[]{:S(2)}) async-start(), calls=%async_computation.6 | async-start | bytes 8912896 | tf_op jit(solution)/shard_map/all_gather | solution.py:274
  7.3 11.0 %copy-start.5 = (f32[128,128,128]{2,1,0:T(8,128)S(1)}, f32[128,128,128]{2,1,0:T(8,128)}, u32[]{:S(2)}) copy-start(f32[128,128,128]{2,1,0:T(8,128)} %tiles.3) | copy-start | bytes 25165828
  14.9 51.6 %collective-permute-start = (f32[30,128,128]{2,1,0:T(8,128)}, f32[30,128,128]{2,1,0:T(8,128)}, u32[]{:S(2)}, u32[]{:S(2)}) collective-permute-start(f32[30,128,128]{2,1,0:T(8,128)} %get-tuple-element.65), channel_id=1, source_target_pairs={{0,32},{32,64},{64,96},{96,0},{1,33},{33,65},{65,97},{97,1},{2,34}... | collective-permute-start | bytes 5898248 | tf_op jit(solution)/shard_map/ppermute | solution.py:315
  16.6 50.0 %collective-permute-start.1 = (f32[30,128,128]{2,1,0:T(8,128)S(1)}, f32[30,128,128]{2,1,0:T(8,128)}, u32[]{:S(2)}, u32[]{:S(2)}) collective-permute-start(f32[30,128,128]{2,1,0:T(8,128)S(1)} %get-tuple-element.66), channel_id=1, source_target_pairs={{0,96},{32,0},{64,32},{96,64},{1,97},{33,1},{65,33},{97,65},{2,98}... | collective-permute-start | bytes 5898248 | tf_op jit(solution)/shard_map/ppermute | solution.py:315
  30.3 1.3 copy-start.4
  31.6 56.4 %collective-permute-start.2 = (f32[40,128,128]{2,1,0:T(8,128)}, f32[40,128,128]{2,1,0:T(8,128)}, u32[]{:S(2)}, u32[]{:S(2)}) collective-permute-start(f32[40,128,128]{2,1,0:T(8,128)} %get-tuple-element.64.refs_2_), channel_id=1, source_target_pairs={{0,1},{1,0},{2,3},{3,2},{4,5},{5,4},{6,7},{7,6},{8,9},{9,8},{10,11... | collective-permute-start | bytes 7864328 | tf_op jit(solution)/shard_map/ppermute | solution.py:339
  33.0 33.4 %all-to-all-start.3 = ((f32[128,1,41]{2,1,0:T(1,128)}), f32[128,1,41]{2,1,0:T(1,128)S(1)}, u32[]{:S(2)}, u32[]{:S(2)}) async-start(f32[128,1,41]{2,1,0:T(1,128)} %bitcast.13), calls=%async_computation.4 | async-start | bytes 131072 | tf_op jit(solution)/shard_map/all_to_all | solution.py:327
  66.5 21.5 %collective-permute-start.3 = (f32[30,128,128]{2,1,0:T(8,128)}, f32[30,128,128]{2,1,0:T(8,128)}, u32[]{:S(2)}, u32[]{:S(2)}) collective-permute-start(f32[30,128,128]{2,1,0:T(8,128)} %shard_map.60.refs_3_), channel_id=1, source_target_pairs={{0,1},{1,0},{2,3},{3,2},{4,5},{5,4},{6,7},{7,6},{8,9},{9,8},{10,11... | collective-permute-start | bytes 5898248 | tf_op jit(solution)/shard_map/ppermute | solution.py:339
  66.6 21.4 %collective-permute-start.4 = (f32[30,128,128]{2,1,0:T(8,128)}, f32[30,128,128]{2,1,0:T(8,128)}, u32[]{:S(2)}, u32[]{:S(2)}) collective-permute-start(f32[30,128,128]{2,1,0:T(8,128)} %shard_map.61.refs_4_), channel_id=1, source_target_pairs={{0,1},{1,0},{2,3},{3,2},{4,5},{5,4},{6,7},{7,6},{8,9},{9,8},{10,11... | collective-permute-start | bytes 5898248 | tf_op jit(solution)/shard_map/ppermute | solution.py:339
  67.1 46.6 %collective-permute-start.5 = (f32[30,128,128]{2,1,0:T(8,128)}, f32[30,128,128]{2,1,0:T(8,128)S(1)}, u32[]{:S(2)}, u32[]{:S(2)}) collective-permute-start(f32[30,128,128]{2,1,0:T(8,128)} %copy-done.4), channel_id=1, source_target_pairs={{0,64},{32,96},{64,0},{96,32},{1,65},{33,97},{65,1},{97,33},{2,66}... | collective-permute-start | bytes 5898248 | tf_op jit(solution)/shard_map/ppermute | solution.py:317
  83.5 3.4 %copy-start = (f32[128,16384]{1,0:T(8,128)S(1)}, f32[128,16384]{1,0:T(8,128)}, u32[]{:S(2)}) copy-start(f32[128,16384]{1,0:T(8,128)} %all-gather.3.cloned.1.call-done) | copy-start | bytes 25165828
  113.7 4.0 %collective-permute-start.6 = (f32[30,128,128]{2,1,0:T(8,128)S(1)}, f32[30,128,128]{2,1,0:T(8,128)S(1)}, u32[]{:S(2)}, u32[]{:S(2)}) collective-permute-start(f32[30,128,128]{2,1,0:T(8,128)S(1)} %shard_map.63.refs_3_), channel_id=1, source_target_pairs={{0,1},{1,0},{2,3},{3,2},{4,5},{5,4},{6,7},{7,6},{8,9},{9,8},{10,11... | collective-permute-start | bytes 5898248 | tf_op jit(solution)/shard_map/ppermute | solution.py:339
  113.7 32.7 %collective-permute-start.21 = (f32[10,128,128]{2,1,0:T(8,128)}, f32[10,128,128]{2,1,0:T(8,128)}, u32[]{:S(2)}, u32[]{:S(2)}) collective-permute-start(f32[10,128,128]{2,1,0:T(8,128)} %get-tuple-element.80), channel_id=1, source_target_pairs={{0,32},{32,64},{64,96},{96,0},{1,33},{33,65},{65,97},{97,1},{2,34}... | collective-permute-start | bytes 1966088 | tf_op jit(solution)/shard_map/ppermute | solution.py:318
  114.6 31.8 %collective-permute-start.22 = (f32[10,128,128]{2,1,0:T(8,128)}, f32[10,128,128]{2,1,0:T(8,128)S(1)}, u32[]{:S(2)}, u32[]{:S(2)}) collective-permute-start(f32[10,128,128]{2,1,0:T(8,128)} %get-tuple-element.82), channel_id=1, source_target_pairs={{0,96},{32,0},{64,32},{96,64},{1,97},{33,1},{65,33},{97,65},{2,98}... | collective-permute-start | bytes 1966088 | tf_op jit(solution)/shard_map/ppermute | solution.py:318
  116.9 30.0 %collective-permute-start.23 = (f32[10,128,128]{2,1,0:T(8,128)}, f32[10,128,128]{2,1,0:T(8,128)S(1)}, u32[]{:S(2)}, u32[]{:S(2)}) collective-permute-start(f32[10,128,128]{2,1,0:T(8,128)} %get-tuple-element.83), channel_id=1, source_target_pairs={{0,64},{32,96},{64,0},{96,32},{1,65},{33,97},{65,1},{97,33},{2,66}... | collective-permute-start | bytes 1966088 | tf_op jit(solution)/shard_map/ppermute | solution.py:318
  128.6 37.4 %copy-start.8 = (f32[4,8,4096]{2,1,0:T(8,128)S(1)}, f32[4,8,4096]{2,1,0:T(8,128)}, u32[]{:S(2)}) copy-start(f32[4,8,4096]{2,1,0:T(8,128)} %get-tuple-element.72) | copy-start | bytes 1572868
  128.6 18.4 %collective-permute-start.14 = (f32[2,8,4096]{2,1,0:T(8,128)}, f32[2,8,4096]{2,1,0:T(8,128)S(1)}, u32[]{:S(2)}, u32[]{:S(2)}) collective-permute-start(f32[2,8,4096]{2,1,0:T(8,128)} %get-tuple-element.76), channel_id=1, source_target_pairs={{0,8},{1,9},{2,10},{3,11},{4,12},{5,13},{6,14},{7,15},{8,16},{9,17... | collective-permute-start | bytes 786440 | tf_op jit(solution)/shard_map/ppermute | solution.py:297
  130.1 40.0 %copy-start.2 = (f32[4,4,8,8192]{3,2,1,0:T(8,128)S(1)}, f32[4,4,8,8192]{3,2,1,0:T(8,128)}, u32[]{:S(2)}) copy-start(f32[4,4,8,8192]{3,2,1,0:T(8,128)} %get-tuple-element.79.refs_3_) | copy-start | bytes 12582916
  146.4 19.7 %collective-permute-start.24 = (f32[10,128,128]{2,1,0:T(8,128)}, f32[10,128,128]{2,1,0:T(8,128)S(1)}, u32[]{:S(2)}, u32[]{:S(2)}) collective-permute-start(f32[10,128,128]{2,1,0:T(8,128)} %shard_map.65.refs_4_), channel_id=1, source_target_pairs={{0,1},{1,0},{2,3},{3,2},{4,5},{5,4},{6,7},{7,6},{8,9},{9,8},{10,11... | collective-permute-start | bytes 1966088 | tf_op jit(solution)/shard_map/ppermute | solution.py:339
  146.4 20.9 %collective-permute-start.25 = (f32[10,128,128]{2,1,0:T(8,128)S(1)}, f32[10,128,128]{2,1,0:T(8,128)S(1)}, u32[]{:S(2)}, u32[]{:S(2)}) collective-permute-start(f32[10,128,128]{2,1,0:T(8,128)S(1)} %shard_map.66.refs_5_), channel_id=1, source_target_pairs={{0,1},{1,0},{2,3},{3,2},{4,5},{5,4},{6,7},{7,6},{8,9},{9,8},{10,11... | collective-permute-start | bytes 1966088 | tf_op jit(solution)/shard_map/ppermute | solution.py:339
  146.9 23.2 %collective-permute-start.26 = (f32[10,128,128]{2,1,0:T(8,128)S(1)}, f32[10,128,128]{2,1,0:T(8,128)S(1)}, u32[]{:S(2)}, u32[]{:S(2)}) collective-permute-start(f32[10,128,128]{2,1,0:T(8,128)S(1)} %shard_map.67.refs_6_), channel_id=1, source_target_pairs={{0,1},{1,0},{2,3},{3,2},{4,5},{5,4},{6,7},{7,6},{8,9},{9,8},{10,11... | collective-permute-start | bytes 1966088 | tf_op jit(solution)/shard_map/ppermute | solution.py:339
  147.0 8.9 %collective-permute-start.16 = (f32[2,8,4096]{2,1,0:T(8,128)}, f32[2,8,4096]{2,1,0:T(8,128)S(1)}, u32[]{:S(2)}, u32[]{:S(2)}) collective-permute-start(f32[2,8,4096]{2,1,0:T(8,128)} %get-tuple-element.78), channel_id=1, source_target_pairs={{0,24},{1,25},{2,26},{3,27},{4,28},{5,29},{6,30},{7,31},{8,0},{9,1... | collective-permute-start | bytes 786440 | tf_op jit(solution)/shard_map/ppermute | solution.py:297
  147.0 12.7 %collective-permute-start.7 = (f32[2,8,4096]{2,1,0:T(8,128)}, f32[2,8,4096]{2,1,0:T(8,128)S(1)}, u32[]{:S(2)}, u32[]{:S(2)}) collective-permute-start(f32[2,8,4096]{2,1,0:T(8,128)} %get-tuple-element.71), channel_id=1, source_target_pairs={{0,2},{1,3},{2,4},{3,5},{4,6},{5,7},{6,0},{7,1},{8,10},{9,11},{10,... | collective-permute-start | bytes 786440 | tf_op jit(solution)/shard_map/ppermute | solution.py:296
  155.9 8.4 %collective-permute-start.9 = (f32[2,8,4096]{2,1,0:T(8,128)}, f32[2,8,4096]{2,1,0:T(8,128)S(1)}, u32[]{:S(2)}, u32[]{:S(2)}) collective-permute-start(f32[2,8,4096]{2,1,0:T(8,128)} %get-tuple-element.73), channel_id=1, source_target_pairs={{0,6},{1,7},{2,0},{3,1},{4,2},{5,3},{6,4},{7,5},{8,14},{9,15},{10,... | collective-permute-start | bytes 786440 | tf_op jit(solution)/shard_map/ppermute | solution.py:296
  159.7 20.3 %collective-permute-start.15 = (f32[4,8,4096]{2,1,0:T(8,128)S(1)}, f32[4,8,4096]{2,1,0:T(8,128)S(1)}, u32[]{:S(2)}, u32[]{:S(2)}) collective-permute-start(f32[4,8,4096]{2,1,0:T(8,128)S(1)} %pad_maximum_fusion.2), channel_id=1, source_target_pairs={{0,8},{1,9},{2,10},{3,11},{4,12},{5,13},{6,14},{7,15},{8,16},{9,17... | collective-permute-start | bytes 1572872 | tf_op jit(solution)/shard_map/ppermute | solution.py:307
  164.3 18.1 %collective-permute-start.17 = (f32[4,8,4096]{2,1,0:T(8,128)S(1)}, f32[4,8,4096]{2,1,0:T(8,128)S(1)}, u32[]{:S(2)}, u32[]{:S(2)}) collective-permute-start(f32[4,8,4096]{2,1,0:T(8,128)S(1)} %pad_maximum_fusion.3), channel_id=1, source_target_pairs={{0,24},{1,25},{2,26},{3,27},{4,28},{5,29},{6,30},{7,31},{8,0},{9,1... | collective-permute-start | bytes 1572872 | tf_op jit(solution)/shard_map/ppermute | solution.py:307
  166.1 16.3 %copy-start.10 = (f32[4,8,4096]{2,1,0:T(8,128)S(1)}, f32[4,8,4096]{2,1,0:T(8,128)}, u32[]{:S(2)}) copy-start(f32[4,8,4096]{2,1,0:T(8,128)} %get-tuple-element.74) | copy-start | bytes 1572868
  166.1 16.3 %collective-permute-start.8 = (f32[4,8,4096]{2,1,0:T(8,128)S(1)}, f32[4,8,4096]{2,1,0:T(8,128)S(1)}, u32[]{:S(2)}, u32[]{:S(2)}) collective-permute-start(f32[4,8,4096]{2,1,0:T(8,128)S(1)} %pad_maximum_fusion), channel_id=1, source_target_pairs={{0,2},{1,3},{2,4},{3,5},{4,6},{5,7},{6,0},{7,1},{8,10},{9,11},{10,... | collective-permute-start | bytes 1572872 | tf_op jit(solution)/shard_map/ppermute | solution.py:306
  167.3 18.4 %collective-permute-start.10 = (f32[4,8,4096]{2,1,0:T(8,128)S(1)}, f32[4,8,4096]{2,1,0:T(8,128)S(1)}, u32[]{:S(2)}, u32[]{:S(2)}) collective-permute-start(f32[4,8,4096]{2,1,0:T(8,128)S(1)} %pad_maximum_fusion.1), channel_id=1, source_target_pairs={{0,6},{1,7},{2,0},{3,1},{4,2},{5,3},{6,4},{7,5},{8,14},{9,15},{10,... | collective-permute-start | bytes 1572872 | tf_op jit(solution)/shard_map/ppermute | solution.py:306
  170.1 3.4 %copy-start.1 = (f32[128,16384]{1,0:T(8,128)S(1)}, f32[128,16384]{1,0:T(8,128)}, u32[]{:S(2)}) copy-start(f32[128,16384]{1,0:T(8,128)} %all-gather.3.cloned.1.call-done) | copy-start | bytes 25165828
  173.5 12.3 %copy-start.9 = (f32[4,8,4096]{2,1,0:T(8,128)S(1)}, f32[4,8,4096]{2,1,0:T(8,128)}, u32[]{:S(2)}) copy-start(f32[4,8,4096]{2,1,0:T(8,128)} %get-tuple-element.69) | copy-start | bytes 1572868
  179.0 17.0 %copy-start.7 = (f32[4,8,4096]{2,1,0:T(8,128)S(1)}, f32[4,8,4096]{2,1,0:T(8,128)}, u32[]{:S(2)}) copy-start(f32[4,8,4096]{2,1,0:T(8,128)} %get-tuple-element.87) | copy-start | bytes 1572868
  179.0 27.6 %copy-start.12 = (f32[4,8,4096]{2,1,0:T(8,128)S(1)}, f32[4,8,4096]{2,1,0:T(8,128)}, u32[]{:S(2)}) copy-start(f32[4,8,4096]{2,1,0:T(8,128)} %get-tuple-element.89) | copy-start | bytes 1572868
  179.0 37.9 %copy-start.11 = (f32[4,8,4096]{2,1,0:T(8,128)S(1)}, f32[4,8,4096]{2,1,0:T(8,128)}, u32[]{:S(2)}) copy-start(f32[4,8,4096]{2,1,0:T(8,128)} %get-tuple-element.84) | copy-start | bytes 1572868
  179.0 8.1 %collective-permute-start.34 = (f32[2,8,4096]{2,1,0:T(8,128)}, f32[2,8,4096]{2,1,0:T(8,128)S(1)}, u32[]{:S(2)}, u32[]{:S(2)}) collective-permute-start(f32[2,8,4096]{2,1,0:T(8,128)} %get-tuple-element.91), channel_id=1, source_target_pairs={{0,8},{1,9},{2,10},{3,11},{4,12},{5,13},{6,14},{7,15},{8,16},{9,17... | collective-permute-start | bytes 786440 | tf_op jit(solution)/shard_map/ppermute | solution.py:297
  180.1 10.2 %collective-permute-start.36 = (f32[2,8,4096]{2,1,0:T(8,128)}, f32[2,8,4096]{2,1,0:T(8,128)S(1)}, u32[]{:S(2)}, u32[]{:S(2)}) collective-permute-start(f32[2,8,4096]{2,1,0:T(8,128)} %get-tuple-element.93), channel_id=1, source_target_pairs={{0,24},{1,25},{2,26},{3,27},{4,28},{5,29},{6,30},{7,31},{8,0},{9,1... | collective-permute-start | bytes 786440 | tf_op jit(solution)/shard_map/ppermute | solution.py:297
  182.4 9.1 %collective-permute-start.27 = (f32[2,8,4096]{2,1,0:T(8,128)}, f32[2,8,4096]{2,1,0:T(8,128)S(1)}, u32[]{:S(2)}, u32[]{:S(2)}) collective-permute-start(f32[2,8,4096]{2,1,0:T(8,128)} %get-tuple-element.86), channel_id=1, source_target_pairs={{0,2},{1,3},{2,4},{3,5},{4,6},{5,7},{6,0},{7,1},{8,10},{9,11},{10,... | collective-permute-start | bytes 786440 | tf_op jit(solution)/shard_map/ppermute | solution.py:296
  182.5 10.3 %collective-permute-start.29 = (f32[2,8,4096]{2,1,0:T(8,128)}, f32[2,8,4096]{2,1,0:T(8,128)S(1)}, u32[]{:S(2)}, u32[]{:S(2)}) collective-permute-start(f32[2,8,4096]{2,1,0:T(8,128)} %get-tuple-element.88), channel_id=1, source_target_pairs={{0,6},{1,7},{2,0},{3,1},{4,2},{5,3},{6,4},{7,5},{8,14},{9,15},{10,... | collective-permute-start | bytes 786440 | tf_op jit(solution)/shard_map/ppermute | solution.py:296
  185.8 21.0 %collective-permute-start.18 = (f32[8,4096]{1,0:T(8,128)S(1)}, f32[8,4096]{1,0:T(8,128)S(1)}, u32[]{:S(2)}, u32[]{:S(2)}) collective-permute-start(f32[8,4096]{1,0:T(8,128)S(1)} %get-tuple-element.107), channel_id=1, source_target_pairs={{0,2},{1,3},{2,4},{3,5},{4,6},{5,7},{6,0},{7,1},{8,10},{9,11},{10,... | collective-permute-start | bytes 393224 | tf_op jit(solution)/shard_map/ppermute | solution.py:311
  185.9 46.2 %copy-start.13 = (s32[128,1]{0,1:T(1,128)S(1)}, s32[128,1]{0,1:T(1,128)}, u32[]{:S(2)}) copy-start(s32[128,1]{0,1:T(1,128)} %param.9) | copy-start | bytes 1540
  185.9 46.2 %copy-start.14 = (s32[128]{0:T(128)S(1)}, s32[128]{0:T(128)}, u32[]{:S(2)}) copy-start(s32[128]{0:T(128)} %param.11) | copy-start | bytes 1540
  185.9 46.2 %copy-start.15 = (s32[128]{0:T(128)S(1)}, s32[128]{0:T(128)}, u32[]{:S(2)}) copy-start(s32[128]{0:T(128)} %param.10) | copy-start | bytes 1540
  187.2 19.7 %collective-permute-start.19 = (f32[8,4096]{1,0:T(8,128)S(1)}, f32[8,4096]{1,0:T(8,128)S(1)}, u32[]{:S(2)}, u32[]{:S(2)}) collective-permute-start(f32[8,4096]{1,0:T(8,128)S(1)} %get-tuple-element.106), channel_id=1, source_target_pairs={{0,6},{1,7},{2,0},{3,1},{4,2},{5,3},{6,4},{7,5},{8,14},{9,15},{10,... | collective-permute-start | bytes 393224 | tf_op jit(solution)/shard_map/ppermute | solution.py:311
  190.3 26.7 %collective-permute-start.20 = (f32[8,4096]{1,0:T(8,128)S(1)}, f32[8,4096]{1,0:T(8,128)S(1)}, u32[]{:S(2)}, u32[]{:S(2)}) collective-permute-start(f32[8,4096]{1,0:T(8,128)S(1)} %get-tuple-element.105), channel_id=1, source_target_pairs={{0,4},{1,5},{2,6},{3,7},{4,0},{5,1},{6,2},{7,3},{8,12},{9,13},{10,... | collective-permute-start | bytes 393224 | tf_op jit(solution)/shard_map/ppermute | solution.py:311
  191.5 11.8 %collective-permute-start.35 = (f32[4,8,4096]{2,1,0:T(8,128)S(1)}, f32[4,8,4096]{2,1,0:T(8,128)S(1)}, u32[]{:S(2)}, u32[]{:S(2)}) collective-permute-start(f32[4,8,4096]{2,1,0:T(8,128)S(1)} %pad_maximum_fusion.6), channel_id=1, source_target_pairs={{0,8},{1,9},{2,10},{3,11},{4,12},{5,13},{6,14},{7,15},{8,16},{9,17... | collective-permute-start | bytes 1572872 | tf_op jit(solution)/shard_map/ppermute | solution.py:307
  192.7 11.5 %collective-permute-start.37 = (f32[4,8,4096]{2,1,0:T(8,128)S(1)}, f32[4,8,4096]{2,1,0:T(8,128)S(1)}, u32[]{:S(2)}, u32[]{:S(2)}) collective-permute-start(f32[4,8,4096]{2,1,0:T(8,128)S(1)} %pad_maximum_fusion.7), channel_id=1, source_target_pairs={{0,24},{1,25},{2,26},{3,27},{4,28},{5,29},{6,30},{7,31},{8,0},{9,1... | collective-permute-start | bytes 1572872 | tf_op jit(solution)/shard_map/ppermute | solution.py:307
  203.4 12.1 %collective-permute-start.28 = (f32[4,8,4096]{2,1,0:T(8,128)S(1)}, f32[4,8,4096]{2,1,0:T(8,128)S(1)}, u32[]{:S(2)}, u32[]{:S(2)}) collective-permute-start(f32[4,8,4096]{2,1,0:T(8,128)S(1)} %pad_maximum_fusion.4), channel_id=1, source_target_pairs={{0,2},{1,3},{2,4},{3,5},{4,6},{5,7},{6,0},{7,1},{8,10},{9,11},{10,... | collective-permute-start | bytes 1572872 | tf_op jit(solution)/shard_map/ppermute | solution.py:306
  204.2 11.9 %collective-permute-start.30 = (f32[4,8,4096]{2,1,0:T(8,128)S(1)}, f32[4,8,4096]{2,1,0:T(8,128)S(1)}, u32[]{:S(2)}, u32[]{:S(2)}) collective-permute-start(f32[4,8,4096]{2,1,0:T(8,128)S(1)} %pad_maximum_fusion.5), channel_id=1, source_target_pairs={{0,6},{1,7},{2,0},{3,1},{4,2},{5,3},{6,4},{7,5},{8,14},{9,15},{10,... | collective-permute-start | bytes 1572872 | tf_op jit(solution)/shard_map/ppermute | solution.py:306
  206.8 13.4 %collective-permute-start.11 = (f32[8,4096]{1,0:T(8,128)S(1)}, f32[8,4096]{1,0:T(8,128)S(1)}, u32[]{:S(2)}, u32[]{:S(2)}) collective-permute-start(f32[8,4096]{1,0:T(8,128)S(1)} %get-tuple-element.111), channel_id=1, source_target_pairs={{0,8},{1,9},{2,10},{3,11},{4,12},{5,13},{6,14},{7,15},{8,16},{9,17... | collective-permute-start | bytes 393224 | tf_op jit(solution)/shard_map/ppermute | solution.py:310
  206.8 14.9 %collective-permute-start.12 = (f32[8,4096]{1,0:T(8,128)S(1)}, f32[8,4096]{1,0:T(8,128)S(1)}, u32[]{:S(2)}, u32[]{:S(2)}) collective-permute-start(f32[8,4096]{1,0:T(8,128)S(1)} %get-tuple-element.110), channel_id=1, source_target_pairs={{0,24},{1,25},{2,26},{3,27},{4,28},{5,29},{6,30},{7,31},{8,0},{9,1... | collective-permute-start | bytes 393224 | tf_op jit(solution)/shard_map/ppermute | solution.py:310
  215.4 7.5 %collective-permute-start.13 = (f32[8,4096]{1,0:T(8,128)S(1)}, f32[8,4096]{1,0:T(8,128)S(1)}, u32[]{:S(2)}, u32[]{:S(2)}) collective-permute-start(f32[8,4096]{1,0:T(8,128)S(1)} %get-tuple-element.109), channel_id=1, source_target_pairs={{0,16},{1,17},{2,18},{3,19},{4,20},{5,21},{6,22},{7,23},{8,24},{9,... | collective-permute-start | bytes 393224 | tf_op jit(solution)/shard_map/ppermute | solution.py:310
  216.2 9.3 %collective-permute-start.38 = (f32[8,4096]{1,0:T(8,128)S(1)}, f32[8,4096]{1,0:T(8,128)S(1)}, u32[]{:S(2)}, u32[]{:S(2)}) collective-permute-start(f32[8,4096]{1,0:T(8,128)S(1)} %get-tuple-element.99), channel_id=1, source_target_pairs={{0,2},{1,3},{2,4},{3,5},{4,6},{5,7},{6,0},{7,1},{8,10},{9,11},{10,... | collective-permute-start | bytes 393224 | tf_op jit(solution)/shard_map/ppermute | solution.py:311
  217.0 11.3 %collective-permute-start.39 = (f32[8,4096]{1,0:T(8,128)S(1)}, f32[8,4096]{1,0:T(8,128)S(1)}, u32[]{:S(2)}, u32[]{:S(2)}) collective-permute-start(f32[8,4096]{1,0:T(8,128)S(1)} %get-tuple-element.98), channel_id=1, source_target_pairs={{0,6},{1,7},{2,0},{3,1},{4,2},{5,3},{6,4},{7,5},{8,14},{9,15},{10,... | collective-permute-start | bytes 393224 | tf_op jit(solution)/shard_map/ppermute | solution.py:311
  220.2 8.2 %collective-permute-start.40 = (f32[8,4096]{1,0:T(8,128)S(1)}, f32[8,4096]{1,0:T(8,128)S(1)}, u32[]{:S(2)}, u32[]{:S(2)}) collective-permute-start(f32[8,4096]{1,0:T(8,128)S(1)} %get-tuple-element.97), channel_id=1, source_target_pairs={{0,4},{1,5},{2,6},{3,7},{4,0},{5,1},{6,2},{7,3},{8,12},{9,13},{10,... | collective-permute-start | bytes 393224 | tf_op jit(solution)/shard_map/ppermute | solution.py:311
  221.7 6.6 %collective-permute-start.31 = (f32[8,4096]{1,0:T(8,128)S(1)}, f32[8,4096]{1,0:T(8,128)S(1)}, u32[]{:S(2)}, u32[]{:S(2)}) collective-permute-start(f32[8,4096]{1,0:T(8,128)S(1)} %get-tuple-element.103), channel_id=1, source_target_pairs={{0,8},{1,9},{2,10},{3,11},{4,12},{5,13},{6,14},{7,15},{8,16},{9,17... | collective-permute-start | bytes 393224 | tf_op jit(solution)/shard_map/ppermute | solution.py:310
  222.9 5.4 %collective-permute-start.32 = (f32[8,4096]{1,0:T(8,128)S(1)}, f32[8,4096]{1,0:T(8,128)S(1)}, u32[]{:S(2)}, u32[]{:S(2)}) collective-permute-start(f32[8,4096]{1,0:T(8,128)S(1)} %get-tuple-element.102), channel_id=1, source_target_pairs={{0,24},{1,25},{2,26},{3,27},{4,28},{5,29},{6,30},{7,31},{8,0},{9,1... | collective-permute-start | bytes 393224 | tf_op jit(solution)/shard_map/ppermute | solution.py:310
  225.5 6.5 %collective-permute-start.33 = (f32[8,4096]{1,0:T(8,128)S(1)}, f32[8,4096]{1,0:T(8,128)S(1)}, u32[]{:S(2)}, u32[]{:S(2)}) collective-permute-start(f32[8,4096]{1,0:T(8,128)S(1)} %get-tuple-element.101), channel_id=1, source_target_pairs={{0,16},{1,17},{2,18},{3,19},{4,20},{5,21},{6,22},{7,23},{8,24},{9,... | collective-permute-start | bytes 393224 | tf_op jit(solution)/shard_map/ppermute | solution.py:310
  232.4 0.8 copy-start.6
Sparse Core Ops, SparseCore 0:
  9.5 73.9 all-gather.2

commit v2 on v1

--- a/solution.py
+++ b/solution.py
@@ -66,7 +66,38 @@
         scratch_shapes=[pltpu.SemaphoreType.DMA((len(spans),))],
         compiler_params=pltpu.CompilerParams(vmem_limit_bytes=16 * 2**20),
         cost_estimate=pl.CostEstimate(flops=0, bytes_accessed=1000, transcendentals=0),
-    )(index, integrals)
+    )(index, in_hbm(integrals))
+
+
+def pack_late_kernel(total, index, me, tiles, out, sem):
+    steps, count = out.shape[:2]
+    for step in range(steps):
+        there = lax.rem(me[0] + step, steps)
+
+        def issue(k, _):
+            pltpu.make_async_copy(tiles.at[index[step * total + total - count + k]], out.at[there, k], sem.at[step]).start()
+            return 0
+
+        lax.fori_loop(0, count, issue, 0)
+    for step in range(steps):
+        pltpu.make_async_copy(tiles.at[pl.ds(0, count)], out.at[step], sem.at[step]).wait()
+
+
+def pack_late(integrals, index, me, total, steps, count):
+    smem = pl.BlockSpec(memory_space=pltpu.SMEM)
+    return pl.pallas_call(
+        functools.partial(pack_late_kernel, total),
+        out_shape=jax.ShapeDtypeStruct((steps, count, TILE, TILE), jnp.float32),
+        in_specs=[smem, smem, pl.BlockSpec(memory_space=pl.ANY)],
+        out_specs=pl.BlockSpec(memory_space=pltpu.VMEM),
+        scratch_shapes=[pltpu.SemaphoreType.DMA((steps,))],
+        compiler_params=pltpu.CompilerParams(vmem_limit_bytes=8 * 2**20),
+        cost_estimate=pl.CostEstimate(flops=0, bytes_accessed=1000, transcendentals=0),
+    )(index, me, in_hbm(integrals))
+
+
+def in_hbm(value):
+    return pltpu.with_memory_space_constraint(value, pltpu.HBM)
 
 
 def add_kernel(one, two, out):
@@ -131,7 +162,7 @@
         scratch_shapes=[pltpu.SemaphoreType.DMA],
         compiler_params=pltpu.CompilerParams(vmem_limit_bytes=2**20),
         cost_estimate=pl.CostEstimate(flops=0, bytes_accessed=1000, transcendentals=0),
-    )(where, amp)
+    )(where, in_hbm(amp))
 
 
 def multiply(code, counts, tiles, tile_v, tile_sem, amp_v, acc_v, low, blocks):
@@ -232,7 +263,7 @@
         given, into = [keep(amp), keep(held)], [vmem] * 2
         shapes, specs = [*parts, pltpu.HBM((4, 4, 8, blocks * TILE - width), jnp.float32), token], [any_spec] * 11 + [vmem]
     else:
-        given, into, shapes, specs = [amp, *held], [any_spec, smem, any_spec], parts, [any_spec] * 10
+        given, into, shapes, specs = [in_hbm(amp), *held], [any_spec, smem, any_spec], parts, [any_spec] * 10
     scratch = [pltpu.VMEM((n, TILE, TILE), jnp.float32) for n in counts]
     scratch += [pltpu.SemaphoreType.DMA((len(tiles),)), pltpu.SemaphoreType.DMA((11,))]
     limit = 2**21 + sum(counts) * TILE * TILE * 4
@@ -309,13 +340,13 @@
         s2 = [parts[9][q] + got_zu[q] + got_zd[q] for q in range(4)]
         f1 = [lax.ppermute(s1[s], "inner", along_z[s]) for s in (1, 3, 2)]
         f2 = [lax.ppermute(s2[s], "inner", along_x[s]) for s in (1, 3, 2)]
-        return [s1[0], *f1, s2[0], *f2]
+        return [s1[0], *f1, s2[0], *f2], (x_up, x_down, z_up, z_down)
 
     p1, p3 = pack(integrals, index, ((1, 0, FIRST), (3, 0, FIRST)), total)
     r1, r3 = lax.ppermute(p1, "grp", along_y[1]), lax.ppermute(p3, "grp", along_y[3])
-    p2, p4, p5, p6, p0 = pack(integrals, index, ((2, 0, FIRST), (1, FIRST, total), (2, FIRST, total), (3, FIRST, total), (0, 0, total)), total)
+    p2, p0 = pack(integrals, index, ((2, 0, FIRST), (0, 0, FIRST)), total)
     r2 = lax.ppermute(p2, "grp", along_y[2])
-    late = [lax.ppermute(p, "grp", along_y[s]) for p, s in ((p4, 1), (p6, 3), (p5, 2))]
+    late = pack_late(integrals, index, grp.reshape(1).astype(jnp.int32), total, n_grp, total - FIRST)
     codes, _ = lax.optimization_barrier((codes, p2))
     note = jnp.concatenate(
         [
@@ -328,9 +359,10 @@
     overflow = jnp.sum(note[:, total]) > 0.5
     note = note[:, :total].reshape(n_grp, n_inner // 2, 2, total)
     note = lax.dynamic_index_in_dim(note, inner // 2, axis=1, keepdims=False)
-    note = jnp.stack([lax.dynamic_index_in_dim(note, (grp - s + n_grp) % n_grp, axis=0, keepdims=False) for s in range(4)])
     note = jnp.stack([lax.dynamic_index_in_dim(note, core, axis=1, keepdims=False), lax.dynamic_index_in_dim(note, 1 - core, axis=1, keepdims=False)])
     note = note.astype(jnp.int32)
+    late_codes = note[:, :, FIRST:].reshape(-1)
+    note = jnp.stack([lax.dynamic_index_in_dim(note, (grp - s + n_grp) % n_grp, axis=1, keepdims=False) for s in range(4)], axis=1)
 
     def codes_of(*pieces):
         return jnp.concatenate([note[side, s, lo:hi] for side in range(2) for s, lo, hi in pieces])
@@ -338,13 +370,14 @@
     def with_other(tiles):
         return [*tiles, *[lax.ppermute(t, "inner", across) for t in tiles]]
 
+    late_sent = late
+    late = lax.all_to_all(late, "grp", split_axis=0, concat_axis=0, tiled=True).reshape(-1, TILE, TILE)
     held = arrange(where, amp)
-    acc, token = ladder(0, codes_of((0, 0, total), (1, 0, FIRST), (3, 0, FIRST)), held, None, with_other([p0, gate(r1, note), gate(r3, note)]), blocks, GUESS[0])
+    acc, token = ladder(0, codes_of((0, 0, FIRST), (1, 0, FIRST), (3, 0, FIRST)), held, None, with_other([p0, gate(r1, note, late_sent), gate(r3, note)]), blocks, GUESS[0])
     *parts, acc, token = ladder(1, codes_of((2, 0, FIRST)), held, acc, with_other([gate(r2, token)]), blocks, GUESS[1])
-    pieces = finish(parts)
-    late = with_other([gate(r, token) for r in late])
-    parts = ladder(2, codes_of((1, FIRST, total), (3, FIRST, total), (2, FIRST, total)), amp, (where, acc), late, blocks, GUESS[2])
-    pieces += finish(parts)
+    pieces, under_way = finish(parts)
+    parts = ladder(2, late_codes, amp, (where, acc), with_other([gate(late, token, *under_way)]), blocks, GUESS[2])
+    pieces += finish(parts)[0]
     out = small(total_kernel, (rows, width), *pieces)
 
     def with_rest(out):

time: 242 us -> 274 us (1.13); the launches traced: 240 us -> 269 us
  waiting for transfers between devices: 86.5 us -> 108 us
  other arithmetic: 12.9 us -> 18.1 us
  Pallas kernels: 56 us -> 59.3 us
    all_to_all x0 -> x1, waiting for transfers between devices: none -> 16.7 us  [per_device(): lax.all_to_all(late, 'grp', split_axis=0, concat_axis=0, tiled=True)]
    ppermute x3 -> x0, waiting for transfers between devices: 16.3 us -> none  [per_device(): lax.ppermute(p, 'grp', along_y[s])]
    ppermute x4, waiting for transfers between devices: 8.46 us -> 21.6 us  [finish(): lax.ppermute(z_up, 'inner', along_z[1])]
    pallas_call x2, Pallas kernels: 16.1 us -> 9.41 us  [pack(): pl.pallas_call(functools.partial(pack_kernel, spans, total), out_shape=[j...]
    all_to_all x1, waiting for transfers between devices: 23.3 us -> 28.1 us  [per_device(): lax.all_to_all(note.reshape(devices, total + 1), AXES, split_axis=0, conc...]
    ppermute x4, waiting for transfers between devices: 6.27 us -> 2.18 us  [finish(): lax.ppermute(z_down, 'inner', along_z[3])]
    pallas_call x0 -> x1, Pallas kernels: none -> 3.77 us  [pack_late(): pl.pallas_call(functools.partial(pack_late_kernel, total), out_shape=jax....]
    ppermute x7 -> x5, waiting for transfers between devices: 0.41 us -> 4.12 us  [with_other(): return [*tiles, *[lax.ppermute(t, 'inner', across) for t in tiles]]]
  transfers between devices with their start and end apart: 43 -> 39, of which waited for: 13 -> 17; matrix products, arithmetic and copies ran while one was open for 6% -> 7% of each run, Pallas kernels for 23% -> 18%
where the time goes in v2:
time: 274 us; the launch traced here: 269 us
  waiting for transfers between devices  108 us (39%)
  starting transfers between devices  61 us (22%)
  Pallas kernels  59.3 us (22%)
  other arithmetic  18.1 us (7%)
  between operations  14.7 us (5%)
  local copies, waits for them, and re-layouts  8.07 us (3%)
    pallas_call x3, Pallas kernels, ladder(): pl.pallas_call(functools.partial(ladder_kernel, step, counts, LOW), out_s...  42.1 us
    all_to_all x1, waiting for transfers between devices, per_device(): lax.all_to_all(note.reshape(devices, total + 1), AXES, split_axis=0, conc...  28.1 us
    ppermute x4, waiting for transfers between devices, finish(): lax.ppermute(z_up, 'inner', along_z[1])  21.6 us
    all_to_all x1, waiting for transfers between devices, per_device(): lax.all_to_all(late, 'grp', split_axis=0, concat_axis=0, tiled=True)  16.7 us
    all_gather x1, waiting for transfers between devices, per_device(): lax.all_gather(amplitude, 'inner', axis=0, axis_index_groups=same_core)  13.6 us
    all_to_all x1, starting transfers between devices, per_device(): lax.all_to_all(note.reshape(devices, total + 1), AXES, split_axis=0, conc...  11.4 us
    ppermute x4, starting transfers between devices, finish(): lax.ppermute(z_down, 'inner', along_z[3])  10.4 us
    pallas_call x2, Pallas kernels, pack(): pl.pallas_call(functools.partial(pack_kernel, spans, total), out_shape=[j...  9.41 us
  transfers between devices with their start and end apart: 39, of which 17 were waited for; matrix products, arithmetic and copies ran while one was open for 7% of the time, Pallas kernels for 18%

profile of v2, /device:TPU:0, one launch (start us, length us, event | category | flops | bytes accessed | tf_op | source)
XLA Modules:
  0.0 268.9 jit_solution(1291516560769621172)
XLA Ops:
  8.8 1.4 fusion.33
  10.3 4.7 %shard_map.59 = (f32[30,128,128]{2,1,0:T(8,128)}, f32[30,128,128]{2,1,0:T(8,128)}) custom-call(s32[160]{0:T(256)S(1)} %select_reduce_fusion.index, f32[128,128,128]{2,1,0:T(8,128)} %tiles.5), custom_call_target="tpu_custom_call" | custom-call | bytes 1000 | tf_op jit(solution)/shard_map/pallas_call | solution.py:61
  15.0 3.2 %collective-permute-start.1 = (f32[30,128,128]{2,1,0:T(8,128)}, f32[30,128,128]{2,1,0:T(8,128)}, u32[]{:S(2)}, u32[]{:S(2)}) collective-permute-start(f32[30,128,128]{2,1,0:T(8,128)} %get-tuple-element.63), channel_id=1, source_target_pairs={{0,96},{32,0},{64,32},{96,64},{1,97},{33,1},{65,33},{97,65},{2,98}... | collective-permute-start | bytes 5898248 | tf_op jit(solution)/shard_map/ppermute | solution.py:346
  18.2 4.7 %shard_map.57 = (f32[30,128,128]{2,1,0:T(8,128)}, f32[30,128,128]{2,1,0:T(8,128)}) custom-call(s32[160]{0:T(256)S(1)} %select_reduce_fusion.index, f32[128,128,128]{2,1,0:T(8,128)} %tiles.5), custom_call_target="tpu_custom_call" | custom-call | bytes 1000 | tf_op jit(solution)/shard_map/pallas_call | solution.py:61
  23.1 1.3 pad_convert_fusion
  24.4 11.4 %all-to-all-start.3 = ((f32[128,1,41]{2,1,0:T(1,128)}), f32[128,1,41]{2,1,0:T(1,128)S(1)}, u32[]{:S(2)}, u32[]{:S(2)}) async-start(f32[128,1,41]{2,1,0:T(1,128)} %bitcast.13), calls=%async_computation.4 | async-start | bytes 131072 | tf_op jit(solution)/shard_map/all_to_all | solution.py:358
  36.0 3.8 %shard_map.60.refs_2_ = f32[4,10,128,128]{3,2,1,0:T(8,128)S(1)} custom-call(s32[160]{0:T(256)S(1)} %select_reduce_fusion.index, s32[1]{0:T(128)} %bitcast.29.me, f32[128,128,128]{2,1,0:T(8,128)} %tiles.5), custom_call_target="tpu_custom_call" | custom-call | bytes 1000 | tf_op jit(solution)/shard_map/pallas_call | solution.py:88
  39.8 28.1 %all-to-all-done.3 = f32[128,1,41]{2,1,0:T(1,128)S(1)} async-done(((f32[128,1,41]{2,1,0:T(1,128)}), f32[128,1,41]{2,1,0:T(1,128)S(1)}, u32[]{:S(2)}, u32[]{:S(2)}) %all-to-all-start.3) | async-done | bytes 21024 | tf_op jit(solution)/shard_map/all_to_all | solution.py:358
  69.4 13.6 %all-gather.3.cloned.1.call-done = f32[128,16384]{1,0:T(8,128)} async-done(((f32[8,16384]{1,0:T(8,128)}), f32[128,16384]{1,0:T(8,128)}) %all-gather.3.cloned.1.call-update) | async-done | bytes 8388624 | tf_op jit(solution)/shard_map/all_gather | solution.py:305
  83.1 3.9 %shard_map.58.refs_1_ = f32[16,8,16384]{2,1,0:T(8,128)S(1)} custom-call(s32[2]{0:T(128)S(1)} %pad_add_fusion.2.where.refs_2_, f32[16,8,16384]{2,1,0:T(8,128)} %bitcast.106), custom_call_target="tpu_custom_call" | custom-call | bytes 1000 | tf_op jit(solution)/shard_map/pallas_call | solution.py:157
  87.1 22.0 %shard_map.63 = (f32[4,4,8,16384]{3,2,1,0:T(8,128)S(1)}, f32[8,128]{1,0:T(8,128)S(1)}) custom-call(s32[180]{0:T(256)S(1)} %concatenate.35.refs_0_, f32[16,8,16384]{2,1,0:T(8,128)S(1)} %shard_map.58.refs_1_, f32[30,128,128]{2,1,0:T(8,128)} %get-tuple-element.61.refs_2_, f32[30,128,128]{2,1,0:T(8,128)} %shard_map.61.refs_3_, ...), custom_call_target="tpu_custom_call" | custom-call | bytes 80000000 | tf_op jit(solution)/shard_map/pallas_call | solution.py:273
  109.1 6.3 %collective-permute-done.5.refs_0_ = f32[30,128,128]{2,1,0:T(8,128)} collective-permute-done((f32[30,128,128]{2,1,0:T(8,128)}, f32[30,128,128]{2,1,0:T(8,128)}, u32[]{:S(2)}, u32[]{:S(2)}) %collective-permute-start.5) | collective-permute-done | bytes 1966112 | tf_op jit(solution)/shard_map/ppermute | solution.py:348
  115.4 4.1 %collective-permute-done.6.refs_4_ = f32[30,128,128]{2,1,0:T(8,128)S(1)} collective-permute-done((f32[30,128,128]{2,1,0:T(8,128)}, f32[30,128,128]{2,1,0:T(8,128)S(1)}, u32[]{:S(2)}, u32[]{:S(2)}) %collective-permute-start.6) | collective-permute-done | bytes 1966112 | tf_op jit(solution)/shard_map/ppermute | solution.py:371
  119.5 12.1 %shard_map.65 = (f32[2,8,4096]{2,1,0:T(8,128)}, f32[2,8,4096]{2,1,0:T(8,128)}, f32[2,8,4096]{2,1,0:T(8,128)}, f32[2,8,4096]{2,1,0:T(8,128)}, f32[4,8,4096]{2,1,0...) custom-call(s32[60]{0:T(128)S(1)} %pad_add_fusion.1.refs_0_, ...), custom_call_target="tpu_custom_call" | custom-call | bytes 35000000 | tf_op jit(solution)/shard_map/pallas_call | solution.py:273
  131.6 1.1 collective-permute-start.14
  132.6 3.7 %all-to-all-start.4 = ((f32[4,10,128,128]{3,2,1,0:T(8,128)}), f32[4,10,128,128]{3,2,1,0:T(8,128)S(1)}, u32[]{:S(2)}, u32[]{:S(2)}) async-start(f32[4,10,128,128]{3,2,1,0:T(8,128)} %copy-done), calls=%async_computation.5 | async-start | bytes 5242880 | tf_op jit(solution)/shard_map/all_to_all | solution.py:374
  136.3 2.3 collective-permute-start.16
  138.6 1.7 collective-permute-start.7
  140.3 1.5 collective-permute-start.9
  141.9 1.1 slice_add_fusion.5
  142.9 1.7 collective-permute-done.16
  144.7 1.1 fusion.47
  145.8 0.9 pad_maximum_fusion.2.refs_4_
  146.6 1.2 collective-permute-done.7
  147.9 1.1 slice_add_fusion.7
  148.9 0.9 pad_maximum_fusion.3.refs_5_
  149.8 1.1 fusion.48
  150.9 0.8 pad_maximum_fusion.1.refs_3_
  151.8 16.7 %all-to-all-done.4 = f32[4,10,128,128]{3,2,1,0:T(8,128)S(1)} async-done(((f32[4,10,128,128]{3,2,1,0:T(8,128)}), f32[4,10,128,128]{3,2,1,0:T(8,128)S(1)}, u32[]{:S(2)}, u32[]{:S(2)}) %all-to-all-start.4) | async-done | bytes 2621472 | tf_op jit(solution)/shard_map/all_to_all | solution.py:374
  168.5 1.0 copy-done.2
  169.6 1.0 copy-done.3
  170.6 1.0 copy-done.4
  172.3 2.6 collective-permute-start.17
  175.0 1.7 collective-permute-start.8
  176.7 1.5 collective-permute-start.10
  178.3 9.2 %collective-permute-done.15 = f32[4,8,4096]{2,1,0:T(8,128)} collective-permute-done((f32[4,8,4096]{2,1,0:T(8,128)}, f32[4,8,4096]{2,1,0:T(8,128)}, u32[]{:S(2)}, u32[]{:S(2)}) %collective-permute-start.15) | collective-permute-done | bytes 524320 | tf_op jit(solution)/shard_map/ppermute | solution.py:338
  187.5 1.5 fusion.19
  189.0 1.8 collective-permute-start.18
  190.8 1.5 collective-permute-start.19
  192.3 1.8 collective-permute-start.20
  194.2 2.2 copy-done.1
  196.3 8.0 %shard_map.67 = (f32[2,8,4096]{2,1,0:T(8,128)}, f32[2,8,4096]{2,1,0:T(8,128)}, f32[2,8,4096]{2,1,0:T(8,128)}, f32[2,8,4096]{2,1,0:T(8,128)}, f32[4,8,4096]{2,1,0...) custom-call(s32[80]{0:T(128)S(1)} %reshape.126.refs_0_, ...), custom_call_target="tpu_custom_call" | custom-call | bytes 20000000 | tf_op jit(solution)/shard_map/pallas_call | solution.py:273
  204.4 1.1 collective-permute-start.29
  205.7 2.2 collective-permute-start.31
  207.9 5.1 %collective-permute-done.29 = f32[2,8,4096]{2,1,0:T(8,128)S(1)} collective-permute-done((f32[2,8,4096]{2,1,0:T(8,128)}, f32[2,8,4096]{2,1,0:T(8,128)S(1)}, u32[]{:S(2)}, u32[]{:S(2)}) %collective-permute-start.29) | collective-permute-done | bytes 262176 | tf_op jit(solution)/shard_map/ppermute | solution.py:328
  213.0 1.0 collective-permute-start.22
  214.0 1.1 slice_add_fusion.1
  215.1 2.3 collective-permute-start.24
  217.4 1.1 fusion.45
  218.5 2.3 collective-permute-done.22
  220.8 1.1 slice_add_fusion.3
  222.0 3.3 %collective-permute-start.32 = (f32[4,8,4096]{2,1,0:T(8,128)S(1)}, f32[4,8,4096]{2,1,0:T(8,128)S(1)}, u32[]{:S(2)}, u32[]{:S(2)}) collective-permute-start(f32[4,8,4096]{2,1,0:T(8,128)S(1)} %pad_maximum_fusion.7), channel_id=1, source_target_pairs={{0,24},{1,25},{2,26},{3,27},{4,28},{5,29},{6,30},{7,31},{8,0},{9,1... | collective-permute-start | bytes 1572872 | tf_op jit(solution)/shard_map/ppermute | solution.py:338
  225.4 7.3 %collective-permute-done.30 = f32[4,8,4096]{2,1,0:T(8,128)S(1)} collective-permute-done((f32[4,8,4096]{2,1,0:T(8,128)S(1)}, f32[4,8,4096]{2,1,0:T(8,128)S(1)}, u32[]{:S(2)}, u32[]{:S(2)}) %collective-permute-start.30) | collective-permute-done | bytes 524320 | tf_op jit(solution)/shard_map/ppermute | solution.py:338
  233.1 3.6 %collective-permute-start.25 = (f32[4,8,4096]{2,1,0:T(8,128)S(1)}, f32[4,8,4096]{2,1,0:T(8,128)S(1)}, u32[]{:S(2)}, u32[]{:S(2)}) collective-permute-start(f32[4,8,4096]{2,1,0:T(8,128)S(1)} %pad_maximum_fusion.5), channel_id=1, source_target_pairs={{0,6},{1,7},{2,0},{3,1},{4,2},{5,3},{6,4},{7,5},{8,14},{9,15},{10,... | collective-permute-start | bytes 1572872 | tf_op jit(solution)/shard_map/ppermute | solution.py:337
  236.9 3.2 %collective-permute-start.12 = (f32[8,4096]{1,0:T(8,128)S(1)}, f32[8,4096]{1,0:T(8,128)S(1)}, u32[]{:S(2)}, u32[]{:S(2)}) collective-permute-start(f32[8,4096]{1,0:T(8,128)S(1)} %get-tuple-element.104), channel_id=1, source_target_pairs={{0,24},{1,25},{2,26},{3,27},{4,28},{5,29},{6,30},{7,31},{8,0},{9,1... | collective-permute-start | bytes 393224 | tf_op jit(solution)/shard_map/ppermute | solution.py:341
  240.1 4.7 %collective-permute-done.23 = f32[4,8,4096]{2,1,0:T(8,128)S(1)} collective-permute-done((f32[4,8,4096]{2,1,0:T(8,128)S(1)}, f32[4,8,4096]{2,1,0:T(8,128)S(1)}, u32[]{:S(2)}, u32[]{:S(2)}) %collective-permute-start.23) | collective-permute-done | bytes 524320 | tf_op jit(solution)/shard_map/ppermute | solution.py:337
  246.2 3.2 %collective-permute-start.34 = (f32[8,4096]{1,0:T(8,128)S(1)}, f32[8,4096]{1,0:T(8,128)S(1)}, u32[]{:S(2)}, u32[]{:S(2)}) collective-permute-start(f32[8,4096]{1,0:T(8,128)S(1)} %get-tuple-element.92), channel_id=1, source_target_pairs={{0,6},{1,7},{2,0},{3,1},{4,2},{5,3},{6,4},{7,5},{8,14},{9,15},{10,... | collective-permute-start | bytes 393224 | tf_op jit(solution)/shard_map/ppermute | solution.py:342
  249.4 0.8 collective-permute-start.35
  250.2 2.4 collective-permute-done.13.refs_3_
  252.6 0.9 collective-permute-start.27
  253.5 1.5 collective-permute-start.28
  256.6 0.9 collective-permute-done.27.refs_10_
  257.6 2.4 collective-permute-done.28.refs_11_
  260.0 0.9 copy-done.7
  (104 shorter events, 9.4 us)
Async XLA Ops:
  6.5 76.5 %all-gather.3.cloned.1.call-start = ((), (), s32[]{:S(2)}) async-start(), calls=%async_computation.7 | async-start | bytes 8912896 | tf_op jit(solution)/shard_map/all_gather | solution.py:305
  15.0 53.1 %collective-permute-start.1 = (f32[30,128,128]{2,1,0:T(8,128)}, f32[30,128,128]{2,1,0:T(8,128)}, u32[]{:S(2)}, u32[]{:S(2)}) collective-permute-start(f32[30,128,128]{2,1,0:T(8,128)} %get-tuple-element.63), channel_id=1, source_target_pairs={{0,96},{32,0},{64,32},{96,64},{1,97},{33,1},{65,33},{97,65},{2,98}... | collective-permute-start | bytes 5898248 | tf_op jit(solution)/shard_map/ppermute | solution.py:346
  18.2 50.0 %collective-permute-start = (f32[30,128,128]{2,1,0:T(8,128)}, f32[30,128,128]{2,1,0:T(8,128)}, u32[]{:S(2)}, u32[]{:S(2)}) collective-permute-start(f32[30,128,128]{2,1,0:T(8,128)} %get-tuple-element.62), channel_id=1, source_target_pairs={{0,32},{32,64},{64,96},{96,0},{1,33},{33,65},{65,97},{97,1},{2,34}... | collective-permute-start | bytes 5898248 | tf_op jit(solution)/shard_map/ppermute | solution.py:346
  24.4 43.5 %all-to-all-start.3 = ((f32[128,1,41]{2,1,0:T(1,128)}), f32[128,1,41]{2,1,0:T(1,128)S(1)}, u32[]{:S(2)}, u32[]{:S(2)}) async-start(f32[128,1,41]{2,1,0:T(1,128)} %bitcast.13), calls=%async_computation.4 | async-start | bytes 131072 | tf_op jit(solution)/shard_map/all_to_all | solution.py:358
  35.8 51.2 %collective-permute-start.2 = (f32[30,128,128]{2,1,0:T(8,128)}, f32[30,128,128]{2,1,0:T(8,128)}, u32[]{:S(2)}, u32[]{:S(2)}) collective-permute-start(f32[30,128,128]{2,1,0:T(8,128)} %get-tuple-element.61.refs_2_), channel_id=1, source_target_pairs={{0,1},{1,0},{2,3},{3,2},{4,5},{5,4},{6,7},{7,6},{8,9},{9,8},{10,11... | collective-permute-start | bytes 5898248 | tf_op jit(solution)/shard_map/ppermute | solution.py:371
  39.8 47.2 %copy-start = (f32[4,10,128,128]{3,2,1,0:T(8,128)}, f32[4,10,128,128]{3,2,1,0:T(8,128)S(1)}, u32[]{:S(2)}) copy-start(f32[4,10,128,128]{3,2,1,0:T(8,128)S(1)} %shard_map.60.refs_2_) | copy-start | bytes 7864324
  68.0 19.0 %copy-start.13 = (f32[128,1,41]{2,1,0:T(1,128)}, f32[128,1,41]{2,1,0:T(1,128)S(1)}, u32[]{:S(2)}) copy-start(f32[128,1,41]{2,1,0:T(1,128)S(1)} %all-to-all-done.3) | copy-start | bytes 62980
  68.1 19.0 %collective-permute-start.4 = (f32[30,128,128]{2,1,0:T(8,128)}, f32[30,128,128]{2,1,0:T(8,128)}, u32[]{:S(2)}, u32[]{:S(2)}) collective-permute-start(f32[30,128,128]{2,1,0:T(8,128)} %shard_map.62.refs_4_), channel_id=1, source_target_pairs={{0,1},{1,0},{2,3},{3,2},{4,5},{5,4},{6,7},{7,6},{8,9},{9,8},{10,11... | collective-permute-start | bytes 5898248 | tf_op jit(solution)/shard_map/ppermute | solution.py:371
  68.2 18.9 %collective-permute-start.3 = (f32[30,128,128]{2,1,0:T(8,128)}, f32[30,128,128]{2,1,0:T(8,128)}, u32[]{:S(2)}, u32[]{:S(2)}) collective-permute-start(f32[30,128,128]{2,1,0:T(8,128)} %shard_map.61.refs_3_), channel_id=1, source_target_pairs={{0,1},{1,0},{2,3},{3,2},{4,5},{5,4},{6,7},{7,6},{8,9},{9,8},{10,11... | collective-permute-start | bytes 5898248 | tf_op jit(solution)/shard_map/ppermute | solution.py:371
  68.7 46.7 %collective-permute-start.5 = (f32[30,128,128]{2,1,0:T(8,128)}, f32[30,128,128]{2,1,0:T(8,128)}, u32[]{:S(2)}, u32[]{:S(2)}) collective-permute-start(f32[30,128,128]{2,1,0:T(8,128)} %get-tuple-element.59), channel_id=1, source_target_pairs={{0,64},{32,96},{64,0},{96,32},{1,65},{33,97},{65,1},{97,33},{2,66}... | collective-permute-start | bytes 5898248 | tf_op jit(solution)/shard_map/ppermute | solution.py:348
  115.3 4.2 %collective-permute-start.6 = (f32[30,128,128]{2,1,0:T(8,128)}, f32[30,128,128]{2,1,0:T(8,128)S(1)}, u32[]{:S(2)}, u32[]{:S(2)}) collective-permute-start(f32[30,128,128]{2,1,0:T(8,128)} %shard_map.64.refs_3_), channel_id=1, source_target_pairs={{0,1},{1,0},{2,3},{3,2},{4,5},{5,4},{6,7},{7,6},{8,9},{9,8},{10,11... | collective-permute-start | bytes 5898248 | tf_op jit(solution)/shard_map/ppermute | solution.py:371
  131.6 10.3 %collective-permute-start.14 = (f32[2,8,4096]{2,1,0:T(8,128)}, f32[2,8,4096]{2,1,0:T(8,128)S(1)}, u32[]{:S(2)}, u32[]{:S(2)}) collective-permute-start(f32[2,8,4096]{2,1,0:T(8,128)} %get-tuple-element.73), channel_id=1, source_target_pairs={{0,8},{1,9},{2,10},{3,11},{4,12},{5,13},{6,14},{7,15},{8,16},{9,17... | collective-permute-start | bytes 786440 | tf_op jit(solution)/shard_map/ppermute | solution.py:328
  132.6 35.9 %all-to-all-start.4 = ((f32[4,10,128,128]{3,2,1,0:T(8,128)}), f32[4,10,128,128]{3,2,1,0:T(8,128)S(1)}, u32[]{:S(2)}, u32[]{:S(2)}) async-start(f32[4,10,128,128]{3,2,1,0:T(8,128)} %copy-done), calls=%async_computation.5 | async-start | bytes 5242880 | tf_op jit(solution)/shard_map/all_to_all | solution.py:374
  136.3 8.4 %collective-permute-start.16 = (f32[2,8,4096]{2,1,0:T(8,128)}, f32[2,8,4096]{2,1,0:T(8,128)S(1)}, u32[]{:S(2)}, u32[]{:S(2)}) collective-permute-start(f32[2,8,4096]{2,1,0:T(8,128)} %get-tuple-element.75), channel_id=1, source_target_pairs={{0,24},{1,25},{2,26},{3,27},{4,28},{5,29},{6,30},{7,31},{8,0},{9,1... | collective-permute-start | bytes 786440 | tf_op jit(solution)/shard_map/ppermute | solution.py:328
  138.6 9.2 %collective-permute-start.7 = (f32[2,8,4096]{2,1,0:T(8,128)}, f32[2,8,4096]{2,1,0:T(8,128)S(1)}, u32[]{:S(2)}, u32[]{:S(2)}) collective-permute-start(f32[2,8,4096]{2,1,0:T(8,128)} %get-tuple-element.68), channel_id=1, source_target_pairs={{0,2},{1,3},{2,4},{3,5},{4,6},{5,7},{6,0},{7,1},{8,10},{9,11},{10,... | collective-permute-start | bytes 786440 | tf_op jit(solution)/shard_map/ppermute | solution.py:327
  140.3 9.5 %collective-permute-start.9 = (f32[2,8,4096]{2,1,0:T(8,128)}, f32[2,8,4096]{2,1,0:T(8,128)S(1)}, u32[]{:S(2)}, u32[]{:S(2)}) collective-permute-start(f32[2,8,4096]{2,1,0:T(8,128)} %get-tuple-element.70), channel_id=1, source_target_pairs={{0,6},{1,7},{2,0},{3,1},{4,2},{5,3},{6,4},{7,5},{8,14},{9,15},{10,... | collective-permute-start | bytes 786440 | tf_op jit(solution)/shard_map/ppermute | solution.py:327
  168.5 1.0 copy-start.2
  169.6 1.0 copy-start.3
  170.6 1.0 copy-start.4
  171.6 20.7 %collective-permute-start.21 = (f32[40,128,128]{2,1,0:T(8,128)S(1)}, f32[40,128,128]{2,1,0:T(8,128)}, u32[]{:S(2)}, u32[]{:S(2)}) collective-permute-start(f32[40,128,128]{2,1,0:T(8,128)S(1)} %shard_map.66.refs_4_), channel_id=1, source_target_pairs={{0,1},{1,0},{2,3},{3,2},{4,5},{5,4},{6,7},{7,6},{8,9},{9,8},{10,11... | collective-permute-start | bytes 7864328 | tf_op jit(solution)/shard_map/ppermute | solution.py:371
  171.7 15.9 %collective-permute-start.15 = (f32[4,8,4096]{2,1,0:T(8,128)}, f32[4,8,4096]{2,1,0:T(8,128)}, u32[]{:S(2)}, u32[]{:S(2)}) collective-permute-start(f32[4,8,4096]{2,1,0:T(8,128)} %pad_maximum_fusion.2.refs_4_), channel_id=1, source_target_pairs={{0,8},{1,9},{2,10},{3,11},{4,12},{5,13},{6,14},{7,15},{8,16},{9,17... | collective-permute-start | bytes 1572872 | tf_op jit(solution)/shard_map/ppermute | solution.py:338
  172.3 15.2 %collective-permute-start.17 = (f32[4,8,4096]{2,1,0:T(8,128)}, f32[4,8,4096]{2,1,0:T(8,128)}, u32[]{:S(2)}, u32[]{:S(2)}) collective-permute-start(f32[4,8,4096]{2,1,0:T(8,128)} %pad_maximum_fusion.3.refs_5_), channel_id=1, source_target_pairs={{0,24},{1,25},{2,26},{3,27},{4,28},{5,29},{6,30},{7,31},{8,0},{9,1... | collective-permute-start | bytes 1572872 | tf_op jit(solution)/shard_map/ppermute | solution.py:338
  175.0 29.4 %collective-permute-start.8 = (f32[4,8,4096]{2,1,0:T(8,128)S(1)}, f32[4,8,4096]{2,1,0:T(8,128)S(1)}, u32[]{:S(2)}, u32[]{:S(2)}) collective-permute-start(f32[4,8,4096]{2,1,0:T(8,128)S(1)} %pad_maximum_fusion.refs_2_), channel_id=1, source_target_pairs={{0,2},{1,3},{2,4},{3,5},{4,6},{5,7},{6,0},{7,1},{8,10},{9,11},{10,... | collective-permute-start | bytes 1572872 | tf_op jit(solution)/shard_map/ppermute | solution.py:337
  176.7 28.8 %collective-permute-start.10 = (f32[4,8,4096]{2,1,0:T(8,128)}, f32[4,8,4096]{2,1,0:T(8,128)S(1)}, u32[]{:S(2)}, u32[]{:S(2)}) collective-permute-start(f32[4,8,4096]{2,1,0:T(8,128)} %pad_maximum_fusion.1.refs_3_), channel_id=1, source_target_pairs={{0,6},{1,7},{2,0},{3,1},{4,2},{5,3},{6,4},{7,5},{8,14},{9,15},{10,... | collective-permute-start | bytes 1572872 | tf_op jit(solution)/shard_map/ppermute | solution.py:337
  189.0 47.7 %collective-permute-start.18 = (f32[8,4096]{1,0:T(8,128)S(1)}, f32[8,4096]{1,0:T(8,128)S(1)}, u32[]{:S(2)}, u32[]{:S(2)}) collective-permute-start(f32[8,4096]{1,0:T(8,128)S(1)} %get-tuple-element.101), channel_id=1, source_target_pairs={{0,2},{1,3},{2,4},{3,5},{4,6},{5,7},{6,0},{7,1},{8,10},{9,11},{10,... | collective-permute-start | bytes 393224 | tf_op jit(solution)/shard_map/ppermute | solution.py:342
  190.8 46.1 %collective-permute-start.19 = (f32[8,4096]{1,0:T(8,128)S(1)}, f32[8,4096]{1,0:T(8,128)S(1)}, u32[]{:S(2)}, u32[]{:S(2)}) collective-permute-start(f32[8,4096]{1,0:T(8,128)S(1)} %get-tuple-element.100), channel_id=1, source_target_pairs={{0,6},{1,7},{2,0},{3,1},{4,2},{5,3},{6,4},{7,5},{8,14},{9,15},{10,... | collective-permute-start | bytes 393224 | tf_op jit(solution)/shard_map/ppermute | solution.py:342
  192.3 53.2 %collective-permute-start.20 = (f32[8,4096]{1,0:T(8,128)S(1)}, f32[8,4096]{1,0:T(8,128)S(1)}, u32[]{:S(2)}, u32[]{:S(2)}) collective-permute-start(f32[8,4096]{1,0:T(8,128)S(1)} %get-tuple-element.99), channel_id=1, source_target_pairs={{0,4},{1,5},{2,6},{3,7},{4,0},{5,1},{6,2},{7,3},{8,12},{9,13},{10,... | collective-permute-start | bytes 393224 | tf_op jit(solution)/shard_map/ppermute | solution.py:342
  194.2 2.2 copy-start.1
  196.3 9.2 %copy-start.10 = (f32[4,8,4096]{2,1,0:T(8,128)S(1)}, f32[4,8,4096]{2,1,0:T(8,128)}, u32[]{:S(2)}) copy-start(f32[4,8,4096]{2,1,0:T(8,128)} %get-tuple-element.66) | copy-start | bytes 1572868
  204.4 20.9 %copy-start.9 = (f32[4,8,4096]{2,1,0:T(8,128)S(1)}, f32[4,8,4096]{2,1,0:T(8,128)}, u32[]{:S(2)}) copy-start(f32[4,8,4096]{2,1,0:T(8,128)} %get-tuple-element.81) | copy-start | bytes 1572868
  204.4 32.3 %copy-start.12 = (f32[4,8,4096]{2,1,0:T(8,128)S(1)}, f32[4,8,4096]{2,1,0:T(8,128)}, u32[]{:S(2)}) copy-start(f32[4,8,4096]{2,1,0:T(8,128)} %get-tuple-element.83) | copy-start | bytes 1572868
  204.4 40.4 %copy-start.11 = (f32[4,8,4096]{2,1,0:T(8,128)S(1)}, f32[4,8,4096]{2,1,0:T(8,128)}, u32[]{:S(2)}) copy-start(f32[4,8,4096]{2,1,0:T(8,128)} %get-tuple-element.78) | copy-start | bytes 1572868
  204.4 50.6 %copy-start.14 = (f32[128,1,41]{2,1,0:T(1,128)S(1)}, f32[128,1,41]{2,1,0:T(1,128)}, u32[]{:S(2)}) copy-start(f32[128,1,41]{2,1,0:T(1,128)} %copy-done.13) | copy-start | bytes 62980
  204.4 8.6 %collective-permute-start.29 = (f32[2,8,4096]{2,1,0:T(8,128)}, f32[2,8,4096]{2,1,0:T(8,128)S(1)}, u32[]{:S(2)}, u32[]{:S(2)}) collective-permute-start(f32[2,8,4096]{2,1,0:T(8,128)} %get-tuple-element.85), channel_id=1, source_target_pairs={{0,8},{1,9},{2,10},{3,11},{4,12},{5,13},{6,14},{7,15},{8,16},{9,17... | collective-permute-start | bytes 786440 | tf_op jit(solution)/shard_map/ppermute | solution.py:328
  205.7 55.3 %copy-start.15 = (s32[128,1]{0,1:T(1,128)S(1)}, s32[128,1]{0,1:T(1,128)}, u32[]{:S(2)}) copy-start(s32[128,1]{0,1:T(1,128)} %param.9) | copy-start | bytes 1540
  205.7 55.3 %copy-start.16 = (s32[128]{0:T(128)S(1)}, s32[128]{0:T(128)}, u32[]{:S(2)}) copy-start(s32[128]{0:T(128)} %param.11) | copy-start | bytes 1540
  205.7 55.3 %copy-start.17 = (s32[128]{0:T(128)S(1)}, s32[128]{0:T(128)}, u32[]{:S(2)}) copy-start(s32[128]{0:T(128)} %param.10) | copy-start | bytes 1540
  205.7 9.4 %collective-permute-start.31 = (f32[2,8,4096]{2,1,0:T(8,128)}, f32[2,8,4096]{2,1,0:T(8,128)S(1)}, u32[]{:S(2)}, u32[]{:S(2)}) collective-permute-start(f32[2,8,4096]{2,1,0:T(8,128)} %get-tuple-element.87), channel_id=1, source_target_pairs={{0,24},{1,25},{2,26},{3,27},{4,28},{5,29},{6,30},{7,31},{8,0},{9,1... | collective-permute-start | bytes 786440 | tf_op jit(solution)/shard_map/ppermute | solution.py:328
  213.0 7.8 %collective-permute-start.22 = (f32[2,8,4096]{2,1,0:T(8,128)}, f32[2,8,4096]{2,1,0:T(8,128)S(1)}, u32[]{:S(2)}, u32[]{:S(2)}) collective-permute-start(f32[2,8,4096]{2,1,0:T(8,128)} %get-tuple-element.80), channel_id=1, source_target_pairs={{0,2},{1,3},{2,4},{3,5},{4,6},{5,7},{6,0},{7,1},{8,10},{9,11},{10,... | collective-permute-start | bytes 786440 | tf_op jit(solution)/shard_map/ppermute | solution.py:327
  215.1 6.8 %collective-permute-start.24 = (f32[2,8,4096]{2,1,0:T(8,128)}, f32[2,8,4096]{2,1,0:T(8,128)S(1)}, u32[]{:S(2)}, u32[]{:S(2)}) collective-permute-start(f32[2,8,4096]{2,1,0:T(8,128)} %get-tuple-element.82), channel_id=1, source_target_pairs={{0,6},{1,7},{2,0},{3,1},{4,2},{5,3},{6,4},{7,5},{8,14},{9,15},{10,... | collective-permute-start | bytes 786440 | tf_op jit(solution)/shard_map/ppermute | solution.py:327
  220.8 11.9 %collective-permute-start.30 = (f32[4,8,4096]{2,1,0:T(8,128)S(1)}, f32[4,8,4096]{2,1,0:T(8,128)S(1)}, u32[]{:S(2)}, u32[]{:S(2)}) collective-permute-start(f32[4,8,4096]{2,1,0:T(8,128)S(1)} %pad_maximum_fusion.6), channel_id=1, source_target_pairs={{0,8},{1,9},{2,10},{3,11},{4,12},{5,13},{6,14},{7,15},{8,16},{9,17... | collective-permute-start | bytes 1572872 | tf_op jit(solution)/shard_map/ppermute | solution.py:338
  222.0 11.2 %collective-permute-start.32 = (f32[4,8,4096]{2,1,0:T(8,128)S(1)}, f32[4,8,4096]{2,1,0:T(8,128)S(1)}, u32[]{:S(2)}, u32[]{:S(2)}) collective-permute-start(f32[4,8,4096]{2,1,0:T(8,128)S(1)} %pad_maximum_fusion.7), channel_id=1, source_target_pairs={{0,24},{1,25},{2,26},{3,27},{4,28},{5,29},{6,30},{7,31},{8,0},{9,1... | collective-permute-start | bytes 1572872 | tf_op jit(solution)/shard_map/ppermute | solution.py:338
  232.7 12.1 %collective-permute-start.23 = (f32[4,8,4096]{2,1,0:T(8,128)S(1)}, f32[4,8,4096]{2,1,0:T(8,128)S(1)}, u32[]{:S(2)}, u32[]{:S(2)}) collective-permute-start(f32[4,8,4096]{2,1,0:T(8,128)S(1)} %pad_maximum_fusion.4), channel_id=1, source_target_pairs={{0,2},{1,3},{2,4},{3,5},{4,6},{5,7},{6,0},{7,1},{8,10},{9,11},{10,... | collective-permute-start | bytes 1572872 | tf_op jit(solution)/shard_map/ppermute | solution.py:337
  233.1 11.6 %collective-permute-start.25 = (f32[4,8,4096]{2,1,0:T(8,128)S(1)}, f32[4,8,4096]{2,1,0:T(8,128)S(1)}, u32[]{:S(2)}, u32[]{:S(2)}) collective-permute-start(f32[4,8,4096]{2,1,0:T(8,128)S(1)} %pad_maximum_fusion.5), channel_id=1, source_target_pairs={{0,6},{1,7},{2,0},{3,1},{4,2},{5,3},{6,4},{7,5},{8,14},{9,15},{10,... | collective-permute-start | bytes 1572872 | tf_op jit(solution)/shard_map/ppermute | solution.py:337
  236.8 12.6 %collective-permute-start.11 = (f32[8,4096]{1,0:T(8,128)S(1)}, f32[8,4096]{1,0:T(8,128)S(1)}, u32[]{:S(2)}, u32[]{:S(2)}) collective-permute-start(f32[8,4096]{1,0:T(8,128)S(1)} %get-tuple-element.105), channel_id=1, source_target_pairs={{0,8},{1,9},{2,10},{3,11},{4,12},{5,13},{6,14},{7,15},{8,16},{9,17... | collective-permute-start | bytes 393224 | tf_op jit(solution)/shard_map/ppermute | solution.py:341
  236.9 13.4 %collective-permute-start.12 = (f32[8,4096]{1,0:T(8,128)S(1)}, f32[8,4096]{1,0:T(8,128)S(1)}, u32[]{:S(2)}, u32[]{:S(2)}) collective-permute-start(f32[8,4096]{1,0:T(8,128)S(1)} %get-tuple-element.104), channel_id=1, source_target_pairs={{0,24},{1,25},{2,26},{3,27},{4,28},{5,29},{6,30},{7,31},{8,0},{9,1... | collective-permute-start | bytes 393224 | tf_op jit(solution)/shard_map/ppermute | solution.py:341
  244.8 7.8 %collective-permute-start.13 = (f32[8,4096]{1,0:T(8,128)S(1)}, f32[8,4096]{1,0:T(8,128)S(1)}, u32[]{:S(2)}, u32[]{:S(2)}) collective-permute-start(f32[8,4096]{1,0:T(8,128)S(1)} %get-tuple-element.103), channel_id=1, source_target_pairs={{0,16},{1,17},{2,18},{3,19},{4,20},{5,21},{6,22},{7,23},{8,24},{9,... | collective-permute-start | bytes 393224 | tf_op jit(solution)/shard_map/ppermute | solution.py:341
  244.8 8.7 %collective-permute-start.33 = (f32[8,4096]{1,0:T(8,128)S(1)}, f32[8,4096]{1,0:T(8,128)S(1)}, u32[]{:S(2)}, u32[]{:S(2)}) collective-permute-start(f32[8,4096]{1,0:T(8,128)S(1)} %get-tuple-element.93), channel_id=1, source_target_pairs={{0,2},{1,3},{2,4},{3,5},{4,6},{5,7},{6,0},{7,1},{8,10},{9,11},{10,... | collective-permute-start | bytes 393224 | tf_op jit(solution)/shard_map/ppermute | solution.py:342
  245.5 0.7 copy-start.6
  246.2 10.2 %collective-permute-start.34 = (f32[8,4096]{1,0:T(8,128)S(1)}, f32[8,4096]{1,0:T(8,128)S(1)}, u32[]{:S(2)}, u32[]{:S(2)}) collective-permute-start(f32[8,4096]{1,0:T(8,128)S(1)} %get-tuple-element.92), channel_id=1, source_target_pairs={{0,6},{1,7},{2,0},{3,1},{4,2},{5,3},{6,4},{7,5},{8,14},{9,15},{10,... | collective-permute-start | bytes 393224 | tf_op jit(solution)/shard_map/ppermute | solution.py:342
  249.4 7.0 %collective-permute-start.35 = (f32[8,4096]{1,0:T(8,128)S(1)}, f32[8,4096]{1,0:T(8,128)S(1)}, u32[]{:S(2)}, u32[]{:S(2)}) collective-permute-start(f32[8,4096]{1,0:T(8,128)S(1)} %get-tuple-element.91), channel_id=1, source_target_pairs={{0,4},{1,5},{2,6},{3,7},{4,0},{5,1},{6,2},{7,3},{8,12},{9,13},{10,... | collective-permute-start | bytes 393224 | tf_op jit(solution)/shard_map/ppermute | solution.py:342
  250.2 6.4 %collective-permute-start.26 = (f32[8,4096]{1,0:T(8,128)}, f32[8,4096]{1,0:T(8,128)S(1)}, u32[]{:S(2)}, u32[]{:S(2)}) collective-permute-start(f32[8,4096]{1,0:T(8,128)} %get-tuple-element.97), channel_id=1, source_target_pairs={{0,8},{1,9},{2,10},{3,11},{4,12},{5,13},{6,14},{7,15},{8,16},{9,17... | collective-permute-start | bytes 393224 | tf_op jit(solution)/shard_map/ppermute | solution.py:341
  252.6 5.0 %collective-permute-start.27 = (f32[8,4096]{1,0:T(8,128)S(1)}, f32[8,4096]{1,0:T(8,128)S(1)}, u32[]{:S(2)}, u32[]{:S(2)}) collective-permute-start(f32[8,4096]{1,0:T(8,128)S(1)} %get-tuple-element.96), channel_id=1, source_target_pairs={{0,24},{1,25},{2,26},{3,27},{4,28},{5,29},{6,30},{7,31},{8,0},{9,1... | collective-permute-start | bytes 393224 | tf_op jit(solution)/shard_map/ppermute | solution.py:341
  253.5 6.5 %collective-permute-start.28 = (f32[8,4096]{1,0:T(8,128)S(1)}, f32[8,4096]{1,0:T(8,128)S(1)}, u32[]{:S(2)}, u32[]{:S(2)}) collective-permute-start(f32[8,4096]{1,0:T(8,128)S(1)} %get-tuple-element.95), channel_id=1, source_target_pairs={{0,16},{1,17},{2,18},{3,19},{4,20},{5,21},{6,22},{7,23},{8,24},{9,... | collective-permute-start | bytes 393224 | tf_op jit(solution)/shard_map/ppermute | solution.py:341
  260.0 0.9 copy-start.7
  261.2 0.8 copy-start.8
Sparse Core Ops, SparseCore 0:
  9.5 73.5 all-gather.2

commit v3 on v0

--- a/solution.py
+++ b/solution.py
@@ -10,6 +10,7 @@
 TILE = 128
 SLOTS = 40
 FIRST = 30
+EARLY = 20
 VMEM = 24 * 1024 * 1024
 AXES = ("grp", "inner")
 
@@ -269,11 +270,13 @@
         f2 = [lax.ppermute(s2[s], "inner", along_x[s]) for s in (1, 3, 2)]
         return [s1[0] + f1[0] + f1[1] + f1[2], s2[0] + f2[0] + f2[1] + f2[2]]
 
-    p1, p3 = pack(integrals, index, ((1, 0, total), (3, 0, total)), total)
+    p1, p3 = pack(integrals, index, ((1, 0, EARLY), (3, 0, EARLY)), total)
     r1, r3 = lax.ppermute(p1, "grp", along_y[1]), lax.ppermute(p3, "grp", along_y[3])
-    p2, p4, p0 = pack(integrals, index, ((2, 0, FIRST), (2, FIRST, total), (0, 0, total)), total)
+    codes, _ = lax.optimization_barrier((codes, p1))
+    later, _ = lax.optimization_barrier((index, codes))
+    p5, p6, p2, p4, p0 = pack(integrals, later, ((1, EARLY, total), (3, EARLY, total), (2, 0, FIRST), (2, FIRST, total), (0, 0, total)), total)
+    r5, r6 = lax.ppermute(p5, "grp", along_y[1]), lax.ppermute(p6, "grp", along_y[3])
     r2, r4 = lax.ppermute(p2, "grp", along_y[2]), lax.ppermute(p4, "grp", along_y[2])
-    codes, _ = lax.optimization_barrier((codes, p4))
     note = jnp.concatenate(
         [
             jnp.broadcast_to(codes.reshape(n_grp, 1, total), (n_grp, n_inner, total)),
@@ -289,16 +292,16 @@
     note = jnp.stack([lax.dynamic_index_in_dim(note, core, axis=1, keepdims=False), lax.dynamic_index_in_dim(note, 1 - core, axis=1, keepdims=False)])
     note = note.astype(jnp.int32)
 
-    def codes_of(steps, lo, hi):
-        return jnp.concatenate([note[side, s, lo:hi] for side in range(2) for s in steps])
+    def codes_of(*pieces):
+        return jnp.concatenate([note[side, s, lo:hi] for side in range(2) for s, lo, hi in pieces])
 
     def with_other(tiles):
         return [*tiles, *[lax.ppermute(t, "inner", across) for t in tiles]]
 
     amp = arrange(where, amp)
-    acc, token = ladder(codes_of((0, 1, 3), 0, total), amp, None, with_other([p0, gate(r1, note), gate(r3, note)]), False, blocks)
-    acc, token = ladder(codes_of((2,), 0, FIRST), amp, acc, with_other([gate(r2, token)]), False, blocks)
-    parts = ladder(codes_of((2,), FIRST, total), amp, acc, with_other([gate(r4, token)]), True, blocks)
+    acc, token = ladder(codes_of((0, 0, total), (1, 0, EARLY), (3, 0, EARLY), (1, EARLY, total), (3, EARLY, total)), amp, None, with_other([p0, gate(r1, note), gate(r3, note), r5, r6]), False, blocks)
+    acc, token = ladder(codes_of((2, 0, FIRST)), amp, acc, with_other([gate(r2, token)]), False, blocks)
+    parts = ladder(codes_of((2, FIRST, total)), amp, acc, with_other([gate(r4, token)]), True, blocks)
     pieces = finish(parts)
     out = jnp.concatenate(pieces, axis=1)
 

time: 229 us -> 248 us (1.083); the launches traced: 230 us -> 245 us
  waiting for transfers between devices: 105 us -> 116 us
  starting transfers between devices: 38.4 us -> 48.8 us
  Pallas kernels: 57.2 us -> 47.2 us
  local copies, waits for them, and re-layouts: 6.02 us -> 10.2 us
    ppermute x0 -> x2, waiting for transfers between devices: none -> 61.3 us  [the longest x1 41.3 us: per_device(): lax.ppermute(p6, 'grp', along_y[3])]
    all_to_all x1, waiting for transfers between devices: 40 us -> 10.4 us  [per_device(): lax.all_to_all(note.reshape(devices, total + 1), AXES, split_axis=0, conc...]
    ppermute x1, waiting for transfers between devices: 12.4 us -> 0.01 us  [per_device(): lax.ppermute(p2, 'grp', along_y[2])]
    pallas_call x2, Pallas kernels: 15.3 us -> 10.1 us  [pack(): pl.pallas_call(functools.partial(pack_kernel, spans, total), out_shape=[j...]
    pallas_call x3, Pallas kernels: 40.7 us -> 35.9 us  [ladder(): pl.pallas_call(functools.partial(ladder_kernel, counts, blocks, acc is No...]
    unnamed x24 -> x32, local copies, waits for them, and re-layouts: 5.75 us -> 9.89 us
    ppermute x3, starting transfers between devices: 3.31 us -> 6.57 us  [finish(): f1 = [lax.ppermute(s1[s], 'inner', along_z[s]) for s in (1, 3, 2)]]
    ppermute x0 -> x2, starting transfers between devices: none -> 3.24 us  [the longest x1 2.28 us: per_device(): lax.ppermute(p6, 'grp', along_y[3])]
  transfers between devices with their start and end apart: 25 -> 29, of which waited for: 13 -> 17; matrix products, arithmetic and copies ran while one was open for 4% -> 3% of each run, Pallas kernels for 22% -> 17%
where the time goes in v3:
time: 248 us; the launch traced here: 245 us
  waiting for transfers between devices  116 us (47%)
  starting transfers between devices  48.8 us (20%)
  Pallas kernels  47.2 us (19%)
  between operations  14.4 us (6%)
  local copies, waits for them, and re-layouts  10.2 us (4%)
  other arithmetic  8.05 us (3%)
    ppermute x1, waiting for transfers between devices, per_device(): lax.ppermute(p6, 'grp', along_y[3])  41.3 us
    pallas_call x3, Pallas kernels, ladder(): pl.pallas_call(functools.partial(ladder_kernel, counts, blocks, acc is No...  35.9 us
    ppermute x2, waiting for transfers between devices, finish(): lax.ppermute(x_up, 'inner', along_x[1])  22.8 us
    ppermute x1, waiting for transfers between devices, per_device(): lax.ppermute(p5, 'grp', along_y[1])  20 us
    all_to_all x1, waiting for transfers between devices, per_device(): lax.all_to_all(note.reshape(devices, total + 1), AXES, split_axis=0, conc...  10.4 us
    pallas_call x2, Pallas kernels, pack(): pl.pallas_call(functools.partial(pack_kernel, spans, total), out_shape=[j...  10.1 us
    all_to_all x1, starting transfers between devices, per_device(): lax.all_to_all(note.reshape(devices, total + 1), AXES, split_axis=0, conc...  9.93 us
    unnamed x32, local copies, waits for them, and re-layouts  9.89 us
  transfers between devices with their start and end apart: 29, of which 17 were waited for; matrix products, arithmetic and copies ran while one was open for 3% of the time, Pallas kernels for 17%

profile of v3, /device:TPU:0, one launch (start us, length us, event | category | flops | bytes accessed | tf_op | source)
XLA Modules:
  0.0 244.5 jit_solution(17375986957187687112)
XLA Ops:
  6.5 0.7 all-gather.3.cloned.1.call-update
  7.3 0.7 fusion.36
  7.9 0.7 and_select_fusion.2
  8.6 0.2 convert_reduce_fusion.2
  8.8 0.7 fusion.33
  9.6 3.4 %shard_map.57 = (f32[20,128,128]{2,1,0:T(8,128)}, f32[20,128,128]{2,1,0:T(8,128)S(1)}) custom-call(s32[160]{0:T(256)S(1)} %get-tuple-element.55.index, f32[128,128,128]{2,1,0:T(8,128)} %tiles.3), custom_call_target="tpu_custom_call" | custom-call | bytes 1000 | tf_op jit(solution)/shard_map/pallas_call | solution.py:61
  13.1 1.7 collective-permute-start
  14.8 1.6 collective-permute-start.1
  16.5 1.3 pad_convert_fusion
  17.7 9.9 %all-to-all-start.3 = ((f32[128,1,41]{2,1,0:T(1,128)}), f32[128,1,41]{2,1,0:T(1,128)S(1)}, u32[]{:S(2)}, u32[]{:S(2)}) async-start(f32[128,1,41]{2,1,0:T(1,128)} %bitcast.13), calls=%async_computation.4 | async-start | bytes 131072 | tf_op jit(solution)/shard_map/all_to_all | solution.py:287
  27.7 6.6 %shard_map.59 = (f32[20,128,128]{2,1,0:T(8,128)}, f32[20,128,128]{2,1,0:T(8,128)}, f32[30,128,128]{2,1,0:T(8,128)S(1)}, f32[10,128,128]{2,1,0:T(8,128)S(1)}, f32[40,128,128]{2,1,0:T(8,128)S(1)}) custom-call(s32[160]{0:T(256)S(1)} %get-tuple-element.55.index, f32[128,128,128]{2,1,0:T(8,128)} %tiles.3), custom_call_target="tpu_custom_call" | custom-call | bytes 1000 | tf_op jit(solution)/shard_map/pallas_call | solution.py:61
  34.3 1.5 copy-done.1
  35.8 1.3 copy-done.5
  37.1 0.9 copy-done.6
  38.0 1.0 collective-permute-start.2
  39.0 2.3 collective-permute-start.3
  41.2 10.4 %all-to-all-done.3 = f32[128,1,41]{2,1,0:T(1,128)S(1)} async-done(((f32[128,1,41]{2,1,0:T(1,128)}), f32[128,1,41]{2,1,0:T(1,128)S(1)}, u32[]{:S(2)}, u32[]{:S(2)}) %all-to-all-start.3) | async-done | bytes 21024 | tf_op jit(solution)/shard_map/all_to_all | solution.py:287
  51.8 0.5 collective-permute-start.4
  52.3 1.8 collective-permute-start.9
  54.1 20.0 %collective-permute-done.2.refs_5_ = f32[20,128,128]{2,1,0:T(8,128)} collective-permute-done((f32[20,128,128]{2,1,0:T(8,128)}, f32[20,128,128]{2,1,0:T(8,128)}, u32[]{:S(2)}, u32[]{:S(2)}) %collective-permute-start.2) | collective-permute-done | bytes 1310752 | tf_op jit(solution)/shard_map/ppermute | solution.py:278
  74.1 41.3 %collective-permute-done.3.refs_6_ = f32[20,128,128]{2,1,0:T(8,128)} collective-permute-done((f32[20,128,128]{2,1,0:T(8,128)}, f32[20,128,128]{2,1,0:T(8,128)}, u32[]{:S(2)}, u32[]{:S(2)}) %collective-permute-start.3) | collective-permute-done | bytes 1310752 | tf_op jit(solution)/shard_map/ppermute | solution.py:278
  115.4 1.1 copy-done.3
  116.5 0.5 collective-permute-start.8
  117.3 3.4 %copy-done = f32[128,16384]{1,0:T(8,128)S(1)} copy-done((f32[128,16384]{1,0:T(8,128)S(1)}, f32[128,16384]{1,0:T(8,128)}, u32[]{:S(2)}) %copy-start) | copy-done | bytes 8388632
  120.7 1.2 shard_map.58.refs_1_
  121.9 0.5 copy-done.2
  122.4 0.4 copy-done.4
  122.8 23.5 %shard_map.62 = (f32[4,4,8,16384]{3,2,1,0:T(8,128)S(1)}, f32[8,128]{1,0:T(8,128)S(1)}) custom-call(s32[240]{0:T(256)S(1)} %concatenate.33.refs_0_, f32[16,8,16384]{2,1,0:T(8,128)S(1)} %shard_map.58.refs_1_, f32[40,128,128]{2,1,0:T(8,128)S(1)} %copy-done.2, f32[20,128,128]{2,1,0:T(8,128)} %shard_map.60.refs_3_, f32[20,128,128]{2,1,0:T(8,128)S(1)} %shard_map.61.refs_4_, ...), custom_call_target="tpu_custom_call" | custom-call | bytes 1000 | tf_op jit(solution)/shard_map/pallas_call | solution.py:196
  146.4 2.8 %collective-permute-start.11 = (f32[10,128,128]{2,1,0:T(8,128)S(1)}, f32[10,128,128]{2,1,0:T(8,128)S(1)}, u32[]{:S(2)}, u32[]{:S(2)}) collective-permute-start(f32[10,128,128]{2,1,0:T(8,128)S(1)} %copy-done.7), channel_id=1, source_target_pairs={{0,64},{32,96},{64,0},{96,32},{1,65},{33,97},{65,1},{97,33},{2,66}... | collective-permute-start | bytes 1966088 | tf_op jit(solution)/shard_map/ppermute | solution.py:279
  149.4 1.0 collective-permute-done.10.refs_4_
  150.4 7.9 %shard_map.64 = (f32[4,4,8,16384]{3,2,1,0:T(8,128)S(1)}, f32[8,128]{1,0:T(8,128)S(1)}) custom-call(s32[60]{0:T(128)S(1)} %pad_add_fusion.2.refs_0_, f32[16,8,16384]{2,1,0:T(8,128)S(1)} %shard_map.58.refs_1_, f32[4,4,8,16384]{3,2,1,0:T(8,128)S(1)} %get-tuple-element.60.refs_2_, ...), custom_call_target="tpu_custom_call", output_to_operand_aliasing={{0}: (2, {})} | custom-call | bytes 1000 | tf_op jit(solution)/shard_map/pallas_call | solution.py:196
  158.3 6.8 %collective-permute-done.11.refs_0_ = f32[10,128,128]{2,1,0:T(8,128)S(1)} collective-permute-done((f32[10,128,128]{2,1,0:T(8,128)S(1)}, f32[10,128,128]{2,1,0:T(8,128)S(1)}, u32[]{:S(2)}, u32[]{:S(2)}) %collective-permute-start.11) | collective-permute-done | bytes 655392 | tf_op jit(solution)/shard_map/ppermute | solution.py:279
  165.2 1.9 collective-permute-done.12.refs_4_
  167.2 4.5 %shard_map.66 = (f32[2,8,8192]{2,1,0:T(8,128)}, f32[2,8,8192]{2,1,0:T(8,128)}, f32[2,8,8192]{2,1,0:T(8,128)}, f32[2,8,8192]{2,1,0:T(8,128)}, f32[4,8,8192]{2,1,0...) custom-call(s32[20]{0:T(128)S(1)} %pad_add_fusion.refs_0_, ...), custom_call_target="tpu_custom_call" | custom-call | bytes 1000 | tf_op jit(solution)/shard_map/pallas_call | solution.py:196
  171.7 2.0 collective-permute-start.13
  173.7 0.7 slice_reduce_fusion
  175.0 1.4 collective-permute-start.15
  176.4 1.9 collective-permute-start.20
  178.3 2.1 collective-permute-start.22
  180.4 6.8 %collective-permute-done.13 = f32[2,8,8192]{2,1,0:T(8,128)S(1)} collective-permute-done((f32[2,8,8192]{2,1,0:T(8,128)}, f32[2,8,8192]{2,1,0:T(8,128)S(1)}, u32[]{:S(2)}, u32[]{:S(2)}) %collective-permute-start.13) | collective-permute-done | bytes 524320 | tf_op jit(solution)/shard_map/ppermute | solution.py:255
  187.2 1.3 slice_add_fusion.3
  188.6 0.7 collective-permute-start.14
  189.3 1.4 fusion.37
  190.8 2.6 %collective-permute-start.16 = (f32[4,8,8192]{2,1,0:T(8,128)S(1)}, f32[4,8,8192]{2,1,0:T(8,128)S(1)}, u32[]{:S(2)}, u32[]{:S(2)}) collective-permute-start(f32[4,8,8192]{2,1,0:T(8,128)S(1)} %pad_maximum_fusion.1), channel_id=1, source_target_pairs={{0,6},{1,7},{2,0},{3,1},{4,2},{5,3},{6,4},{7,5},{8,14},{9,15},{10,... | collective-permute-start | bytes 3145736 | tf_op jit(solution)/shard_map/ppermute | solution.py:265
  193.6 2.3 collective-permute-start.21
  196.1 2.2 collective-permute-start.23
  198.3 16.0 %collective-permute-done.14 = f32[4,8,8192]{2,1,0:T(8,128)S(1)} collective-permute-done((f32[4,8,8192]{2,1,0:T(8,128)S(1)}, f32[4,8,8192]{2,1,0:T(8,128)S(1)}, u32[]{:S(2)}, u32[]{:S(2)}) %collective-permute-start.14) | collective-permute-done | bytes 1048608 | tf_op jit(solution)/shard_map/ppermute | solution.py:265
  214.2 0.8 collective-permute-done.16
  215.2 2.0 collective-permute-start.17
  217.1 2.2 collective-permute-start.18
  219.3 2.4 collective-permute-start.19
  221.7 0.2 collective-permute-done.21
  221.9 0.6 collective-permute-done.23
  222.6 0.3 collective-permute-start.24
  222.9 3.0 %collective-permute-start.25 = (f32[8,8192]{1,0:T(8,128)S(1)}, f32[8,8192]{1,0:T(8,128)S(1)}, u32[]{:S(2)}, u32[]{:S(2)}) collective-permute-start(f32[8,8192]{1,0:T(8,128)S(1)} %get-tuple-element.82), channel_id=1, source_target_pairs={{0,6},{1,7},{2,0},{3,1},{4,2},{5,3},{6,4},{7,5},{8,14},{9,15},{10,... | collective-permute-start | bytes 786440 | tf_op jit(solution)/shard_map/ppermute | solution.py:270
  226.0 0.4 collective-permute-done.17
  226.3 1.4 collective-permute-start.26
  227.8 0.4 collective-permute-done.18
  228.1 4.3 %collective-permute-done.19 = f32[8,8192]{1,0:T(8,128)S(1)} collective-permute-done((f32[8,8192]{1,0:T(8,128)S(1)}, f32[8,8192]{1,0:T(8,128)S(1)}, u32[]{:S(2)}, u32[]{:S(2)}) %collective-permute-start.19) | collective-permute-done | bytes 262176 | tf_op jit(solution)/shard_map/ppermute | solution.py:269
  232.6 0.4 collective-permute-done.24
  233.0 1.6 collective-permute-done.25
  234.6 1.9 collective-permute-done.26
  236.7 0.2 conditional.1
  236.9 0.8 copy-done.8
  (74 shorter events, 1.9 us)
Async XLA Ops:
  6.5 110.8 %all-gather.3.cloned.1.call-start = ((), (), s32[]{:S(2)}) async-start(), calls=%async_computation.6 | async-start | bytes 8912896 | tf_op jit(solution)/shard_map/all_gather | solution.py:233
  13.1 38.7 %collective-permute-start = (f32[20,128,128]{2,1,0:T(8,128)}, f32[20,128,128]{2,1,0:T(8,128)}, u32[]{:S(2)}, u32[]{:S(2)}) collective-permute-start(f32[20,128,128]{2,1,0:T(8,128)} %get-tuple-element.53), channel_id=1, source_target_pairs={{0,32},{32,64},{64,96},{96,0},{1,33},{33,65},{65,97},{97,1},{2,34}... | collective-permute-start | bytes 3932168 | tf_op jit(solution)/shard_map/ppermute | solution.py:274
  14.8 37.5 %collective-permute-start.1 = (f32[20,128,128]{2,1,0:T(8,128)S(1)}, f32[20,128,128]{2,1,0:T(8,128)S(1)}, u32[]{:S(2)}, u32[]{:S(2)}) collective-permute-start(f32[20,128,128]{2,1,0:T(8,128)S(1)} %get-tuple-element.57), channel_id=1, source_target_pairs={{0,96},{32,0},{64,32},{96,64},{1,97},{33,1},{65,33},{97,65},{2,98}... | collective-permute-start | bytes 3932168 | tf_op jit(solution)/shard_map/ppermute | solution.py:274
  17.7 33.9 %all-to-all-start.3 = ((f32[128,1,41]{2,1,0:T(1,128)}), f32[128,1,41]{2,1,0:T(1,128)S(1)}, u32[]{:S(2)}, u32[]{:S(2)}) async-start(f32[128,1,41]{2,1,0:T(1,128)} %bitcast.13), calls=%async_computation.4 | async-start | bytes 131072 | tf_op jit(solution)/shard_map/all_to_all | solution.py:287
  34.3 1.5 copy-start.1
  35.8 1.3 copy-start.5
  37.1 0.9 copy-start.6
  38.0 36.1 %collective-permute-start.2 = (f32[20,128,128]{2,1,0:T(8,128)}, f32[20,128,128]{2,1,0:T(8,128)}, u32[]{:S(2)}, u32[]{:S(2)}) collective-permute-start(f32[20,128,128]{2,1,0:T(8,128)} %get-tuple-element.58), channel_id=1, source_target_pairs={{0,32},{32,64},{64,96},{96,0},{1,33},{33,65},{65,97},{97,1},{2,34}... | collective-permute-start | bytes 3932168 | tf_op jit(solution)/shard_map/ppermute | solution.py:278
  39.0 76.4 %collective-permute-start.3 = (f32[20,128,128]{2,1,0:T(8,128)}, f32[20,128,128]{2,1,0:T(8,128)}, u32[]{:S(2)}, u32[]{:S(2)}) collective-permute-start(f32[20,128,128]{2,1,0:T(8,128)} %get-tuple-element.59), channel_id=1, source_target_pairs={{0,96},{32,0},{64,32},{96,64},{1,97},{33,1},{65,33},{97,65},{2,98}... | collective-permute-start | bytes 3932168 | tf_op jit(solution)/shard_map/ppermute | solution.py:278
  51.7 63.7 %collective-permute-start.5 = (f32[20,128,128]{2,1,0:T(8,128)}, f32[20,128,128]{2,1,0:T(8,128)S(1)}, u32[]{:S(2)}, u32[]{:S(2)}) collective-permute-start(f32[20,128,128]{2,1,0:T(8,128)} %shard_map.60.refs_3_), channel_id=1, source_target_pairs={{0,1},{1,0},{2,3},{3,2},{4,5},{5,4},{6,7},{7,6},{8,9},{9,8},{10,11... | collective-permute-start | bytes 3932168 | tf_op jit(solution)/shard_map/ppermute | solution.py:299
  51.8 70.1 %collective-permute-start.4 = (f32[40,128,128]{2,1,0:T(8,128)}, f32[40,128,128]{2,1,0:T(8,128)}, u32[]{:S(2)}, u32[]{:S(2)}) collective-permute-start(f32[40,128,128]{2,1,0:T(8,128)} %copy-done.1), channel_id=1, source_target_pairs={{0,1},{1,0},{2,3},{3,2},{4,5},{5,4},{6,7},{7,6},{8,9},{9,8},{10,11... | collective-permute-start | bytes 7864328 | tf_op jit(solution)/shard_map/ppermute | solution.py:299
  52.3 94.0 %collective-permute-start.9 = (f32[30,128,128]{2,1,0:T(8,128)}, f32[30,128,128]{2,1,0:T(8,128)S(1)}, u32[]{:S(2)}, u32[]{:S(2)}) collective-permute-start(f32[30,128,128]{2,1,0:T(8,128)} %copy-done.5), channel_id=1, source_target_pairs={{0,64},{32,96},{64,0},{96,32},{1,65},{33,97},{65,1},{97,33},{2,66}... | collective-permute-start | bytes 5898248 | tf_op jit(solution)/shard_map/ppermute | solution.py:279
  74.1 47.8 %collective-permute-start.6 = (f32[20,128,128]{2,1,0:T(8,128)S(1)}, f32[20,128,128]{2,1,0:T(8,128)}, u32[]{:S(2)}, u32[]{:S(2)}) collective-permute-start(f32[20,128,128]{2,1,0:T(8,128)S(1)} %shard_map.61.refs_4_), channel_id=1, source_target_pairs={{0,1},{1,0},{2,3},{3,2},{4,5},{5,4},{6,7},{7,6},{8,9},{9,8},{10,11... | collective-permute-start | bytes 3932168 | tf_op jit(solution)/shard_map/ppermute | solution.py:299
  115.4 6.5 %collective-permute-start.7 = (f32[20,128,128]{2,1,0:T(8,128)}, f32[20,128,128]{2,1,0:T(8,128)}, u32[]{:S(2)}, u32[]{:S(2)}) collective-permute-start(f32[20,128,128]{2,1,0:T(8,128)} %collective-permute-done.2.refs_5_), channel_id=1, source_target_pairs={{0,1},{1,0},{2,3},{3,2},{4,5},{5,4},{6,7},{7,6},{8,9},{9,8},{10,11... | collective-permute-start | bytes 3932168 | tf_op jit(solution)/shard_map/ppermute | solution.py:299
  115.4 1.1 copy-start.3
  116.5 5.4 %collective-permute-start.8 = (f32[20,128,128]{2,1,0:T(8,128)}, f32[20,128,128]{2,1,0:T(8,128)}, u32[]{:S(2)}, u32[]{:S(2)}) collective-permute-start(f32[20,128,128]{2,1,0:T(8,128)} %collective-permute-done.3.refs_6_), channel_id=1, source_target_pairs={{0,1},{1,0},{2,3},{3,2},{4,5},{5,4},{6,7},{7,6},{8,9},{9,8},{10,11... | collective-permute-start | bytes 3932168 | tf_op jit(solution)/shard_map/ppermute | solution.py:299
  117.3 3.4 %copy-start = (f32[128,16384]{1,0:T(8,128)S(1)}, f32[128,16384]{1,0:T(8,128)}, u32[]{:S(2)}) copy-start(f32[128,16384]{1,0:T(8,128)} %all-gather.3.cloned.1.call-done) | copy-start | bytes 25165828
  120.7 1.7 copy-start.2
  120.7 2.1 copy-start.4
  121.9 24.6 %copy-start.7 = (f32[10,128,128]{2,1,0:T(8,128)S(1)}, f32[10,128,128]{2,1,0:T(8,128)}, u32[]{:S(2)}) copy-start(f32[10,128,128]{2,1,0:T(8,128)} %copy-done.6) | copy-start | bytes 1966084
  146.3 4.1 %collective-permute-start.10 = (f32[30,128,128]{2,1,0:T(8,128)S(1)}, f32[30,128,128]{2,1,0:T(8,128)S(1)}, u32[]{:S(2)}, u32[]{:S(2)}) collective-permute-start(f32[30,128,128]{2,1,0:T(8,128)S(1)} %shard_map.63.refs_3_), channel_id=1, source_target_pairs={{0,1},{1,0},{2,3},{3,2},{4,5},{5,4},{6,7},{7,6},{8,9},{9,8},{10,11... | collective-permute-start | bytes 5898248 | tf_op jit(solution)/shard_map/ppermute | solution.py:299
  146.4 18.7 %collective-permute-start.11 = (f32[10,128,128]{2,1,0:T(8,128)S(1)}, f32[10,128,128]{2,1,0:T(8,128)S(1)}, u32[]{:S(2)}, u32[]{:S(2)}) collective-permute-start(f32[10,128,128]{2,1,0:T(8,128)S(1)} %copy-done.7), channel_id=1, source_target_pairs={{0,64},{32,96},{64,0},{96,32},{1,65},{33,97},{65,1},{97,33},{2,66}... | collective-permute-start | bytes 1966088 | tf_op jit(solution)/shard_map/ppermute | solution.py:279
  165.1 2.1 collective-permute-start.12
  171.7 21.7 %copy-start.12 = (f32[4,8,8192]{2,1,0:T(8,128)S(1)}, f32[4,8,8192]{2,1,0:T(8,128)}, u32[]{:S(2)}) copy-start(f32[4,8,8192]{2,1,0:T(8,128)} %get-tuple-element.72) | copy-start | bytes 3145732
  171.7 24.2 %copy-start.11 = (f32[4,8,8192]{2,1,0:T(8,128)S(1)}, f32[4,8,8192]{2,1,0:T(8,128)}, u32[]{:S(2)}) copy-start(f32[4,8,8192]{2,1,0:T(8,128)} %get-tuple-element.74) | copy-start | bytes 3145732
  171.7 15.5 %collective-permute-start.13 = (f32[2,8,8192]{2,1,0:T(8,128)}, f32[2,8,8192]{2,1,0:T(8,128)S(1)}, u32[]{:S(2)}, u32[]{:S(2)}) collective-permute-start(f32[2,8,8192]{2,1,0:T(8,128)} %get-tuple-element.68), channel_id=1, source_target_pairs={{0,2},{1,3},{2,4},{3,5},{4,6},{5,7},{6,0},{7,1},{8,10},{9,11},{10,... | collective-permute-start | bytes 1572872 | tf_op jit(solution)/shard_map/ppermute | solution.py:255
  175.0 14.4 %collective-permute-start.15 = (f32[2,8,8192]{2,1,0:T(8,128)}, f32[2,8,8192]{2,1,0:T(8,128)S(1)}, u32[]{:S(2)}, u32[]{:S(2)}) collective-permute-start(f32[2,8,8192]{2,1,0:T(8,128)} %get-tuple-element.70), channel_id=1, source_target_pairs={{0,6},{1,7},{2,0},{3,1},{4,2},{5,3},{6,4},{7,5},{8,14},{9,15},{10,... | collective-permute-start | bytes 1572872 | tf_op jit(solution)/shard_map/ppermute | solution.py:255
  176.4 17.1 %collective-permute-start.20 = (f32[2,8,8192]{2,1,0:T(8,128)}, f32[2,8,8192]{2,1,0:T(8,128)S(1)}, u32[]{:S(2)}, u32[]{:S(2)}) collective-permute-start(f32[2,8,8192]{2,1,0:T(8,128)} %get-tuple-element.73), channel_id=1, source_target_pairs={{0,8},{1,9},{2,10},{3,11},{4,12},{5,13},{6,14},{7,15},{8,16},{9,17... | collective-permute-start | bytes 1572872 | tf_op jit(solution)/shard_map/ppermute | solution.py:256
  178.3 17.6 %collective-permute-start.22 = (f32[2,8,8192]{2,1,0:T(8,128)}, f32[2,8,8192]{2,1,0:T(8,128)S(1)}, u32[]{:S(2)}, u32[]{:S(2)}) collective-permute-start(f32[2,8,8192]{2,1,0:T(8,128)} %get-tuple-element.75), channel_id=1, source_target_pairs={{0,24},{1,25},{2,26},{3,27},{4,28},{5,29},{6,30},{7,31},{8,0},{9,1... | collective-permute-start | bytes 1572872 | tf_op jit(solution)/shard_map/ppermute | solution.py:256
  188.5 26.5 %copy-start.10 = (f32[4,8,8192]{2,1,0:T(8,128)S(1)}, f32[4,8,8192]{2,1,0:T(8,128)}, u32[]{:S(2)}) copy-start(f32[4,8,8192]{2,1,0:T(8,128)} %get-tuple-element.66) | copy-start | bytes 3145732
  188.6 25.7 %collective-permute-start.14 = (f32[4,8,8192]{2,1,0:T(8,128)S(1)}, f32[4,8,8192]{2,1,0:T(8,128)S(1)}, u32[]{:S(2)}, u32[]{:S(2)}) collective-permute-start(f32[4,8,8192]{2,1,0:T(8,128)S(1)} %pad_maximum_fusion), channel_id=1, source_target_pairs={{0,2},{1,3},{2,4},{3,5},{4,6},{5,7},{6,0},{7,1},{8,10},{9,11},{10,... | collective-permute-start | bytes 3145736 | tf_op jit(solution)/shard_map/ppermute | solution.py:265
  189.3 33.2 %copy-start.9 = (f32[4,8,8192]{2,1,0:T(8,128)S(1)}, f32[4,8,8192]{2,1,0:T(8,128)}, u32[]{:S(2)}) copy-start(f32[4,8,8192]{2,1,0:T(8,128)} %get-tuple-element.71) | copy-start | bytes 3145732
  190.8 24.2 %collective-permute-start.16 = (f32[4,8,8192]{2,1,0:T(8,128)S(1)}, f32[4,8,8192]{2,1,0:T(8,128)S(1)}, u32[]{:S(2)}, u32[]{:S(2)}) collective-permute-start(f32[4,8,8192]{2,1,0:T(8,128)S(1)} %pad_maximum_fusion.1), channel_id=1, source_target_pairs={{0,6},{1,7},{2,0},{3,1},{4,2},{5,3},{6,4},{7,5},{8,14},{9,15},{10,... | collective-permute-start | bytes 3145736 | tf_op jit(solution)/shard_map/ppermute | solution.py:265
  193.6 43.0 %copy-start.13 = (s32[128,1]{0,1:T(1,128)S(1)}, s32[128,1]{0,1:T(1,128)}, u32[]{:S(2)}) copy-start(s32[128,1]{0,1:T(1,128)} %param.9) | copy-start | bytes 1540
  193.6 43.0 %copy-start.14 = (s32[128]{0:T(128)S(1)}, s32[128]{0:T(128)}, u32[]{:S(2)}) copy-start(s32[128]{0:T(128)} %param.11) | copy-start | bytes 1540
  193.6 43.0 %copy-start.15 = (s32[128]{0:T(128)S(1)}, s32[128]{0:T(128)}, u32[]{:S(2)}) copy-start(s32[128]{0:T(128)} %param.10) | copy-start | bytes 1540
  193.6 28.3 %collective-permute-start.21 = (f32[4,8,8192]{2,1,0:T(8,128)S(1)}, f32[4,8,8192]{2,1,0:T(8,128)S(1)}, u32[]{:S(2)}, u32[]{:S(2)}) collective-permute-start(f32[4,8,8192]{2,1,0:T(8,128)S(1)} %pad_maximum_fusion.2), channel_id=1, source_target_pairs={{0,8},{1,9},{2,10},{3,11},{4,12},{5,13},{6,14},{7,15},{8,16},{9,17... | collective-permute-start | bytes 3145736 | tf_op jit(solution)/shard_map/ppermute | solution.py:266
  196.1 26.5 %collective-permute-start.23 = (f32[4,8,8192]{2,1,0:T(8,128)S(1)}, f32[4,8,8192]{2,1,0:T(8,128)S(1)}, u32[]{:S(2)}, u32[]{:S(2)}) collective-permute-start(f32[4,8,8192]{2,1,0:T(8,128)S(1)} %pad_maximum_fusion.3), channel_id=1, source_target_pairs={{0,24},{1,25},{2,26},{3,27},{4,28},{5,29},{6,30},{7,31},{8,0},{9,1... | collective-permute-start | bytes 3145736 | tf_op jit(solution)/shard_map/ppermute | solution.py:266
  215.2 11.2 %collective-permute-start.17 = (f32[8,8192]{1,0:T(8,128)S(1)}, f32[8,8192]{1,0:T(8,128)S(1)}, u32[]{:S(2)}, u32[]{:S(2)}) collective-permute-start(f32[8,8192]{1,0:T(8,128)S(1)} %get-tuple-element.77), channel_id=1, source_target_pairs={{0,8},{1,9},{2,10},{3,11},{4,12},{5,13},{6,14},{7,15},{8,16},{9,17... | collective-permute-start | bytes 786440 | tf_op jit(solution)/shard_map/ppermute | solution.py:269
  217.1 11.0 %collective-permute-start.18 = (f32[8,8192]{1,0:T(8,128)S(1)}, f32[8,8192]{1,0:T(8,128)S(1)}, u32[]{:S(2)}, u32[]{:S(2)}) collective-permute-start(f32[8,8192]{1,0:T(8,128)S(1)} %get-tuple-element.79), channel_id=1, source_target_pairs={{0,24},{1,25},{2,26},{3,27},{4,28},{5,29},{6,30},{7,31},{8,0},{9,1... | collective-permute-start | bytes 786440 | tf_op jit(solution)/shard_map/ppermute | solution.py:269
  219.3 13.2 %collective-permute-start.19 = (f32[8,8192]{1,0:T(8,128)S(1)}, f32[8,8192]{1,0:T(8,128)S(1)}, u32[]{:S(2)}, u32[]{:S(2)}) collective-permute-start(f32[8,8192]{1,0:T(8,128)S(1)} %get-tuple-element.78), channel_id=1, source_target_pairs={{0,16},{1,17},{2,18},{3,19},{4,20},{5,21},{6,22},{7,23},{8,24},{9,... | collective-permute-start | bytes 786440 | tf_op jit(solution)/shard_map/ppermute | solution.py:269
  222.6 10.3 %collective-permute-start.24 = (f32[8,8192]{1,0:T(8,128)S(1)}, f32[8,8192]{1,0:T(8,128)S(1)}, u32[]{:S(2)}, u32[]{:S(2)}) collective-permute-start(f32[8,8192]{1,0:T(8,128)S(1)} %get-tuple-element.80), channel_id=1, source_target_pairs={{0,2},{1,3},{2,4},{3,5},{4,6},{5,7},{6,0},{7,1},{8,10},{9,11},{10,... | collective-permute-start | bytes 786440 | tf_op jit(solution)/shard_map/ppermute | solution.py:270
  222.9 11.7 %collective-permute-start.25 = (f32[8,8192]{1,0:T(8,128)S(1)}, f32[8,8192]{1,0:T(8,128)S(1)}, u32[]{:S(2)}, u32[]{:S(2)}) collective-permute-start(f32[8,8192]{1,0:T(8,128)S(1)} %get-tuple-element.82), channel_id=1, source_target_pairs={{0,6},{1,7},{2,0},{3,1},{4,2},{5,3},{6,4},{7,5},{8,14},{9,15},{10,... | collective-permute-start | bytes 786440 | tf_op jit(solution)/shard_map/ppermute | solution.py:270
  226.3 10.2 %collective-permute-start.26 = (f32[8,8192]{1,0:T(8,128)S(1)}, f32[8,8192]{1,0:T(8,128)S(1)}, u32[]{:S(2)}, u32[]{:S(2)}) collective-permute-start(f32[8,8192]{1,0:T(8,128)S(1)} %get-tuple-element.81), channel_id=1, source_target_pairs={{0,4},{1,5},{2,6},{3,7},{4,0},{5,1},{6,2},{7,3},{8,12},{9,13},{10,... | collective-permute-start | bytes 786440 | tf_op jit(solution)/shard_map/ppermute | solution.py:270
  236.9 0.8 copy-start.8
Sparse Core Ops, SparseCore 0:
  9.5 73.6 all-gather.2

commit v4 on v3

--- a/solution.py
+++ b/solution.py
@@ -9,8 +9,8 @@
 
 TILE = 128
 SLOTS = 40
-FIRST = 30
-EARLY = 20
+FIRST = 34
+EARLY = 28
 VMEM = 24 * 1024 * 1024
 AXES = ("grp", "inner")
 
@@ -276,7 +276,7 @@
     later, _ = lax.optimization_barrier((index, codes))
     p5, p6, p2, p4, p0 = pack(integrals, later, ((1, EARLY, total), (3, EARLY, total), (2, 0, FIRST), (2, FIRST, total), (0, 0, total)), total)
     r5, r6 = lax.ppermute(p5, "grp", along_y[1]), lax.ppermute(p6, "grp", along_y[3])
-    r2, r4 = lax.ppermute(p2, "grp", along_y[2]), lax.ppermute(p4, "grp", along_y[2])
+    r2, r4 = lax.ppermute(gate(p2, r5, r6), "grp", along_y[2]), lax.ppermute(p4, "grp", along_y[2])
     note = jnp.concatenate(
         [
             jnp.broadcast_to(codes.reshape(n_grp, 1, total), (n_grp, n_inner, total)),

time: 248 us -> 223 us (0.90); the launches traced: 245 us -> 223 us
  waiting for transfers between devices: 116 us -> 82.7 us
  Pallas kernels: 47.2 us -> 57.4 us
    ppermute x1, waiting for transfers between devices: 41.3 us -> 0.06 us  [per_device(): lax.ppermute(p6, 'grp', along_y[3])]
    all_to_all x1, waiting for transfers between devices: 10.4 us -> 0.01 us  [per_device(): lax.all_to_all(note.reshape(devices, total + 1), AXES, split_axis=0, conc...]
    ppermute x1, waiting for transfers between devices: 20 us -> 30.4 us  [per_device(): lax.ppermute(p5, 'grp', along_y[1])]
    ppermute x1, waiting for transfers between devices: 0.01 us -> 8.89 us  [per_device(): lax.ppermute(gate(p2, r5, r6), 'grp', along_y[2])]
    ppermute x1, waiting for transfers between devices: 6.81 us -> 0.01 us  [per_device(): lax.ppermute(p4, 'grp', along_y[2])]
    pallas_call x2, Pallas kernels: 10.1 us -> 16.3 us  [pack(): pl.pallas_call(functools.partial(pack_kernel, spans, total), out_shape=[j...]
    ppermute x7, waiting for transfers between devices: 2.98 us -> 8.69 us  [with_other(): return [*tiles, *[lax.ppermute(t, 'inner', across) for t in tiles]]]
    pallas_call x3, Pallas kernels: 35.9 us -> 40 us  [ladder(): pl.pallas_call(functools.partial(ladder_kernel, counts, blocks, acc is No...]
  transfers between devices with their start and end apart: 29 -> 29, of which waited for: 17 -> 17; matrix products, arithmetic and copies ran while one was open for 3% -> 4% of each run, Pallas kernels for 17% -> 24%
where the time goes in v4:
time: 223 us
  waiting for transfers between devices  82.7 us (37%)
  Pallas kernels  57.4 us (26%)
  starting transfers between devices  47.5 us (21%)
  between operations  14.5 us (7%)
  local copies, waits for them, and re-layouts  11.6 us (5%)
  other arithmetic  9.04 us (4%)
    pallas_call x3, Pallas kernels, ladder(): pl.pallas_call(functools.partial(ladder_kernel, counts, blocks, acc is No...  40 us
    ppermute x1, waiting for transfers between devices, per_device(): lax.ppermute(p5, 'grp', along_y[1])  30.4 us
    ppermute x2, waiting for transfers between devices, finish(): lax.ppermute(x_up, 'inner', along_x[1])  21.9 us
    pallas_call x2, Pallas kernels, pack(): pl.pallas_call(functools.partial(pack_kernel, spans, total), out_shape=[j...  16.3 us
    unnamed x34, local copies, waits for them, and re-layouts  10.5 us
    all_to_all x1, starting transfers between devices, per_device(): lax.all_to_all(note.reshape(devices, total + 1), AXES, split_axis=0, conc...  9.37 us
    ppermute x1, waiting for transfers between devices, per_device(): lax.ppermute(gate(p2, r5, r6), 'grp', along_y[2])  8.89 us
    ppermute x7, waiting for transfers between devices, with_other(): return [*tiles, *[lax.ppermute(t, 'inner', across) for t in tiles]]  8.69 us
  transfers between devices with their start and end apart: 29, of which 17 were waited for; matrix products, arithmetic and copies ran while one was open for 4% of the time, Pallas kernels for 24%

profile of v4, /device:TPU:0, one launch (start us, length us, event | category | flops | bytes accessed | tf_op | source)
XLA Modules:
  0.0 222.9 jit_solution(5803342943045250874)
XLA Ops:
  6.5 0.7 all-gather.3.cloned.1.call-update
  7.3 0.8 fusion.36
  8.1 0.8 and_select_fusion.2
  8.9 0.2 convert_reduce_fusion.2
  9.1 0.6 fusion.33
  9.7 0.1 select_reduce_fusion
  9.9 4.5 %shard_map.57 = (f32[28,128,128]{2,1,0:T(8,128)}, f32[28,128,128]{2,1,0:T(8,128)}) custom-call(s32[160]{0:T(256)S(1)} %get-tuple-element.55.index, f32[128,128,128]{2,1,0:T(8,128)} %tiles.3), custom_call_target="tpu_custom_call" | custom-call | bytes 1000 | tf_op jit(solution)/shard_map/pallas_call | solution.py:61
  14.3 1.7 collective-permute-start
  16.1 1.6 collective-permute-start.1
  17.6 11.8 %shard_map.59 = (f32[12,128,128]{2,1,0:T(8,128)S(1)}, f32[12,128,128]{2,1,0:T(8,128)S(1)}, f32[34,128,128]{2,1,0:T(8,128)S(1)}, f32[6,128,128]{2,1,0:T(8,128)S(1)}, f32[40,128,128]{2,1,0:T(8,128)}) custom-call(s32[160]{0:T(256)S(1)} %get-tuple-element.55.index, f32[128,128,128]{2,1,0:T(8,128)S(1)} %copy-done.8), custom_call_target="tpu_custom_call" | custom-call | bytes 1000 | tf_op jit(solution)/shard_map/pallas_call | solution.py:61
  29.5 1.3 copy-done.3
  30.8 0.4 collective-permute-start.2
  31.2 2.8 %collective-permute-start.3 = (f32[12,128,128]{2,1,0:T(8,128)S(1)}, f32[12,128,128]{2,1,0:T(8,128)S(1)}, u32[]{:S(2)}, u32[]{:S(2)}) collective-permute-start(f32[12,128,128]{2,1,0:T(8,128)S(1)} %get-tuple-element.59), channel_id=1, source_target_pairs={{0,96},{32,0},{64,32},{96,64},{1,97},{33,1},{65,33},{97,65},{2,98}... | collective-permute-start | bytes 2359304 | tf_op jit(solution)/shard_map/ppermute | solution.py:278
  34.1 1.2 pad_convert_fusion
  35.3 9.4 %all-to-all-start.3 = ((f32[128,1,41]{2,1,0:T(1,128)}), f32[128,1,41]{2,1,0:T(1,128)}, u32[]{:S(2)}, u32[]{:S(2)}) async-start(f32[128,1,41]{2,1,0:T(1,128)} %bitcast.120), calls=%async_computation.4 | async-start | bytes 131072 | tf_op jit(solution)/shard_map/all_to_all | solution.py:287
  44.8 30.4 %collective-permute-done.2.refs_5_.refs_1_ = f32[12,128,128]{2,1,0:T(8,128)S(1)} collective-permute-done((f32[12,128,128]{2,1,0:T(8,128)S(1)}, f32[12,128,128]{2,1,0:T(8,128)S(1)}, u32[]{:S(2)}, u32[]{:S(2)}) %collective-permute-start.2) | collective-permute-done | bytes 786464 | tf_op jit(solution)/shard_map/ppermute | solution.py:278
  75.2 1.6 copy-done.4
  76.8 0.9 copy-done.1
  77.7 1.3 copy-done.5
  79.1 2.9 %collective-permute-start.9 = (f32[34,128,128]{2,1,0:T(8,128)}, f32[34,128,128]{2,1,0:T(8,128)S(1)}, u32[]{:S(2)}, u32[]{:S(2)}) collective-permute-start(f32[34,128,128]{2,1,0:T(8,128)} %copy-done.5), channel_id=1, source_target_pairs={{0,64},{32,96},{64,0},{96,32},{1,65},{33,97},{65,1},{97,33},{2,66}... | collective-permute-start | bytes 6684680 | tf_op jit(solution)/shard_map/ppermute | solution.py:279
  82.0 0.7 fusion.25
  82.8 0.5 collective-permute-start.6
  83.4 5.4 %collective-permute-done.7.refs_10_ = f32[12,128,128]{2,1,0:T(8,128)S(1)} collective-permute-done((f32[12,128,128]{2,1,0:T(8,128)S(1)}, f32[12,128,128]{2,1,0:T(8,128)S(1)}, u32[]{:S(2)}, u32[]{:S(2)}) %collective-permute-start.7) | collective-permute-done | bytes 786464 | tf_op jit(solution)/shard_map/ppermute | solution.py:299
  88.8 1.0 copy-done.6
  90.2 3.4 %copy-done = f32[128,16384]{1,0:T(8,128)S(1)} copy-done((f32[128,16384]{1,0:T(8,128)S(1)}, f32[128,16384]{1,0:T(8,128)}, u32[]{:S(2)}) %copy-start) | copy-done | bytes 8388632
  93.6 1.2 shard_map.58.refs_1_
  94.8 0.1 copy-done.7
  95.0 26.4 %shard_map.62 = (f32[4,4,8,16384]{3,2,1,0:T(8,128)S(1)}, f32[8,128]{1,0:T(8,128)S(1)}) custom-call(s32[240]{0:T(256)S(1)} %concatenate.33.refs_0_, f32[16,8,16384]{2,1,0:T(8,128)S(1)} %shard_map.58.refs_1_, f32[40,128,128]{2,1,0:T(8,128)} %get-tuple-element.56.refs_2_, f32[28,128,128]{2,1,0:T(8,128)} %shard_map.60.refs_3_, ...), custom_call_target="tpu_custom_call" | custom-call | bytes 1000 | tf_op jit(solution)/shard_map/pallas_call | solution.py:196
  121.4 8.9 %collective-permute-done.9.refs_0_ = f32[34,128,128]{2,1,0:T(8,128)S(1)} collective-permute-done((f32[34,128,128]{2,1,0:T(8,128)}, f32[34,128,128]{2,1,0:T(8,128)S(1)}, u32[]{:S(2)}, u32[]{:S(2)}) %collective-permute-start.9) | collective-permute-done | bytes 2228256 | tf_op jit(solution)/shard_map/ppermute | solution.py:279
  130.3 2.4 %collective-permute-start.11 = (f32[6,128,128]{2,1,0:T(8,128)S(1)}, f32[6,128,128]{2,1,0:T(8,128)S(1)}, u32[]{:S(2)}, u32[]{:S(2)}) collective-permute-start(f32[6,128,128]{2,1,0:T(8,128)S(1)} %get-tuple-element.64), channel_id=1, source_target_pairs={{0,64},{32,96},{64,0},{96,32},{1,65},{33,97},{65,1},{97,33},{2,66}... | collective-permute-start | bytes 1179656 | tf_op jit(solution)/shard_map/ppermute | solution.py:279
  132.8 1.8 collective-permute-done.10.refs_4_
  134.6 8.8 %shard_map.65 = (f32[4,4,8,16384]{3,2,1,0:T(8,128)S(1)}, f32[8,128]{1,0:T(8,128)S(1)}) custom-call(s32[68]{0:T(128)S(1)} %pad_add_fusion.2.refs_0_, f32[16,8,16384]{2,1,0:T(8,128)S(1)} %shard_map.58.refs_1_, f32[4,4,8,16384]{3,2,1,0:T(8,128)S(1)} %get-tuple-element.60.refs_2_, ...), custom_call_target="tpu_custom_call", output_to_operand_aliasing={{0}: (2, {})} | custom-call | bytes 1000 | tf_op jit(solution)/shard_map/pallas_call | solution.py:196
  143.4 0.2 collective-permute-start.12
  143.8 1.4 collective-permute-done.12.refs_4_
  145.3 4.8 %shard_map.67 = (f32[2,8,8192]{2,1,0:T(8,128)}, f32[2,8,8192]{2,1,0:T(8,128)}, f32[2,8,8192]{2,1,0:T(8,128)}, f32[2,8,8192]{2,1,0:T(8,128)}, f32[4,8,8192]{2,1,0...) custom-call(s32[12]{0:T(128)S(1)} %pad_add_fusion.refs_0_, ...), custom_call_target="tpu_custom_call" | custom-call | bytes 1000 | tf_op jit(solution)/shard_map/pallas_call | solution.py:196
  150.1 1.5 collective-permute-start.13
  151.6 1.5 slice_reduce_fusion
  153.7 1.9 collective-permute-start.15
  155.6 2.0 collective-permute-start.20
  157.6 1.7 collective-permute-start.22
  159.3 6.2 %collective-permute-done.13 = f32[2,8,8192]{2,1,0:T(8,128)S(1)} collective-permute-done((f32[2,8,8192]{2,1,0:T(8,128)}, f32[2,8,8192]{2,1,0:T(8,128)S(1)}, u32[]{:S(2)}, u32[]{:S(2)}) %collective-permute-start.13) | collective-permute-done | bytes 524320 | tf_op jit(solution)/shard_map/ppermute | solution.py:255
  165.6 1.3 slice_add_fusion.3
  166.9 0.2 collective-permute-start.14
  167.2 0.6 collective-permute-done.15
  167.8 1.4 fusion.37
  169.2 3.0 %collective-permute-start.16 = (f32[4,8,8192]{2,1,0:T(8,128)S(1)}, f32[4,8,8192]{2,1,0:T(8,128)S(1)}, u32[]{:S(2)}, u32[]{:S(2)}) collective-permute-start(f32[4,8,8192]{2,1,0:T(8,128)S(1)} %pad_maximum_fusion.1), channel_id=1, source_target_pairs={{0,6},{1,7},{2,0},{3,1},{4,2},{5,3},{6,4},{7,5},{8,14},{9,15},{10,... | collective-permute-start | bytes 3145736 | tf_op jit(solution)/shard_map/ppermute | solution.py:265
  172.4 2.5 %collective-permute-start.21 = (f32[4,8,8192]{2,1,0:T(8,128)S(1)}, f32[4,8,8192]{2,1,0:T(8,128)S(1)}, u32[]{:S(2)}, u32[]{:S(2)}) collective-permute-start(f32[4,8,8192]{2,1,0:T(8,128)S(1)} %pad_maximum_fusion.2), channel_id=1, source_target_pairs={{0,8},{1,9},{2,10},{3,11},{4,12},{5,13},{6,14},{7,15},{8,16},{9,17... | collective-permute-start | bytes 3145736 | tf_op jit(solution)/shard_map/ppermute | solution.py:266
  175.1 1.8 collective-permute-start.23
  176.9 15.7 %collective-permute-done.14 = f32[4,8,8192]{2,1,0:T(8,128)S(1)} collective-permute-done((f32[4,8,8192]{2,1,0:T(8,128)S(1)}, f32[4,8,8192]{2,1,0:T(8,128)S(1)}, u32[]{:S(2)}, u32[]{:S(2)}) %collective-permute-start.14) | collective-permute-done | bytes 1048608 | tf_op jit(solution)/shard_map/ppermute | solution.py:265
  192.6 1.2 collective-permute-done.16
  193.9 2.4 %collective-permute-start.17 = (f32[8,8192]{1,0:T(8,128)S(1)}, f32[8,8192]{1,0:T(8,128)S(1)}, u32[]{:S(2)}, u32[]{:S(2)}) collective-permute-start(f32[8,8192]{1,0:T(8,128)S(1)} %get-tuple-element.77), channel_id=1, source_target_pairs={{0,8},{1,9},{2,10},{3,11},{4,12},{5,13},{6,14},{7,15},{8,16},{9,17... | collective-permute-start | bytes 786440 | tf_op jit(solution)/shard_map/ppermute | solution.py:269
  196.3 1.8 collective-permute-start.18
  198.1 1.5 collective-permute-start.19
  199.6 0.9 collective-permute-done.21
  200.5 0.2 collective-permute-done.23
  201.0 3.2 %collective-permute-start.25 = (f32[8,8192]{1,0:T(8,128)S(1)}, f32[8,8192]{1,0:T(8,128)S(1)}, u32[]{:S(2)}, u32[]{:S(2)}) collective-permute-start(f32[8,8192]{1,0:T(8,128)S(1)} %get-tuple-element.82), channel_id=1, source_target_pairs={{0,6},{1,7},{2,0},{3,1},{4,2},{5,3},{6,4},{7,5},{8,14},{9,15},{10,... | collective-permute-start | bytes 786440 | tf_op jit(solution)/shard_map/ppermute | solution.py:270
  204.2 0.8 collective-permute-done.17
  205.0 1.5 collective-permute-start.26
  206.5 3.1 %collective-permute-done.18 = f32[8,8192]{1,0:T(8,128)S(1)} collective-permute-done((f32[8,8192]{1,0:T(8,128)S(1)}, f32[8,8192]{1,0:T(8,128)S(1)}, u32[]{:S(2)}, u32[]{:S(2)}) %collective-permute-start.18) | collective-permute-done | bytes 262176 | tf_op jit(solution)/shard_map/ppermute | solution.py:269
  209.6 1.6 collective-permute-done.19
  211.3 1.9 collective-permute-done.25
  213.2 1.7 collective-permute-done.26
  215.1 0.2 conditional.1
  215.3 0.8 copy-done.9
  (78 shorter events, 2.1 us)
Async XLA Ops:
  6.5 83.7 %all-gather.3.cloned.1.call-start = ((), (), s32[]{:S(2)}) async-start(), calls=%async_computation.6 | async-start | bytes 8912896 | tf_op jit(solution)/shard_map/all_gather | solution.py:233
  7.3 10.4 %copy-start.8 = (f32[128,128,128]{2,1,0:T(8,128)S(1)}, f32[128,128,128]{2,1,0:T(8,128)}, u32[]{:S(2)}) copy-start(f32[128,128,128]{2,1,0:T(8,128)} %tiles.3) | copy-start | bytes 25165828
  14.3 68.4 %collective-permute-start = (f32[28,128,128]{2,1,0:T(8,128)}, f32[28,128,128]{2,1,0:T(8,128)}, u32[]{:S(2)}, u32[]{:S(2)}) collective-permute-start(f32[28,128,128]{2,1,0:T(8,128)} %get-tuple-element.53), channel_id=1, source_target_pairs={{0,32},{32,64},{64,96},{96,0},{1,33},{33,65},{65,97},{97,1},{2,34}... | collective-permute-start | bytes 5505032 | tf_op jit(solution)/shard_map/ppermute | solution.py:274
  16.1 66.8 %collective-permute-start.1 = (f32[28,128,128]{2,1,0:T(8,128)}, f32[28,128,128]{2,1,0:T(8,128)}, u32[]{:S(2)}, u32[]{:S(2)}) collective-permute-start(f32[28,128,128]{2,1,0:T(8,128)} %get-tuple-element.57), channel_id=1, source_target_pairs={{0,96},{32,0},{64,32},{96,64},{1,97},{33,1},{65,33},{97,65},{2,98}... | collective-permute-start | bytes 5505032 | tf_op jit(solution)/shard_map/ppermute | solution.py:274
  29.4 1.4 copy-start.3
  30.8 44.4 %collective-permute-start.2 = (f32[12,128,128]{2,1,0:T(8,128)S(1)}, f32[12,128,128]{2,1,0:T(8,128)S(1)}, u32[]{:S(2)}, u32[]{:S(2)}) collective-permute-start(f32[12,128,128]{2,1,0:T(8,128)S(1)} %get-tuple-element.58), channel_id=1, source_target_pairs={{0,32},{32,64},{64,96},{96,0},{1,33},{33,65},{65,97},{97,1},{2,34}... | collective-permute-start | bytes 2359304 | tf_op jit(solution)/shard_map/ppermute | solution.py:278
  31.2 44.0 %collective-permute-start.3 = (f32[12,128,128]{2,1,0:T(8,128)S(1)}, f32[12,128,128]{2,1,0:T(8,128)S(1)}, u32[]{:S(2)}, u32[]{:S(2)}) collective-permute-start(f32[12,128,128]{2,1,0:T(8,128)S(1)} %get-tuple-element.59), channel_id=1, source_target_pairs={{0,96},{32,0},{64,32},{96,64},{1,97},{33,1},{65,33},{97,65},{2,98}... | collective-permute-start | bytes 2359304 | tf_op jit(solution)/shard_map/ppermute | solution.py:278
  34.0 60.8 %collective-permute-start.4 = (f32[40,128,128]{2,1,0:T(8,128)}, f32[40,128,128]{2,1,0:T(8,128)}, u32[]{:S(2)}, u32[]{:S(2)}) collective-permute-start(f32[40,128,128]{2,1,0:T(8,128)} %get-tuple-element.56.refs_2_), channel_id=1, source_target_pairs={{0,1},{1,0},{2,3},{3,2},{4,5},{5,4},{6,7},{7,6},{8,9},{9,8},{10,11... | collective-permute-start | bytes 7864328 | tf_op jit(solution)/shard_map/ppermute | solution.py:299
  35.3 46.7 %all-to-all-start.3 = ((f32[128,1,41]{2,1,0:T(1,128)}), f32[128,1,41]{2,1,0:T(1,128)}, u32[]{:S(2)}, u32[]{:S(2)}) async-start(f32[128,1,41]{2,1,0:T(1,128)} %bitcast.120), calls=%async_computation.4 | async-start | bytes 131072 | tf_op jit(solution)/shard_map/all_to_all | solution.py:287
  75.2 1.6 copy-start.4
  76.8 0.9 copy-start.1
  77.7 1.4 copy-start.5
  79.1 51.2 %collective-permute-start.9 = (f32[34,128,128]{2,1,0:T(8,128)}, f32[34,128,128]{2,1,0:T(8,128)S(1)}, u32[]{:S(2)}, u32[]{:S(2)}) collective-permute-start(f32[34,128,128]{2,1,0:T(8,128)} %copy-done.5), channel_id=1, source_target_pairs={{0,64},{32,96},{64,0},{96,32},{1,65},{33,97},{65,1},{97,33},{2,66}... | collective-permute-start | bytes 6684680 | tf_op jit(solution)/shard_map/ppermute | solution.py:279
  82.7 12.1 %collective-permute-start.5 = (f32[28,128,128]{2,1,0:T(8,128)}, f32[28,128,128]{2,1,0:T(8,128)}, u32[]{:S(2)}, u32[]{:S(2)}) collective-permute-start(f32[28,128,128]{2,1,0:T(8,128)} %shard_map.60.refs_3_), channel_id=1, source_target_pairs={{0,1},{1,0},{2,3},{3,2},{4,5},{5,4},{6,7},{7,6},{8,9},{9,8},{10,11... | collective-permute-start | bytes 5505032 | tf_op jit(solution)/shard_map/ppermute | solution.py:299
  82.8 12.0 %collective-permute-start.6 = (f32[28,128,128]{2,1,0:T(8,128)}, f32[28,128,128]{2,1,0:T(8,128)}, u32[]{:S(2)}, u32[]{:S(2)}) collective-permute-start(f32[28,128,128]{2,1,0:T(8,128)} %shard_map.61.refs_4_), channel_id=1, source_target_pairs={{0,1},{1,0},{2,3},{3,2},{4,5},{5,4},{6,7},{7,6},{8,9},{9,8},{10,11... | collective-permute-start | bytes 5505032 | tf_op jit(solution)/shard_map/ppermute | solution.py:299
  83.3 5.5 %collective-permute-start.7 = (f32[12,128,128]{2,1,0:T(8,128)S(1)}, f32[12,128,128]{2,1,0:T(8,128)S(1)}, u32[]{:S(2)}, u32[]{:S(2)}) collective-permute-start(f32[12,128,128]{2,1,0:T(8,128)S(1)} %collective-permute-done.2.refs_5_.refs_1_), channel_id=1, source_target_pairs={{0,1},{1,0},{2,3},{3,2},{4,5},{5,4},{6,7},{7,6},{8,9},{9,8},{10,11... | collective-permute-start | bytes 2359304 | tf_op jit(solution)/shard_map/ppermute | solution.py:299
  88.8 1.0 copy-start.6
  89.8 5.0 %collective-permute-start.8 = (f32[12,128,128]{2,1,0:T(8,128)}, f32[12,128,128]{2,1,0:T(8,128)}, u32[]{:S(2)}, u32[]{:S(2)}) collective-permute-start(f32[12,128,128]{2,1,0:T(8,128)} %copy-done.1), channel_id=1, source_target_pairs={{0,1},{1,0},{2,3},{3,2},{4,5},{5,4},{6,7},{7,6},{8,9},{9,8},{10,11... | collective-permute-start | bytes 2359304 | tf_op jit(solution)/shard_map/ppermute | solution.py:299
  90.2 3.4 %copy-start = (f32[128,16384]{1,0:T(8,128)S(1)}, f32[128,16384]{1,0:T(8,128)}, u32[]{:S(2)}) copy-start(f32[128,16384]{1,0:T(8,128)} %all-gather.3.cloned.1.call-done) | copy-start | bytes 25165828
  93.6 1.2 copy-start.2
  93.6 1.4 copy-start.7
  130.3 4.3 %collective-permute-start.10 = (f32[34,128,128]{2,1,0:T(8,128)S(1)}, f32[34,128,128]{2,1,0:T(8,128)S(1)}, u32[]{:S(2)}, u32[]{:S(2)}) collective-permute-start(f32[34,128,128]{2,1,0:T(8,128)S(1)} %shard_map.64.refs_3_), channel_id=1, source_target_pairs={{0,1},{1,0},{2,3},{3,2},{4,5},{5,4},{6,7},{7,6},{8,9},{9,8},{10,11... | collective-permute-start | bytes 6684680 | tf_op jit(solution)/shard_map/ppermute | solution.py:299
  130.3 13.2 %collective-permute-start.11 = (f32[6,128,128]{2,1,0:T(8,128)S(1)}, f32[6,128,128]{2,1,0:T(8,128)S(1)}, u32[]{:S(2)}, u32[]{:S(2)}) collective-permute-start(f32[6,128,128]{2,1,0:T(8,128)S(1)} %get-tuple-element.64), channel_id=1, source_target_pairs={{0,64},{32,96},{64,0},{96,32},{1,65},{33,97},{65,1},{97,33},{2,66}... | collective-permute-start | bytes 1179656 | tf_op jit(solution)/shard_map/ppermute | solution.py:279
  143.4 1.8 collective-permute-start.12
  150.1 22.1 %copy-start.13 = (f32[4,8,8192]{2,1,0:T(8,128)S(1)}, f32[4,8,8192]{2,1,0:T(8,128)}, u32[]{:S(2)}) copy-start(f32[4,8,8192]{2,1,0:T(8,128)} %get-tuple-element.72) | copy-start | bytes 3145732
  150.1 24.8 %copy-start.12 = (f32[4,8,8192]{2,1,0:T(8,128)S(1)}, f32[4,8,8192]{2,1,0:T(8,128)}, u32[]{:S(2)}) copy-start(f32[4,8,8192]{2,1,0:T(8,128)} %get-tuple-element.74) | copy-start | bytes 3145732
  150.1 15.5 %collective-permute-start.13 = (f32[2,8,8192]{2,1,0:T(8,128)}, f32[2,8,8192]{2,1,0:T(8,128)S(1)}, u32[]{:S(2)}, u32[]{:S(2)}) collective-permute-start(f32[2,8,8192]{2,1,0:T(8,128)} %get-tuple-element.68), channel_id=1, source_target_pairs={{0,2},{1,3},{2,4},{3,5},{4,6},{5,7},{6,0},{7,1},{8,10},{9,11},{10,... | collective-permute-start | bytes 1572872 | tf_op jit(solution)/shard_map/ppermute | solution.py:255
  153.7 14.1 %collective-permute-start.15 = (f32[2,8,8192]{2,1,0:T(8,128)}, f32[2,8,8192]{2,1,0:T(8,128)S(1)}, u32[]{:S(2)}, u32[]{:S(2)}) collective-permute-start(f32[2,8,8192]{2,1,0:T(8,128)} %get-tuple-element.70), channel_id=1, source_target_pairs={{0,6},{1,7},{2,0},{3,1},{4,2},{5,3},{6,4},{7,5},{8,14},{9,15},{10,... | collective-permute-start | bytes 1572872 | tf_op jit(solution)/shard_map/ppermute | solution.py:255
  155.6 16.6 %collective-permute-start.20 = (f32[2,8,8192]{2,1,0:T(8,128)}, f32[2,8,8192]{2,1,0:T(8,128)S(1)}, u32[]{:S(2)}, u32[]{:S(2)}) collective-permute-start(f32[2,8,8192]{2,1,0:T(8,128)} %get-tuple-element.73), channel_id=1, source_target_pairs={{0,8},{1,9},{2,10},{3,11},{4,12},{5,13},{6,14},{7,15},{8,16},{9,17... | collective-permute-start | bytes 1572872 | tf_op jit(solution)/shard_map/ppermute | solution.py:256
  157.6 17.3 %collective-permute-start.22 = (f32[2,8,8192]{2,1,0:T(8,128)}, f32[2,8,8192]{2,1,0:T(8,128)S(1)}, u32[]{:S(2)}, u32[]{:S(2)}) collective-permute-start(f32[2,8,8192]{2,1,0:T(8,128)} %get-tuple-element.75), channel_id=1, source_target_pairs={{0,24},{1,25},{2,26},{3,27},{4,28},{5,29},{6,30},{7,31},{8,0},{9,1... | collective-permute-start | bytes 1572872 | tf_op jit(solution)/shard_map/ppermute | solution.py:256
  166.8 26.9 %copy-start.11 = (f32[4,8,8192]{2,1,0:T(8,128)S(1)}, f32[4,8,8192]{2,1,0:T(8,128)}, u32[]{:S(2)}) copy-start(f32[4,8,8192]{2,1,0:T(8,128)} %get-tuple-element.66) | copy-start | bytes 3145732
  166.9 25.7 %collective-permute-start.14 = (f32[4,8,8192]{2,1,0:T(8,128)S(1)}, f32[4,8,8192]{2,1,0:T(8,128)S(1)}, u32[]{:S(2)}, u32[]{:S(2)}) collective-permute-start(f32[4,8,8192]{2,1,0:T(8,128)S(1)} %pad_maximum_fusion), channel_id=1, source_target_pairs={{0,2},{1,3},{2,4},{3,5},{4,6},{5,7},{6,0},{7,1},{8,10},{9,11},{10,... | collective-permute-start | bytes 3145736 | tf_op jit(solution)/shard_map/ppermute | solution.py:265
  167.8 33.0 %copy-start.10 = (f32[4,8,8192]{2,1,0:T(8,128)S(1)}, f32[4,8,8192]{2,1,0:T(8,128)}, u32[]{:S(2)}) copy-start(f32[4,8,8192]{2,1,0:T(8,128)} %get-tuple-element.71) | copy-start | bytes 3145732
  169.2 24.5 %collective-permute-start.16 = (f32[4,8,8192]{2,1,0:T(8,128)S(1)}, f32[4,8,8192]{2,1,0:T(8,128)S(1)}, u32[]{:S(2)}, u32[]{:S(2)}) collective-permute-start(f32[4,8,8192]{2,1,0:T(8,128)S(1)} %pad_maximum_fusion.1), channel_id=1, source_target_pairs={{0,6},{1,7},{2,0},{3,1},{4,2},{5,3},{6,4},{7,5},{8,14},{9,15},{10,... | collective-permute-start | bytes 3145736 | tf_op jit(solution)/shard_map/ppermute | solution.py:265
  172.4 42.7 %copy-start.14 = (s32[128,1]{0,1:T(1,128)S(1)}, s32[128,1]{0,1:T(1,128)}, u32[]{:S(2)}) copy-start(s32[128,1]{0,1:T(1,128)} %param.9) | copy-start | bytes 1540
  172.4 42.7 %copy-start.15 = (s32[128]{0:T(128)S(1)}, s32[128]{0:T(128)}, u32[]{:S(2)}) copy-start(s32[128]{0:T(128)} %param.11) | copy-start | bytes 1540
  172.4 42.7 %copy-start.16 = (s32[128]{0:T(128)S(1)}, s32[128]{0:T(128)}, u32[]{:S(2)}) copy-start(s32[128]{0:T(128)} %param.10) | copy-start | bytes 1540
  172.4 28.1 %collective-permute-start.21 = (f32[4,8,8192]{2,1,0:T(8,128)S(1)}, f32[4,8,8192]{2,1,0:T(8,128)S(1)}, u32[]{:S(2)}, u32[]{:S(2)}) collective-permute-start(f32[4,8,8192]{2,1,0:T(8,128)S(1)} %pad_maximum_fusion.2), channel_id=1, source_target_pairs={{0,8},{1,9},{2,10},{3,11},{4,12},{5,13},{6,14},{7,15},{8,16},{9,17... | collective-permute-start | bytes 3145736 | tf_op jit(solution)/shard_map/ppermute | solution.py:266
  175.1 25.7 %collective-permute-start.23 = (f32[4,8,8192]{2,1,0:T(8,128)S(1)}, f32[4,8,8192]{2,1,0:T(8,128)S(1)}, u32[]{:S(2)}, u32[]{:S(2)}) collective-permute-start(f32[4,8,8192]{2,1,0:T(8,128)S(1)} %pad_maximum_fusion.3), channel_id=1, source_target_pairs={{0,24},{1,25},{2,26},{3,27},{4,28},{5,29},{6,30},{7,31},{8,0},{9,1... | collective-permute-start | bytes 3145736 | tf_op jit(solution)/shard_map/ppermute | solution.py:266
  193.9 11.1 %collective-permute-start.17 = (f32[8,8192]{1,0:T(8,128)S(1)}, f32[8,8192]{1,0:T(8,128)S(1)}, u32[]{:S(2)}, u32[]{:S(2)}) collective-permute-start(f32[8,8192]{1,0:T(8,128)S(1)} %get-tuple-element.77), channel_id=1, source_target_pairs={{0,8},{1,9},{2,10},{3,11},{4,12},{5,13},{6,14},{7,15},{8,16},{9,17... | collective-permute-start | bytes 786440 | tf_op jit(solution)/shard_map/ppermute | solution.py:269
  196.3 13.4 %collective-permute-start.18 = (f32[8,8192]{1,0:T(8,128)S(1)}, f32[8,8192]{1,0:T(8,128)S(1)}, u32[]{:S(2)}, u32[]{:S(2)}) collective-permute-start(f32[8,8192]{1,0:T(8,128)S(1)} %get-tuple-element.79), channel_id=1, source_target_pairs={{0,24},{1,25},{2,26},{3,27},{4,28},{5,29},{6,30},{7,31},{8,0},{9,1... | collective-permute-start | bytes 786440 | tf_op jit(solution)/shard_map/ppermute | solution.py:269
  198.1 13.2 %collective-permute-start.19 = (f32[8,8192]{1,0:T(8,128)S(1)}, f32[8,8192]{1,0:T(8,128)S(1)}, u32[]{:S(2)}, u32[]{:S(2)}) collective-permute-start(f32[8,8192]{1,0:T(8,128)S(1)} %get-tuple-element.78), channel_id=1, source_target_pairs={{0,16},{1,17},{2,18},{3,19},{4,20},{5,21},{6,22},{7,23},{8,24},{9,... | collective-permute-start | bytes 786440 | tf_op jit(solution)/shard_map/ppermute | solution.py:269
  200.9 10.4 %collective-permute-start.24 = (f32[8,8192]{1,0:T(8,128)S(1)}, f32[8,8192]{1,0:T(8,128)S(1)}, u32[]{:S(2)}, u32[]{:S(2)}) collective-permute-start(f32[8,8192]{1,0:T(8,128)S(1)} %get-tuple-element.80), channel_id=1, source_target_pairs={{0,2},{1,3},{2,4},{3,5},{4,6},{5,7},{6,0},{7,1},{8,10},{9,11},{10,... | collective-permute-start | bytes 786440 | tf_op jit(solution)/shard_map/ppermute | solution.py:270
  201.0 12.3 %collective-permute-start.25 = (f32[8,8192]{1,0:T(8,128)S(1)}, f32[8,8192]{1,0:T(8,128)S(1)}, u32[]{:S(2)}, u32[]{:S(2)}) collective-permute-start(f32[8,8192]{1,0:T(8,128)S(1)} %get-tuple-element.82), channel_id=1, source_target_pairs={{0,6},{1,7},{2,0},{3,1},{4,2},{5,3},{6,4},{7,5},{8,14},{9,15},{10,... | collective-permute-start | bytes 786440 | tf_op jit(solution)/shard_map/ppermute | solution.py:270
  205.0 10.0 %collective-permute-start.26 = (f32[8,8192]{1,0:T(8,128)S(1)}, f32[8,8192]{1,0:T(8,128)S(1)}, u32[]{:S(2)}, u32[]{:S(2)}) collective-permute-start(f32[8,8192]{1,0:T(8,128)S(1)} %get-tuple-element.81), channel_id=1, source_target_pairs={{0,4},{1,5},{2,6},{3,7},{4,0},{5,1},{6,2},{7,3},{8,12},{9,13},{10,... | collective-permute-start | bytes 786440 | tf_op jit(solution)/shard_map/ppermute | solution.py:270
  215.3 0.8 copy-start.9
Sparse Core Ops, SparseCore 0:
  9.5 73.9 all-gather.2

commit v5 on v4

--- a/solution.py
+++ b/solution.py
@@ -81,11 +81,11 @@
     pass
 
 
-def gate(value, *after):
+def gate(value, *after, array=jax.ShapeDtypeStruct):
     any_spec = pl.BlockSpec(memory_space=pl.ANY)
     return pl.pallas_call(
         gate_kernel,
-        out_shape=jax.ShapeDtypeStruct(value.shape, value.dtype),
+        out_shape=array(value.shape, value.dtype),
         in_specs=[any_spec] * (1 + len(after)),
         out_specs=any_spec,
         input_output_aliases={0: 0},
@@ -276,7 +276,7 @@
     later, _ = lax.optimization_barrier((index, codes))
     p5, p6, p2, p4, p0 = pack(integrals, later, ((1, EARLY, total), (3, EARLY, total), (2, 0, FIRST), (2, FIRST, total), (0, 0, total)), total)
     r5, r6 = lax.ppermute(p5, "grp", along_y[1]), lax.ppermute(p6, "grp", along_y[3])
-    r2, r4 = lax.ppermute(gate(p2, r5, r6), "grp", along_y[2]), lax.ppermute(p4, "grp", along_y[2])
+    r2, r4 = lax.ppermute(gate(pltpu.with_memory_space_constraint(p2, pltpu.HBM), r5, r6, array=pltpu.HBM), "grp", along_y[2]), lax.ppermute(p4, "grp", along_y[2])
     note = jnp.concatenate(
         [
             jnp.broadcast_to(codes.reshape(n_grp, 1, total), (n_grp, n_inner, total)),
@@ -300,6 +300,7 @@
 
     amp = arrange(where, amp)
     acc, token = ladder(codes_of((0, 0, total), (1, 0, EARLY), (3, 0, EARLY), (1, EARLY, total), (3, EARLY, total)), amp, None, with_other([p0, gate(r1, note), gate(r3, note), r5, r6]), False, blocks)
+    token, overflow = lax.optimization_barrier((token, overflow))
     acc, token = ladder(codes_of((2, 0, FIRST)), amp, acc, with_other([gate(r2, token)]), False, blocks)
     parts = ladder(codes_of((2, FIRST, total)), amp, acc, with_other([gate(r4, token)]), True, blocks)
     pieces = finish(parts)

time: 223 us -> 220 us (0.987)
  Pallas kernels: 57.4 us -> 52.5 us
  waiting for transfers between devices: 82.7 us -> 87.4 us
  local copies, waits for them, and re-layouts: 11.6 us -> 7.49 us
    pallas_call x3, Pallas kernels: 40 us -> 35.1 us  [ladder(): pl.pallas_call(functools.partial(ladder_kernel, counts, blocks, acc is No...]
    unnamed x34 -> x26, local copies, waits for them, and re-layouts: 10.5 us -> 6.43 us
    ppermute x2, waiting for transfers between devices: 21.9 us -> 24.2 us  [finish(): lax.ppermute(x_up, 'inner', along_x[1])]
  transfers between devices with their start and end apart: 29 -> 29, of which waited for: 17 -> 17; matrix products, arithmetic and copies ran while one was open for 4% -> 5% of each run, Pallas kernels for 24% -> 22%
where the time goes in v5:
time: 220 us; the launch traced here: 219 us
  waiting for transfers between devices  87.4 us (40%)
  Pallas kernels  52.5 us (24%)
  starting transfers between devices  47.7 us (22%)
  between operations  14.5 us (7%)
  other arithmetic  9.31 us (4%)
  local copies, waits for them, and re-layouts  7.49 us (3%)
    pallas_call x3, Pallas kernels, ladder(): pl.pallas_call(functools.partial(ladder_kernel, counts, blocks, acc is No...  35.1 us
    ppermute x1, waiting for transfers between devices, per_device(): lax.ppermute(p5, 'grp', along_y[1])  30.2 us
    ppermute x2, waiting for transfers between devices, finish(): lax.ppermute(x_up, 'inner', along_x[1])  24.2 us
    pallas_call x2, Pallas kernels, pack(): pl.pallas_call(functools.partial(pack_kernel, spans, total), out_shape=[j...  16.2 us
    ppermute x1, waiting for transfers between devices, per_device(): lax.ppermute(gate(pltpu.with_memory_space_constraint(p2, pltpu.HBM), r5,...  10.4 us
    all_to_all x1, starting transfers between devices, per_device(): lax.all_to_all(note.reshape(devices, total + 1), AXES, split_axis=0, conc...  9.37 us
    ppermute x7, waiting for transfers between devices, with_other(): return [*tiles, *[lax.ppermute(t, 'inner', across) for t in tiles]]  8.88 us
    unnamed x26, local copies, waits for them, and re-layouts  6.43 us
  transfers between devices with their start and end apart: 29, of which 17 were waited for; matrix products, arithmetic and copies ran while one was open for 5% of the time, Pallas kernels for 22%

profile of v5, /device:TPU:0, one launch (start us, length us, event | category | flops | bytes accessed | tf_op | source)
XLA Modules:
  0.0 219.2 jit_solution(5888739085374085254)
XLA Ops:
  6.5 0.7 all-gather.3.cloned.1.call-update
  7.3 0.8 fusion.36
  8.1 0.8 and_select_fusion.2
  8.9 0.2 convert_reduce_fusion.2
  9.1 0.7 fusion.33
  9.8 0.1 select_reduce_fusion
  10.0 4.5 %shard_map.57 = (f32[28,128,128]{2,1,0:T(8,128)}, f32[28,128,128]{2,1,0:T(8,128)}) custom-call(s32[160]{0:T(256)S(1)} %get-tuple-element.57.index, f32[128,128,128]{2,1,0:T(8,128)} %tiles.3), custom_call_target="tpu_custom_call" | custom-call | bytes 1000 | tf_op jit(solution)/shard_map/pallas_call | solution.py:61
  14.4 1.7 collective-permute-start
  16.2 1.6 collective-permute-start.1
  17.8 11.8 %shard_map.59 = (f32[12,128,128]{2,1,0:T(8,128)S(1)}, f32[12,128,128]{2,1,0:T(8,128)S(1)}, f32[34,128,128]{2,1,0:T(8,128)S(1)}, f32[6,128,128]{2,1,0:T(8,128)S(1)}, f32[40,128,128]{2,1,0:T(8,128)}) custom-call(s32[160]{0:T(256)S(1)} %get-tuple-element.57.index, f32[128,128,128]{2,1,0:T(8,128)S(1)} %copy-done.4), custom_call_target="tpu_custom_call" | custom-call | bytes 1000 | tf_op jit(solution)/shard_map/pallas_call | solution.py:61
  29.5 1.3 copy-done.3
  30.9 0.4 collective-permute-start.2
  31.3 2.8 %collective-permute-start.3 = (f32[12,128,128]{2,1,0:T(8,128)S(1)}, f32[12,128,128]{2,1,0:T(8,128)S(1)}, u32[]{:S(2)}, u32[]{:S(2)}) collective-permute-start(f32[12,128,128]{2,1,0:T(8,128)S(1)} %get-tuple-element.61), channel_id=1, source_target_pairs={{0,96},{32,0},{64,32},{96,64},{1,97},{33,1},{65,33},{97,65},{2,98}... | collective-permute-start | bytes 2359304 | tf_op jit(solution)/shard_map/ppermute | solution.py:278
  34.2 1.3 pad_convert_fusion
  35.5 9.4 %all-to-all-start.3 = ((f32[128,1,41]{2,1,0:T(1,128)}), f32[128,1,41]{2,1,0:T(1,128)}, u32[]{:S(2)}, u32[]{:S(2)}) async-start(f32[128,1,41]{2,1,0:T(1,128)} %bitcast.120), calls=%async_computation.4 | async-start | bytes 131072 | tf_op jit(solution)/shard_map/all_to_all | solution.py:287
  45.0 30.2 %collective-permute-done.2.refs_5_.refs_1_ = f32[12,128,128]{2,1,0:T(8,128)S(1)} collective-permute-done((f32[12,128,128]{2,1,0:T(8,128)S(1)}, f32[12,128,128]{2,1,0:T(8,128)S(1)}, u32[]{:S(2)}, u32[]{:S(2)}) %collective-permute-start.2) | collective-permute-done | bytes 786464 | tf_op jit(solution)/shard_map/ppermute | solution.py:278
  75.3 0.9 copy-done.1
  76.2 2.9 %collective-permute-start.9 = (f32[34,128,128]{2,1,0:T(8,128)}, f32[34,128,128]{2,1,0:T(8,128)S(1)}, u32[]{:S(2)}, u32[]{:S(2)}) collective-permute-start(f32[34,128,128]{2,1,0:T(8,128)} %shard_map.63), channel_id=1, source_target_pairs={{0,64},{32,96},{64,0},{96,32},{1,65},{33,97},{65,1},{97,33},{2,66}... | collective-permute-start | bytes 6684680 | tf_op jit(solution)/shard_map/ppermute | solution.py:279
  79.1 1.0 all-to-all-done.3
  80.1 0.7 fusion.25
  81.0 0.5 collective-permute-start.6
  81.5 0.1 collective-permute-start.7
  81.7 5.5 %collective-permute-done.7.refs_10_ = f32[12,128,128]{2,1,0:T(8,128)} collective-permute-done((f32[12,128,128]{2,1,0:T(8,128)S(1)}, f32[12,128,128]{2,1,0:T(8,128)}, u32[]{:S(2)}, u32[]{:S(2)}) %collective-permute-start.7) | collective-permute-done | bytes 786464 | tf_op jit(solution)/shard_map/ppermute | solution.py:299
  87.1 0.1 collective-permute-start.8
  87.3 1.5 slice_reduce_fusion
  89.7 3.4 %copy-done = f32[128,16384]{1,0:T(8,128)S(1)} copy-done((f32[128,16384]{1,0:T(8,128)S(1)}, f32[128,16384]{1,0:T(8,128)}, u32[]{:S(2)}) %copy-start) | copy-done | bytes 8388632
  93.0 1.2 shard_map.58.refs_1_
  94.3 22.7 %shard_map.62 = (f32[4,4,8,16384]{3,2,1,0:T(8,128)S(1)}, f32[8,128]{1,0:T(8,128)S(1)}) custom-call(s32[240]{0:T(256)S(1)} %concatenate.31.refs_0_, f32[16,8,16384]{2,1,0:T(8,128)S(1)} %shard_map.58.refs_1_, f32[40,128,128]{2,1,0:T(8,128)} %get-tuple-element.58.refs_2_, f32[28,128,128]{2,1,0:T(8,128)} %shard_map.60.refs_3_, ...), custom_call_target="tpu_custom_call" | custom-call | bytes 1000 | tf_op jit(solution)/shard_map/pallas_call | solution.py:196
  117.0 10.4 %collective-permute-done.9.refs_0_ = f32[34,128,128]{2,1,0:T(8,128)S(1)} collective-permute-done((f32[34,128,128]{2,1,0:T(8,128)}, f32[34,128,128]{2,1,0:T(8,128)S(1)}, u32[]{:S(2)}, u32[]{:S(2)}) %collective-permute-start.9) | collective-permute-done | bytes 2228256 | tf_op jit(solution)/shard_map/ppermute | solution.py:279
  127.4 2.4 %collective-permute-start.11 = (f32[6,128,128]{2,1,0:T(8,128)S(1)}, f32[6,128,128]{2,1,0:T(8,128)S(1)}, u32[]{:S(2)}, u32[]{:S(2)}) collective-permute-start(f32[6,128,128]{2,1,0:T(8,128)S(1)} %get-tuple-element.68), channel_id=1, source_target_pairs={{0,64},{32,96},{64,0},{96,32},{1,65},{33,97},{65,1},{97,33},{2,66}... | collective-permute-start | bytes 1179656 | tf_op jit(solution)/shard_map/ppermute | solution.py:279
  129.9 1.8 collective-permute-done.10.refs_4_
  131.7 8.0 %shard_map.65 = (f32[4,4,8,16384]{3,2,1,0:T(8,128)S(1)}, f32[8,128]{1,0:T(8,128)S(1)}) custom-call(s32[68]{0:T(128)S(1)} %pad_add_fusion.2.refs_0_, f32[16,8,16384]{2,1,0:T(8,128)S(1)} %shard_map.58.refs_1_, f32[4,4,8,16384]{3,2,1,0:T(8,128)S(1)} %get-tuple-element.64.refs_2_, ...), custom_call_target="tpu_custom_call", output_to_operand_aliasing={{0}: (2, {})} | custom-call | bytes 1000 | tf_op jit(solution)/shard_map/pallas_call | solution.py:196
  139.7 0.7 collective-permute-done.11.refs_0_
  140.6 1.6 collective-permute-done.12.refs_4_
  142.2 4.4 %shard_map.67 = (f32[2,8,8192]{2,1,0:T(8,128)}, f32[2,8,8192]{2,1,0:T(8,128)}, f32[2,8,8192]{2,1,0:T(8,128)}, f32[2,8,8192]{2,1,0:T(8,128)}, f32[4,8,8192]{2,1,0...) custom-call(s32[12]{0:T(128)S(1)} %pad_add_fusion.1.refs_0_, ...), custom_call_target="tpu_custom_call" | custom-call | bytes 1000 | tf_op jit(solution)/shard_map/pallas_call | solution.py:196
  146.6 1.5 collective-permute-start.13
  148.1 1.8 collective-permute-start.15
  149.9 1.8 collective-permute-start.20
  151.8 2.1 collective-permute-start.22
  153.9 8.2 %collective-permute-done.13 = f32[2,8,8192]{2,1,0:T(8,128)S(1)} collective-permute-done((f32[2,8,8192]{2,1,0:T(8,128)}, f32[2,8,8192]{2,1,0:T(8,128)S(1)}, u32[]{:S(2)}, u32[]{:S(2)}) %collective-permute-start.13) | collective-permute-done | bytes 524320 | tf_op jit(solution)/shard_map/ppermute | solution.py:255
  162.1 1.3 slice_add_fusion.3
  163.5 0.3 collective-permute-start.14
  163.7 1.4 fusion.37
  165.2 3.1 %collective-permute-start.16 = (f32[4,8,8192]{2,1,0:T(8,128)S(1)}, f32[4,8,8192]{2,1,0:T(8,128)S(1)}, u32[]{:S(2)}, u32[]{:S(2)}) collective-permute-start(f32[4,8,8192]{2,1,0:T(8,128)S(1)} %pad_maximum_fusion.1), channel_id=1, source_target_pairs={{0,6},{1,7},{2,0},{3,1},{4,2},{5,3},{6,4},{7,5},{8,14},{9,15},{10,... | collective-permute-start | bytes 3145736 | tf_op jit(solution)/shard_map/ppermute | solution.py:265
  168.5 2.2 collective-permute-start.21
  170.9 2.2 %collective-permute-start.23 = (f32[4,8,8192]{2,1,0:T(8,128)S(1)}, f32[4,8,8192]{2,1,0:T(8,128)S(1)}, u32[]{:S(2)}, u32[]{:S(2)}) collective-permute-start(f32[4,8,8192]{2,1,0:T(8,128)S(1)} %pad_maximum_fusion.3), channel_id=1, source_target_pairs={{0,24},{1,25},{2,26},{3,27},{4,28},{5,29},{6,30},{7,31},{8,0},{9,1... | collective-permute-start | bytes 3145736 | tf_op jit(solution)/shard_map/ppermute | solution.py:266
  173.1 16.0 %collective-permute-done.14 = f32[4,8,8192]{2,1,0:T(8,128)S(1)} collective-permute-done((f32[4,8,8192]{2,1,0:T(8,128)S(1)}, f32[4,8,8192]{2,1,0:T(8,128)S(1)}, u32[]{:S(2)}, u32[]{:S(2)}) %collective-permute-start.14) | collective-permute-done | bytes 1048608 | tf_op jit(solution)/shard_map/ppermute | solution.py:265
  189.1 0.8 collective-permute-done.16
  189.9 0.1 fusion.20
  190.0 1.9 collective-permute-start.17
  191.9 2.2 %collective-permute-start.18 = (f32[8,8192]{1,0:T(8,128)S(1)}, f32[8,8192]{1,0:T(8,128)S(1)}, u32[]{:S(2)}, u32[]{:S(2)}) collective-permute-start(f32[8,8192]{1,0:T(8,128)S(1)} %get-tuple-element.83), channel_id=1, source_target_pairs={{0,24},{1,25},{2,26},{3,27},{4,28},{5,29},{6,30},{7,31},{8,0},{9,1... | collective-permute-start | bytes 786440 | tf_op jit(solution)/shard_map/ppermute | solution.py:269
  194.1 1.8 collective-permute-start.19
  195.9 0.8 collective-permute-done.21
  196.7 0.1 fusion.13
  196.8 0.3 collective-permute-start.24
  197.1 3.0 %collective-permute-start.25 = (f32[8,8192]{1,0:T(8,128)S(1)}, f32[8,8192]{1,0:T(8,128)S(1)}, u32[]{:S(2)}, u32[]{:S(2)}) collective-permute-start(f32[8,8192]{1,0:T(8,128)S(1)} %get-tuple-element.86), channel_id=1, source_target_pairs={{0,6},{1,7},{2,0},{3,1},{4,2},{5,3},{6,4},{7,5},{8,14},{9,15},{10,... | collective-permute-start | bytes 786440 | tf_op jit(solution)/shard_map/ppermute | solution.py:270
  200.1 1.0 collective-permute-done.17
  201.1 1.5 collective-permute-start.26
  202.6 3.1 %collective-permute-done.18 = f32[8,8192]{1,0:T(8,128)S(1)} collective-permute-done((f32[8,8192]{1,0:T(8,128)S(1)}, f32[8,8192]{1,0:T(8,128)S(1)}, u32[]{:S(2)}, u32[]{:S(2)}) %collective-permute-start.18) | collective-permute-done | bytes 262176 | tf_op jit(solution)/shard_map/ppermute | solution.py:269
  205.7 1.6 collective-permute-done.19
  207.4 1.7 collective-permute-done.25
  209.1 2.1 collective-permute-done.26
  211.4 0.2 conditional.1
  211.6 0.8 copy-done.5
  (70 shorter events, 1.5 us)
Async XLA Ops:
  6.5 83.1 %all-gather.3.cloned.1.call-start = ((), (), s32[]{:S(2)}) async-start(), calls=%async_computation.6 | async-start | bytes 8912896 | tf_op jit(solution)/shard_map/all_gather | solution.py:233
  7.3 10.5 %copy-start.4 = (f32[128,128,128]{2,1,0:T(8,128)S(1)}, f32[128,128,128]{2,1,0:T(8,128)}, u32[]{:S(2)}) copy-start(f32[128,128,128]{2,1,0:T(8,128)} %tiles.3) | copy-start | bytes 25165828
  14.4 66.4 %collective-permute-start = (f32[28,128,128]{2,1,0:T(8,128)}, f32[28,128,128]{2,1,0:T(8,128)}, u32[]{:S(2)}, u32[]{:S(2)}) collective-permute-start(f32[28,128,128]{2,1,0:T(8,128)} %get-tuple-element.55), channel_id=1, source_target_pairs={{0,32},{32,64},{64,96},{96,0},{1,33},{33,65},{65,97},{97,1},{2,34}... | collective-permute-start | bytes 5505032 | tf_op jit(solution)/shard_map/ppermute | solution.py:274
  16.2 64.8 %collective-permute-start.1 = (f32[28,128,128]{2,1,0:T(8,128)}, f32[28,128,128]{2,1,0:T(8,128)}, u32[]{:S(2)}, u32[]{:S(2)}) collective-permute-start(f32[28,128,128]{2,1,0:T(8,128)} %get-tuple-element.59), channel_id=1, source_target_pairs={{0,96},{32,0},{64,32},{96,64},{1,97},{33,1},{65,33},{97,65},{2,98}... | collective-permute-start | bytes 5505032 | tf_op jit(solution)/shard_map/ppermute | solution.py:274
  29.5 1.4 copy-start.3
  30.9 44.4 %collective-permute-start.2 = (f32[12,128,128]{2,1,0:T(8,128)S(1)}, f32[12,128,128]{2,1,0:T(8,128)S(1)}, u32[]{:S(2)}, u32[]{:S(2)}) collective-permute-start(f32[12,128,128]{2,1,0:T(8,128)S(1)} %get-tuple-element.60), channel_id=1, source_target_pairs={{0,32},{32,64},{64,96},{96,0},{1,33},{33,65},{65,97},{97,1},{2,34}... | collective-permute-start | bytes 2359304 | tf_op jit(solution)/shard_map/ppermute | solution.py:278
  31.3 44.0 %collective-permute-start.3 = (f32[12,128,128]{2,1,0:T(8,128)S(1)}, f32[12,128,128]{2,1,0:T(8,128)S(1)}, u32[]{:S(2)}, u32[]{:S(2)}) collective-permute-start(f32[12,128,128]{2,1,0:T(8,128)S(1)} %get-tuple-element.61), channel_id=1, source_target_pairs={{0,96},{32,0},{64,32},{96,64},{1,97},{33,1},{65,33},{97,65},{2,98}... | collective-permute-start | bytes 2359304 | tf_op jit(solution)/shard_map/ppermute | solution.py:278
  34.1 60.1 %collective-permute-start.4 = (f32[40,128,128]{2,1,0:T(8,128)}, f32[40,128,128]{2,1,0:T(8,128)}, u32[]{:S(2)}, u32[]{:S(2)}) collective-permute-start(f32[40,128,128]{2,1,0:T(8,128)} %get-tuple-element.58.refs_2_), channel_id=1, source_target_pairs={{0,1},{1,0},{2,3},{3,2},{4,5},{5,4},{6,7},{7,6},{8,9},{9,8},{10,11... | collective-permute-start | bytes 7864328 | tf_op jit(solution)/shard_map/ppermute | solution.py:299
  35.5 44.6 %all-to-all-start.3 = ((f32[128,1,41]{2,1,0:T(1,128)}), f32[128,1,41]{2,1,0:T(1,128)}, u32[]{:S(2)}, u32[]{:S(2)}) async-start(f32[128,1,41]{2,1,0:T(1,128)} %bitcast.120), calls=%async_computation.4 | async-start | bytes 131072 | tf_op jit(solution)/shard_map/all_to_all | solution.py:287
  75.3 0.9 copy-start.1
  76.2 51.2 %collective-permute-start.9 = (f32[34,128,128]{2,1,0:T(8,128)}, f32[34,128,128]{2,1,0:T(8,128)S(1)}, u32[]{:S(2)}, u32[]{:S(2)}) collective-permute-start(f32[34,128,128]{2,1,0:T(8,128)} %shard_map.63), channel_id=1, source_target_pairs={{0,64},{32,96},{64,0},{96,32},{1,65},{33,97},{65,1},{97,33},{2,66}... | collective-permute-start | bytes 6684680 | tf_op jit(solution)/shard_map/ppermute | solution.py:279
  80.9 13.4 %collective-permute-start.5 = (f32[28,128,128]{2,1,0:T(8,128)}, f32[28,128,128]{2,1,0:T(8,128)}, u32[]{:S(2)}, u32[]{:S(2)}) collective-permute-start(f32[28,128,128]{2,1,0:T(8,128)} %shard_map.60.refs_3_), channel_id=1, source_target_pairs={{0,1},{1,0},{2,3},{3,2},{4,5},{5,4},{6,7},{7,6},{8,9},{9,8},{10,11... | collective-permute-start | bytes 5505032 | tf_op jit(solution)/shard_map/ppermute | solution.py:299
  81.0 13.3 %collective-permute-start.6 = (f32[28,128,128]{2,1,0:T(8,128)}, f32[28,128,128]{2,1,0:T(8,128)}, u32[]{:S(2)}, u32[]{:S(2)}) collective-permute-start(f32[28,128,128]{2,1,0:T(8,128)} %shard_map.61.refs_4_), channel_id=1, source_target_pairs={{0,1},{1,0},{2,3},{3,2},{4,5},{5,4},{6,7},{7,6},{8,9},{9,8},{10,11... | collective-permute-start | bytes 5505032 | tf_op jit(solution)/shard_map/ppermute | solution.py:299
  81.5 5.7 %collective-permute-start.7 = (f32[12,128,128]{2,1,0:T(8,128)S(1)}, f32[12,128,128]{2,1,0:T(8,128)}, u32[]{:S(2)}, u32[]{:S(2)}) collective-permute-start(f32[12,128,128]{2,1,0:T(8,128)S(1)} %collective-permute-done.2.refs_5_.refs_1_), channel_id=1, source_target_pairs={{0,1},{1,0},{2,3},{3,2},{4,5},{5,4},{6,7},{7,6},{8,9},{9,8},{10,11... | collective-permute-start | bytes 2359304 | tf_op jit(solution)/shard_map/ppermute | solution.py:299
  87.1 7.1 %collective-permute-start.8 = (f32[12,128,128]{2,1,0:T(8,128)}, f32[12,128,128]{2,1,0:T(8,128)}, u32[]{:S(2)}, u32[]{:S(2)}) collective-permute-start(f32[12,128,128]{2,1,0:T(8,128)} %copy-done.1), channel_id=1, source_target_pairs={{0,1},{1,0},{2,3},{3,2},{4,5},{5,4},{6,7},{7,6},{8,9},{9,8},{10,11... | collective-permute-start | bytes 2359304 | tf_op jit(solution)/shard_map/ppermute | solution.py:299
  89.7 3.4 %copy-start = (f32[128,16384]{1,0:T(8,128)S(1)}, f32[128,16384]{1,0:T(8,128)}, u32[]{:S(2)}) copy-start(f32[128,16384]{1,0:T(8,128)} %all-gather.3.cloned.1.call-done) | copy-start | bytes 25165828
  93.0 1.2 copy-start.2
  127.4 4.3 %collective-permute-start.10 = (f32[34,128,128]{2,1,0:T(8,128)S(1)}, f32[34,128,128]{2,1,0:T(8,128)S(1)}, u32[]{:S(2)}, u32[]{:S(2)}) collective-permute-start(f32[34,128,128]{2,1,0:T(8,128)S(1)} %shard_map.64.refs_3_), channel_id=1, source_target_pairs={{0,1},{1,0},{2,3},{3,2},{4,5},{5,4},{6,7},{7,6},{8,9},{9,8},{10,11... | collective-permute-start | bytes 6684680 | tf_op jit(solution)/shard_map/ppermute | solution.py:299
  127.4 13.0 %collective-permute-start.11 = (f32[6,128,128]{2,1,0:T(8,128)S(1)}, f32[6,128,128]{2,1,0:T(8,128)S(1)}, u32[]{:S(2)}, u32[]{:S(2)}) collective-permute-start(f32[6,128,128]{2,1,0:T(8,128)S(1)} %get-tuple-element.68), channel_id=1, source_target_pairs={{0,64},{32,96},{64,0},{96,32},{1,65},{33,97},{65,1},{97,33},{2,66}... | collective-permute-start | bytes 1179656 | tf_op jit(solution)/shard_map/ppermute | solution.py:279
  140.4 1.7 collective-permute-start.12
  146.6 21.7 %copy-start.9 = (f32[4,8,8192]{2,1,0:T(8,128)S(1)}, f32[4,8,8192]{2,1,0:T(8,128)}, u32[]{:S(2)}) copy-start(f32[4,8,8192]{2,1,0:T(8,128)} %get-tuple-element.76) | copy-start | bytes 3145732
  146.6 24.1 %copy-start.8 = (f32[4,8,8192]{2,1,0:T(8,128)S(1)}, f32[4,8,8192]{2,1,0:T(8,128)}, u32[]{:S(2)}) copy-start(f32[4,8,8192]{2,1,0:T(8,128)} %get-tuple-element.78) | copy-start | bytes 3145732
  146.6 15.5 %collective-permute-start.13 = (f32[2,8,8192]{2,1,0:T(8,128)}, f32[2,8,8192]{2,1,0:T(8,128)S(1)}, u32[]{:S(2)}, u32[]{:S(2)}) collective-permute-start(f32[2,8,8192]{2,1,0:T(8,128)} %get-tuple-element.72), channel_id=1, source_target_pairs={{0,2},{1,3},{2,4},{3,5},{4,6},{5,7},{6,0},{7,1},{8,10},{9,11},{10,... | collective-permute-start | bytes 1572872 | tf_op jit(solution)/shard_map/ppermute | solution.py:255
  148.1 15.6 %collective-permute-start.15 = (f32[2,8,8192]{2,1,0:T(8,128)}, f32[2,8,8192]{2,1,0:T(8,128)S(1)}, u32[]{:S(2)}, u32[]{:S(2)}) collective-permute-start(f32[2,8,8192]{2,1,0:T(8,128)} %get-tuple-element.74), channel_id=1, source_target_pairs={{0,6},{1,7},{2,0},{3,1},{4,2},{5,3},{6,4},{7,5},{8,14},{9,15},{10,... | collective-permute-start | bytes 1572872 | tf_op jit(solution)/shard_map/ppermute | solution.py:255
  149.9 18.4 %collective-permute-start.20 = (f32[2,8,8192]{2,1,0:T(8,128)}, f32[2,8,8192]{2,1,0:T(8,128)S(1)}, u32[]{:S(2)}, u32[]{:S(2)}) collective-permute-start(f32[2,8,8192]{2,1,0:T(8,128)} %get-tuple-element.77), channel_id=1, source_target_pairs={{0,8},{1,9},{2,10},{3,11},{4,12},{5,13},{6,14},{7,15},{8,16},{9,17... | collective-permute-start | bytes 1572872 | tf_op jit(solution)/shard_map/ppermute | solution.py:256
  151.8 18.9 %collective-permute-start.22 = (f32[2,8,8192]{2,1,0:T(8,128)}, f32[2,8,8192]{2,1,0:T(8,128)S(1)}, u32[]{:S(2)}, u32[]{:S(2)}) collective-permute-start(f32[2,8,8192]{2,1,0:T(8,128)} %get-tuple-element.79), channel_id=1, source_target_pairs={{0,24},{1,25},{2,26},{3,27},{4,28},{5,29},{6,30},{7,31},{8,0},{9,1... | collective-permute-start | bytes 1572872 | tf_op jit(solution)/shard_map/ppermute | solution.py:256
  163.4 26.5 %copy-start.7 = (f32[4,8,8192]{2,1,0:T(8,128)S(1)}, f32[4,8,8192]{2,1,0:T(8,128)}, u32[]{:S(2)}) copy-start(f32[4,8,8192]{2,1,0:T(8,128)} %get-tuple-element.70) | copy-start | bytes 3145732
  163.5 25.7 %collective-permute-start.14 = (f32[4,8,8192]{2,1,0:T(8,128)S(1)}, f32[4,8,8192]{2,1,0:T(8,128)S(1)}, u32[]{:S(2)}, u32[]{:S(2)}) collective-permute-start(f32[4,8,8192]{2,1,0:T(8,128)S(1)} %pad_maximum_fusion), channel_id=1, source_target_pairs={{0,2},{1,3},{2,4},{3,5},{4,6},{5,7},{6,0},{7,1},{8,10},{9,11},{10,... | collective-permute-start | bytes 3145736 | tf_op jit(solution)/shard_map/ppermute | solution.py:265
  163.7 33.0 %copy-start.6 = (f32[4,8,8192]{2,1,0:T(8,128)S(1)}, f32[4,8,8192]{2,1,0:T(8,128)}, u32[]{:S(2)}) copy-start(f32[4,8,8192]{2,1,0:T(8,128)} %get-tuple-element.75) | copy-start | bytes 3145732
  165.2 24.7 %collective-permute-start.16 = (f32[4,8,8192]{2,1,0:T(8,128)S(1)}, f32[4,8,8192]{2,1,0:T(8,128)S(1)}, u32[]{:S(2)}, u32[]{:S(2)}) collective-permute-start(f32[4,8,8192]{2,1,0:T(8,128)S(1)} %pad_maximum_fusion.1), channel_id=1, source_target_pairs={{0,6},{1,7},{2,0},{3,1},{4,2},{5,3},{6,4},{7,5},{8,14},{9,15},{10,... | collective-permute-start | bytes 3145736 | tf_op jit(solution)/shard_map/ppermute | solution.py:265
  168.5 42.9 %copy-start.10 = (s32[128,1]{0,1:T(1,128)S(1)}, s32[128,1]{0,1:T(1,128)}, u32[]{:S(2)}) copy-start(s32[128,1]{0,1:T(1,128)} %param.9) | copy-start | bytes 1540
  168.5 42.9 %copy-start.11 = (s32[128]{0:T(128)S(1)}, s32[128]{0:T(128)}, u32[]{:S(2)}) copy-start(s32[128]{0:T(128)} %param.11) | copy-start | bytes 1540
  168.5 42.9 %copy-start.12 = (s32[128]{0:T(128)S(1)}, s32[128]{0:T(128)}, u32[]{:S(2)}) copy-start(s32[128]{0:T(128)} %param.10) | copy-start | bytes 1540
  168.5 28.2 %collective-permute-start.21 = (f32[4,8,8192]{2,1,0:T(8,128)S(1)}, f32[4,8,8192]{2,1,0:T(8,128)S(1)}, u32[]{:S(2)}, u32[]{:S(2)}) collective-permute-start(f32[4,8,8192]{2,1,0:T(8,128)S(1)} %pad_maximum_fusion.2), channel_id=1, source_target_pairs={{0,8},{1,9},{2,10},{3,11},{4,12},{5,13},{6,14},{7,15},{8,16},{9,17... | collective-permute-start | bytes 3145736 | tf_op jit(solution)/shard_map/ppermute | solution.py:266
  170.9 25.8 %collective-permute-start.23 = (f32[4,8,8192]{2,1,0:T(8,128)S(1)}, f32[4,8,8192]{2,1,0:T(8,128)S(1)}, u32[]{:S(2)}, u32[]{:S(2)}) collective-permute-start(f32[4,8,8192]{2,1,0:T(8,128)S(1)} %pad_maximum_fusion.3), channel_id=1, source_target_pairs={{0,24},{1,25},{2,26},{3,27},{4,28},{5,29},{6,30},{7,31},{8,0},{9,1... | collective-permute-start | bytes 3145736 | tf_op jit(solution)/shard_map/ppermute | solution.py:266
  190.0 11.1 %collective-permute-start.17 = (f32[8,8192]{1,0:T(8,128)S(1)}, f32[8,8192]{1,0:T(8,128)S(1)}, u32[]{:S(2)}, u32[]{:S(2)}) collective-permute-start(f32[8,8192]{1,0:T(8,128)S(1)} %get-tuple-element.81), channel_id=1, source_target_pairs={{0,8},{1,9},{2,10},{3,11},{4,12},{5,13},{6,14},{7,15},{8,16},{9,17... | collective-permute-start | bytes 786440 | tf_op jit(solution)/shard_map/ppermute | solution.py:269
  191.9 13.8 %collective-permute-start.18 = (f32[8,8192]{1,0:T(8,128)S(1)}, f32[8,8192]{1,0:T(8,128)S(1)}, u32[]{:S(2)}, u32[]{:S(2)}) collective-permute-start(f32[8,8192]{1,0:T(8,128)S(1)} %get-tuple-element.83), channel_id=1, source_target_pairs={{0,24},{1,25},{2,26},{3,27},{4,28},{5,29},{6,30},{7,31},{8,0},{9,1... | collective-permute-start | bytes 786440 | tf_op jit(solution)/shard_map/ppermute | solution.py:269
  194.1 13.2 %collective-permute-start.19 = (f32[8,8192]{1,0:T(8,128)S(1)}, f32[8,8192]{1,0:T(8,128)S(1)}, u32[]{:S(2)}, u32[]{:S(2)}) collective-permute-start(f32[8,8192]{1,0:T(8,128)S(1)} %get-tuple-element.82), channel_id=1, source_target_pairs={{0,16},{1,17},{2,18},{3,19},{4,20},{5,21},{6,22},{7,23},{8,24},{9,... | collective-permute-start | bytes 786440 | tf_op jit(solution)/shard_map/ppermute | solution.py:269
  196.8 10.6 %collective-permute-start.24 = (f32[8,8192]{1,0:T(8,128)S(1)}, f32[8,8192]{1,0:T(8,128)S(1)}, u32[]{:S(2)}, u32[]{:S(2)}) collective-permute-start(f32[8,8192]{1,0:T(8,128)S(1)} %get-tuple-element.84), channel_id=1, source_target_pairs={{0,2},{1,3},{2,4},{3,5},{4,6},{5,7},{6,0},{7,1},{8,10},{9,11},{10,... | collective-permute-start | bytes 786440 | tf_op jit(solution)/shard_map/ppermute | solution.py:270
  197.1 12.0 %collective-permute-start.25 = (f32[8,8192]{1,0:T(8,128)S(1)}, f32[8,8192]{1,0:T(8,128)S(1)}, u32[]{:S(2)}, u32[]{:S(2)}) collective-permute-start(f32[8,8192]{1,0:T(8,128)S(1)} %get-tuple-element.86), channel_id=1, source_target_pairs={{0,6},{1,7},{2,0},{3,1},{4,2},{5,3},{6,4},{7,5},{8,14},{9,15},{10,... | collective-permute-start | bytes 786440 | tf_op jit(solution)/shard_map/ppermute | solution.py:270
  201.1 10.1 %collective-permute-start.26 = (f32[8,8192]{1,0:T(8,128)S(1)}, f32[8,8192]{1,0:T(8,128)S(1)}, u32[]{:S(2)}, u32[]{:S(2)}) collective-permute-start(f32[8,8192]{1,0:T(8,128)S(1)} %get-tuple-element.85), channel_id=1, source_target_pairs={{0,4},{1,5},{2,6},{3,7},{4,0},{5,1},{6,2},{7,3},{8,12},{9,13},{10,... | collective-permute-start | bytes 786440 | tf_op jit(solution)/shard_map/ppermute | solution.py:270
  211.6 0.8 copy-start.5
Sparse Core Ops, SparseCore 0:
  9.5 73.9 all-gather.2

commit v6 on v5

--- a/solution.py
+++ b/solution.py
@@ -9,7 +9,7 @@
 
 TILE = 128
 SLOTS = 40
-FIRST = 34
+FIRST = 32
 EARLY = 28
 VMEM = 24 * 1024 * 1024
 AXES = ("grp", "inner")
@@ -144,11 +144,12 @@
     for k in range(lists):
         copies[k].wait()
         base = sum(counts[:k])
+        group = 4 if counts[k] % 4 == 0 else 2
 
         def pair(j, _):
-            places = [code[base + 2 * j], code[base + 2 * j + 1]]
-
-            @pl.when(jnp.maximum(*places) >= 0)
+            places = [code[base + group * j + i] for i in range(group)]
+
+            @pl.when(functools.reduce(jnp.maximum, places) >= 0)
             def _():
                 terms = []
                 for half, place in enumerate(places):
@@ -156,7 +157,7 @@
                     row = pl.multiple_of((held // blocks) * TILE, TILE)
                     col = pl.multiple_of(lax.rem(held, blocks) * TILE, TILE)
                     a_hi, a_lo = split(amp_v[:, :, pl.ds(row, TILE)].reshape(16 * 8, TILE))
-                    t_hi, t_lo = split(jnp.where(place >= 0, tile_v[k][2 * j + half], 0.0))
+                    t_hi, t_lo = split(jnp.where(place >= 0, tile_v[k][group * j + half], 0.0))
                     left = jnp.concatenate([a_hi, a_lo], axis=1)
                     right = jnp.concatenate([t_hi, t_lo], axis=1)
                     both = jnp.dot(left, jnp.concatenate([right, right], axis=0), preferred_element_type=jnp.float32)
@@ -166,7 +167,7 @@
 
             return 0
 
-        lax.fori_loop(0, counts[k] // 2, pair, 0)
+        lax.fori_loop(0, counts[k] // group, pair, 0)
 
     if last:
         half = blocks * TILE // 2

time: 220 us -> 227 us (1.032)
  waiting for transfers between devices: 87.4 us -> 111 us
  Pallas kernels: 52.5 us -> 43.8 us
  starting transfers between devices: 47.7 us -> 40.6 us
    all_to_all x1, waiting for transfers between devices: 1 us -> 34.9 us  [per_device(): lax.all_to_all(note.reshape(devices, total + 1), AXES, split_axis=0, conc...]
    ppermute x1, waiting for transfers between devices: 30.2 us -> 0.01 us  [per_device(): lax.ppermute(p5, 'grp', along_y[1])]
    pallas_call x3, Pallas kernels: 35.1 us -> 26.4 us  [ladder(): pl.pallas_call(functools.partial(ladder_kernel, counts, blocks, acc is No...]
    ppermute x1, waiting for transfers between devices: 10.4 us -> 17.9 us  [per_device(): lax.ppermute(gate(pltpu.with_memory_space_constraint(p2, pltpu.HBM), r5,...]
    ppermute x1, waiting for transfers between devices: 0.7 us -> 6.41 us  [per_device(): lax.ppermute(p4, 'grp', along_y[2])]
    ppermute x3, waiting for transfers between devices: 3.84 us -> 7.07 us  [finish(): f2 = [lax.ppermute(s2[s], 'inner', along_x[s]) for s in (1, 3, 2)]]
    ppermute x3, starting transfers between devices: 5.87 us -> 3.36 us  [finish(): f1 = [lax.ppermute(s1[s], 'inner', along_z[s]) for s in (1, 3, 2)]]
    unnamed x26 -> x30, local copies, waits for them, and re-layouts: 6.43 us -> 7.19 us
  transfers between devices with their start and end apart: 29 -> 29, of which waited for: 17 -> 12; matrix products, arithmetic and copies ran while one was open for 5% -> 4% of each run, Pallas kernels for 22% -> 17%
where the time goes in v6:
time: 227 us; the launch traced here: 226 us
  waiting for transfers between devices  111 us (49%)
  Pallas kernels  43.8 us (19%)
  starting transfers between devices  40.6 us (18%)
  between operations  14.6 us (6%)
  other arithmetic  8.32 us (4%)
  local copies, waits for them, and re-layouts  7.54 us (3%)
    all_to_all x1, waiting for transfers between devices, per_device(): lax.all_to_all(note.reshape(devices, total + 1), AXES, split_axis=0, conc...  34.9 us
    pallas_call x3, Pallas kernels, ladder(): pl.pallas_call(functools.partial(ladder_kernel, counts, blocks, acc is No...  26.4 us
    ppermute x2, waiting for transfers between devices, finish(): lax.ppermute(x_up, 'inner', along_x[1])  25.7 us
    ppermute x1, waiting for transfers between devices, per_device(): lax.ppermute(gate(pltpu.with_memory_space_constraint(p2, pltpu.HBM), r5,...  17.9 us
    pallas_call x2, Pallas kernels, pack(): pl.pallas_call(functools.partial(pack_kernel, spans, total), out_shape=[j...  16.2 us
    ppermute x7, waiting for transfers between devices, with_other(): return [*tiles, *[lax.ppermute(t, 'inner', across) for t in tiles]]  9.53 us
    all_to_all x1, starting transfers between devices, per_device(): lax.all_to_all(note.reshape(devices, total + 1), AXES, split_axis=0, conc...  8.83 us
    unnamed x30, local copies, waits for them, and re-layouts  7.19 us
  transfers between devices with their start and end apart: 29, of which 12 were waited for; matrix products, arithmetic and copies ran while one was open for 4% of the time, Pallas kernels for 17%

profile of v6, /device:TPU:0, one launch (start us, length us, event | category | flops | bytes accessed | tf_op | source)
XLA Modules:
  0.0 226.4 jit_solution(15286314949234797783)
XLA Ops:
  6.5 0.7 all-gather.3.cloned.1.call-update
  7.3 0.8 fusion.36
  8.1 0.8 and_select_fusion.2
  8.9 0.2 convert_reduce_fusion.2
  9.1 0.6 fusion.33
  9.7 0.1 select_reduce_fusion
  9.9 4.5 %shard_map.57 = (f32[28,128,128]{2,1,0:T(8,128)}, f32[28,128,128]{2,1,0:T(8,128)}) custom-call(s32[160]{0:T(256)S(1)} %get-tuple-element.57.index, f32[128,128,128]{2,1,0:T(8,128)} %tiles.3), custom_call_target="tpu_custom_call" | custom-call | bytes 1000 | tf_op jit(solution)/shard_map/pallas_call | solution.py:61
  14.3 1.7 collective-permute-start
  16.1 1.6 collective-permute-start.1
  17.7 11.8 %shard_map.59 = (f32[12,128,128]{2,1,0:T(8,128)S(1)}, f32[12,128,128]{2,1,0:T(8,128)S(1)}, f32[32,128,128]{2,1,0:T(8,128)S(1)}, f32[8,128,128]{2,1,0:T(8,128)S(1)}, f32[40,128,128]{2,1,0:T(8,128)}) custom-call(s32[160]{0:T(256)S(1)} %get-tuple-element.57.index, f32[128,128,128]{2,1,0:T(8,128)S(1)} %copy-done.6), custom_call_target="tpu_custom_call" | custom-call | bytes 1000 | tf_op jit(solution)/shard_map/pallas_call | solution.py:61
  29.5 1.3 copy-done.3
  30.8 0.8 copy-done.4
  31.6 0.4 collective-permute-start.2
  32.0 2.8 %collective-permute-start.3 = (f32[12,128,128]{2,1,0:T(8,128)S(1)}, f32[12,128,128]{2,1,0:T(8,128)S(1)}, u32[]{:S(2)}, u32[]{:S(2)}) collective-permute-start(f32[12,128,128]{2,1,0:T(8,128)S(1)} %get-tuple-element.61), channel_id=1, source_target_pairs={{0,96},{32,0},{64,32},{96,64},{1,97},{33,1},{65,33},{97,65},{2,98}... | collective-permute-start | bytes 2359304 | tf_op jit(solution)/shard_map/ppermute | solution.py:279
  34.8 0.1 broadcast_in_dim.59
  34.9 1.2 pad_convert_fusion
  36.1 8.8 %all-to-all-start.3 = ((f32[128,1,41]{2,1,0:T(1,128)}), f32[128,1,41]{2,1,0:T(1,128)S(1)}, u32[]{:S(2)}, u32[]{:S(2)}) async-start(f32[128,1,41]{2,1,0:T(1,128)} %bitcast.13), calls=%async_computation.4 | async-start | bytes 131072 | tf_op jit(solution)/shard_map/all_to_all | solution.py:288
  45.0 34.9 %all-to-all-done.3 = f32[128,1,41]{2,1,0:T(1,128)S(1)} async-done(((f32[128,1,41]{2,1,0:T(1,128)}), f32[128,1,41]{2,1,0:T(1,128)S(1)}, u32[]{:S(2)}, u32[]{:S(2)}) %all-to-all-start.3) | async-done | bytes 21024 | tf_op jit(solution)/shard_map/all_to_all | solution.py:288
  79.9 0.9 copy-done.1
  80.8 1.7 collective-permute-start.9
  82.6 0.1 collective-permute-start.5
  82.7 0.5 collective-permute-start.6
  83.2 0.1 collective-permute-start.7
  83.4 5.5 %collective-permute-done.7.refs_10_ = f32[12,128,128]{2,1,0:T(8,128)} collective-permute-done((f32[12,128,128]{2,1,0:T(8,128)S(1)}, f32[12,128,128]{2,1,0:T(8,128)}, u32[]{:S(2)}, u32[]{:S(2)}) %collective-permute-start.7) | collective-permute-done | bytes 786464 | tf_op jit(solution)/shard_map/ppermute | solution.py:300
  88.8 0.1 collective-permute-start.8
  89.0 0.8 slice_reduce_fusion
  90.5 0.1 concatenate.31.refs_0_
  90.6 3.4 %copy-done = f32[128,16384]{1,0:T(8,128)S(1)} copy-done((f32[128,16384]{1,0:T(8,128)S(1)}, f32[128,16384]{1,0:T(8,128)}, u32[]{:S(2)}) %copy-start) | copy-done | bytes 8388632
  94.0 1.2 shard_map.58.refs_1_
  95.3 16.8 %shard_map.62 = (f32[4,4,8,16384]{3,2,1,0:T(8,128)S(1)}, f32[8,128]{1,0:T(8,128)S(1)}) custom-call(s32[240]{0:T(256)S(1)} %concatenate.31.refs_0_, f32[16,8,16384]{2,1,0:T(8,128)S(1)} %shard_map.58.refs_1_, f32[40,128,128]{2,1,0:T(8,128)} %get-tuple-element.58.refs_2_, f32[28,128,128]{2,1,0:T(8,128)} %shard_map.60.refs_3_, ...), custom_call_target="tpu_custom_call" | custom-call | bytes 1000 | tf_op jit(solution)/shard_map/pallas_call | solution.py:197
  112.0 17.9 %collective-permute-done.9.refs_0_ = f32[32,128,128]{2,1,0:T(8,128)S(1)} collective-permute-done((f32[32,128,128]{2,1,0:T(8,128)}, f32[32,128,128]{2,1,0:T(8,128)S(1)}, u32[]{:S(2)}, u32[]{:S(2)}) %collective-permute-start.9) | collective-permute-done | bytes 2097184 | tf_op jit(solution)/shard_map/ppermute | solution.py:280
  129.9 1.8 collective-permute-start.11
  131.7 0.1 pad_add_fusion.2.refs_0_
  131.8 2.3 %collective-permute-done.10.refs_4_ = f32[32,128,128]{2,1,0:T(8,128)S(1)} collective-permute-done((f32[32,128,128]{2,1,0:T(8,128)S(1)}, f32[32,128,128]{2,1,0:T(8,128)S(1)}, u32[]{:S(2)}, u32[]{:S(2)}) %collective-permute-start.10) | collective-permute-done | bytes 2097184 | tf_op jit(solution)/shard_map/ppermute | solution.py:300
  134.1 5.3 %shard_map.65 = (f32[4,4,8,16384]{3,2,1,0:T(8,128)S(1)}, f32[8,128]{1,0:T(8,128)S(1)}) custom-call(s32[64]{0:T(128)S(1)} %pad_add_fusion.2.refs_0_, f32[16,8,16384]{2,1,0:T(8,128)S(1)} %shard_map.58.refs_1_, f32[4,4,8,16384]{3,2,1,0:T(8,128)S(1)} %get-tuple-element.64.refs_2_, ...), custom_call_target="tpu_custom_call", output_to_operand_aliasing={{0}: (2, {})} | custom-call | bytes 1000 | tf_op jit(solution)/shard_map/pallas_call | solution.py:197
  139.3 6.4 %collective-permute-done.11.refs_0_ = f32[8,128,128]{2,1,0:T(8,128)S(1)} collective-permute-done((f32[8,128,128]{2,1,0:T(8,128)S(1)}, f32[8,128,128]{2,1,0:T(8,128)S(1)}, u32[]{:S(2)}, u32[]{:S(2)}) %collective-permute-start.11) | collective-permute-done | bytes 524320 | tf_op jit(solution)/shard_map/ppermute | solution.py:280
  145.9 1.8 collective-permute-done.12.refs_4_
  147.7 4.4 %shard_map.67 = (f32[2,8,8192]{2,1,0:T(8,128)}, f32[2,8,8192]{2,1,0:T(8,128)}, f32[2,8,8192]{2,1,0:T(8,128)}, f32[2,8,8192]{2,1,0:T(8,128)}, f32[4,8,8192]{2,1,0...) custom-call(s32[16]{0:T(128)S(1)} %pad_add_fusion.1.refs_0_, ...), custom_call_target="tpu_custom_call" | custom-call | bytes 1000 | tf_op jit(solution)/shard_map/pallas_call | solution.py:197
  152.0 1.6 collective-permute-start.13
  153.6 1.7 collective-permute-start.15
  155.3 0.9 collective-permute-start.20
  156.3 2.3 %collective-permute-start.22 = (f32[2,8,8192]{2,1,0:T(8,128)}, f32[2,8,8192]{2,1,0:T(8,128)S(1)}, u32[]{:S(2)}, u32[]{:S(2)}) collective-permute-start(f32[2,8,8192]{2,1,0:T(8,128)} %get-tuple-element.79), channel_id=1, source_target_pairs={{0,24},{1,25},{2,26},{3,27},{4,28},{5,29},{6,30},{7,31},{8,0},{9,1... | collective-permute-start | bytes 1572872 | tf_op jit(solution)/shard_map/ppermute | solution.py:257
  158.6 8.9 %collective-permute-done.13 = f32[2,8,8192]{2,1,0:T(8,128)S(1)} collective-permute-done((f32[2,8,8192]{2,1,0:T(8,128)}, f32[2,8,8192]{2,1,0:T(8,128)S(1)}, u32[]{:S(2)}, u32[]{:S(2)}) %collective-permute-start.13) | collective-permute-done | bytes 524320 | tf_op jit(solution)/shard_map/ppermute | solution.py:256
  167.5 1.3 slice_add_fusion.3
  168.9 0.4 collective-permute-start.14
  169.2 1.4 fusion.37
  170.7 3.3 %collective-permute-start.16 = (f32[4,8,8192]{2,1,0:T(8,128)S(1)}, f32[4,8,8192]{2,1,0:T(8,128)S(1)}, u32[]{:S(2)}, u32[]{:S(2)}) collective-permute-start(f32[4,8,8192]{2,1,0:T(8,128)S(1)} %pad_maximum_fusion.1), channel_id=1, source_target_pairs={{0,6},{1,7},{2,0},{3,1},{4,2},{5,3},{6,4},{7,5},{8,14},{9,15},{10,... | collective-permute-start | bytes 3145736 | tf_op jit(solution)/shard_map/ppermute | solution.py:266
  174.0 0.1 slice_add_fusion.1
  174.2 1.0 collective-permute-start.21
  175.2 0.1 fusion.38
  175.4 2.4 %collective-permute-start.23 = (f32[4,8,8192]{2,1,0:T(8,128)S(1)}, f32[4,8,8192]{2,1,0:T(8,128)S(1)}, u32[]{:S(2)}, u32[]{:S(2)}) collective-permute-start(f32[4,8,8192]{2,1,0:T(8,128)S(1)} %pad_maximum_fusion.3), channel_id=1, source_target_pairs={{0,24},{1,25},{2,26},{3,27},{4,28},{5,29},{6,30},{7,31},{8,0},{9,1... | collective-permute-start | bytes 3145736 | tf_op jit(solution)/shard_map/ppermute | solution.py:267
  177.7 16.8 %collective-permute-done.14 = f32[4,8,8192]{2,1,0:T(8,128)S(1)} collective-permute-done((f32[4,8,8192]{2,1,0:T(8,128)S(1)}, f32[4,8,8192]{2,1,0:T(8,128)S(1)}, u32[]{:S(2)}, u32[]{:S(2)}) %collective-permute-start.14) | collective-permute-done | bytes 1048608 | tf_op jit(solution)/shard_map/ppermute | solution.py:266
  194.5 1.1 collective-permute-done.16
  195.6 0.1 fusion.20
  195.7 1.0 collective-permute-start.17
  196.7 2.3 %collective-permute-start.18 = (f32[8,8192]{1,0:T(8,128)S(1)}, f32[8,8192]{1,0:T(8,128)S(1)}, u32[]{:S(2)}, u32[]{:S(2)}) collective-permute-start(f32[8,8192]{1,0:T(8,128)S(1)} %get-tuple-element.83), channel_id=1, source_target_pairs={{0,24},{1,25},{2,26},{3,27},{4,28},{5,29},{6,30},{7,31},{8,0},{9,1... | collective-permute-start | bytes 786440 | tf_op jit(solution)/shard_map/ppermute | solution.py:270
  199.1 1.7 collective-permute-done.21
  200.8 0.1 fusion.13
  201.0 3.2 %collective-permute-start.25 = (f32[8,8192]{1,0:T(8,128)S(1)}, f32[8,8192]{1,0:T(8,128)S(1)}, u32[]{:S(2)}, u32[]{:S(2)}) collective-permute-start(f32[8,8192]{1,0:T(8,128)S(1)} %get-tuple-element.86), channel_id=1, source_target_pairs={{0,6},{1,7},{2,0},{3,1},{4,2},{5,3},{6,4},{7,5},{8,14},{9,15},{10,... | collective-permute-start | bytes 786440 | tf_op jit(solution)/shard_map/ppermute | solution.py:271
  204.2 6.3 %collective-permute-done.17 = f32[8,8192]{1,0:T(8,128)S(1)} collective-permute-done((f32[8,8192]{1,0:T(8,128)S(1)}, f32[8,8192]{1,0:T(8,128)S(1)}, u32[]{:S(2)}, u32[]{:S(2)}) %collective-permute-start.17) | collective-permute-done | bytes 262176 | tf_op jit(solution)/shard_map/ppermute | solution.py:270
  210.5 0.7 collective-permute-start.26
  211.3 7.1 %collective-permute-done.26 = f32[8,8192]{1,0:T(8,128)S(1)} collective-permute-done((f32[8,8192]{1,0:T(8,128)S(1)}, f32[8,8192]{1,0:T(8,128)S(1)}, u32[]{:S(2)}, u32[]{:S(2)}) %collective-permute-start.26) | collective-permute-done | bytes 262176 | tf_op jit(solution)/shard_map/ppermute | solution.py:271
  218.6 0.2 conditional.1
  218.8 0.8 copy-done.7
  (74 shorter events, 1.1 us)
Async XLA Ops:
  6.5 84.1 %all-gather.3.cloned.1.call-start = ((), (), s32[]{:S(2)}) async-start(), calls=%async_computation.6 | async-start | bytes 8912896 | tf_op jit(solution)/shard_map/all_gather | solution.py:234
  7.3 10.4 %copy-start.6 = (f32[128,128,128]{2,1,0:T(8,128)S(1)}, f32[128,128,128]{2,1,0:T(8,128)}, u32[]{:S(2)}) copy-start(f32[128,128,128]{2,1,0:T(8,128)} %tiles.3) | copy-start | bytes 25165828
  14.3 68.2 %collective-permute-start = (f32[28,128,128]{2,1,0:T(8,128)}, f32[28,128,128]{2,1,0:T(8,128)}, u32[]{:S(2)}, u32[]{:S(2)}) collective-permute-start(f32[28,128,128]{2,1,0:T(8,128)} %get-tuple-element.55), channel_id=1, source_target_pairs={{0,32},{32,64},{64,96},{96,0},{1,33},{33,65},{65,97},{97,1},{2,34}... | collective-permute-start | bytes 5505032 | tf_op jit(solution)/shard_map/ppermute | solution.py:275
  16.1 66.6 %collective-permute-start.1 = (f32[28,128,128]{2,1,0:T(8,128)}, f32[28,128,128]{2,1,0:T(8,128)}, u32[]{:S(2)}, u32[]{:S(2)}) collective-permute-start(f32[28,128,128]{2,1,0:T(8,128)} %get-tuple-element.59), channel_id=1, source_target_pairs={{0,96},{32,0},{64,32},{96,64},{1,97},{33,1},{65,33},{97,65},{2,98}... | collective-permute-start | bytes 5505032 | tf_op jit(solution)/shard_map/ppermute | solution.py:275
  29.4 1.3 copy-start.3
  30.8 0.8 copy-start.4
  31.6 48.4 %collective-permute-start.2 = (f32[12,128,128]{2,1,0:T(8,128)S(1)}, f32[12,128,128]{2,1,0:T(8,128)S(1)}, u32[]{:S(2)}, u32[]{:S(2)}) collective-permute-start(f32[12,128,128]{2,1,0:T(8,128)S(1)} %get-tuple-element.60), channel_id=1, source_target_pairs={{0,32},{32,64},{64,96},{96,0},{1,33},{33,65},{65,97},{97,1},{2,34}... | collective-permute-start | bytes 2359304 | tf_op jit(solution)/shard_map/ppermute | solution.py:279
  32.0 47.9 %collective-permute-start.3 = (f32[12,128,128]{2,1,0:T(8,128)S(1)}, f32[12,128,128]{2,1,0:T(8,128)S(1)}, u32[]{:S(2)}, u32[]{:S(2)}) collective-permute-start(f32[12,128,128]{2,1,0:T(8,128)S(1)} %get-tuple-element.61), channel_id=1, source_target_pairs={{0,96},{32,0},{64,32},{96,64},{1,97},{33,1},{65,33},{97,65},{2,98}... | collective-permute-start | bytes 2359304 | tf_op jit(solution)/shard_map/ppermute | solution.py:279
  34.8 60.4 %collective-permute-start.4 = (f32[40,128,128]{2,1,0:T(8,128)}, f32[40,128,128]{2,1,0:T(8,128)}, u32[]{:S(2)}, u32[]{:S(2)}) collective-permute-start(f32[40,128,128]{2,1,0:T(8,128)} %get-tuple-element.58.refs_2_), channel_id=1, source_target_pairs={{0,1},{1,0},{2,3},{3,2},{4,5},{5,4},{6,7},{7,6},{8,9},{9,8},{10,11... | collective-permute-start | bytes 7864328 | tf_op jit(solution)/shard_map/ppermute | solution.py:300
  36.1 43.8 %all-to-all-start.3 = ((f32[128,1,41]{2,1,0:T(1,128)}), f32[128,1,41]{2,1,0:T(1,128)S(1)}, u32[]{:S(2)}, u32[]{:S(2)}) async-start(f32[128,1,41]{2,1,0:T(1,128)} %bitcast.13), calls=%async_computation.4 | async-start | bytes 131072 | tf_op jit(solution)/shard_map/all_to_all | solution.py:288
  79.9 0.9 copy-start.1
  80.8 49.1 %collective-permute-start.9 = (f32[32,128,128]{2,1,0:T(8,128)}, f32[32,128,128]{2,1,0:T(8,128)S(1)}, u32[]{:S(2)}, u32[]{:S(2)}) collective-permute-start(f32[32,128,128]{2,1,0:T(8,128)} %shard_map.63), channel_id=1, source_target_pairs={{0,64},{32,96},{64,0},{96,32},{1,65},{33,97},{65,1},{97,33},{2,66}... | collective-permute-start | bytes 6291464 | tf_op jit(solution)/shard_map/ppermute | solution.py:280
  82.6 12.6 %collective-permute-start.5 = (f32[28,128,128]{2,1,0:T(8,128)}, f32[28,128,128]{2,1,0:T(8,128)}, u32[]{:S(2)}, u32[]{:S(2)}) collective-permute-start(f32[28,128,128]{2,1,0:T(8,128)} %shard_map.60.refs_3_), channel_id=1, source_target_pairs={{0,1},{1,0},{2,3},{3,2},{4,5},{5,4},{6,7},{7,6},{8,9},{9,8},{10,11... | collective-permute-start | bytes 5505032 | tf_op jit(solution)/shard_map/ppermute | solution.py:300
  82.7 12.5 %collective-permute-start.6 = (f32[28,128,128]{2,1,0:T(8,128)}, f32[28,128,128]{2,1,0:T(8,128)}, u32[]{:S(2)}, u32[]{:S(2)}) collective-permute-start(f32[28,128,128]{2,1,0:T(8,128)} %shard_map.61.refs_4_), channel_id=1, source_target_pairs={{0,1},{1,0},{2,3},{3,2},{4,5},{5,4},{6,7},{7,6},{8,9},{9,8},{10,11... | collective-permute-start | bytes 5505032 | tf_op jit(solution)/shard_map/ppermute | solution.py:300
  83.2 5.7 %collective-permute-start.7 = (f32[12,128,128]{2,1,0:T(8,128)S(1)}, f32[12,128,128]{2,1,0:T(8,128)}, u32[]{:S(2)}, u32[]{:S(2)}) collective-permute-start(f32[12,128,128]{2,1,0:T(8,128)S(1)} %collective-permute-done.2.refs_5_.refs_1_), channel_id=1, source_target_pairs={{0,1},{1,0},{2,3},{3,2},{4,5},{5,4},{6,7},{7,6},{8,9},{9,8},{10,11... | collective-permute-start | bytes 2359304 | tf_op jit(solution)/shard_map/ppermute | solution.py:300
  88.8 6.4 %collective-permute-start.8 = (f32[12,128,128]{2,1,0:T(8,128)}, f32[12,128,128]{2,1,0:T(8,128)}, u32[]{:S(2)}, u32[]{:S(2)}) collective-permute-start(f32[12,128,128]{2,1,0:T(8,128)} %copy-done.1), channel_id=1, source_target_pairs={{0,1},{1,0},{2,3},{3,2},{4,5},{5,4},{6,7},{7,6},{8,9},{9,8},{10,11... | collective-permute-start | bytes 2359304 | tf_op jit(solution)/shard_map/ppermute | solution.py:300
  90.6 3.4 %copy-start = (f32[128,16384]{1,0:T(8,128)S(1)}, f32[128,16384]{1,0:T(8,128)}, u32[]{:S(2)}) copy-start(f32[128,16384]{1,0:T(8,128)} %all-gather.3.cloned.1.call-done) | copy-start | bytes 25165828
  94.0 1.2 copy-start.2
  95.2 34.7 %copy-start.5 = (f32[8,128,128]{2,1,0:T(8,128)S(1)}, f32[8,128,128]{2,1,0:T(8,128)}, u32[]{:S(2)}) copy-start(f32[8,128,128]{2,1,0:T(8,128)} %copy-done.4) | copy-start | bytes 1572868
  129.9 4.2 %collective-permute-start.10 = (f32[32,128,128]{2,1,0:T(8,128)S(1)}, f32[32,128,128]{2,1,0:T(8,128)S(1)}, u32[]{:S(2)}, u32[]{:S(2)}) collective-permute-start(f32[32,128,128]{2,1,0:T(8,128)S(1)} %shard_map.64.refs_3_), channel_id=1, source_target_pairs={{0,1},{1,0},{2,3},{3,2},{4,5},{5,4},{6,7},{7,6},{8,9},{9,8},{10,11... | collective-permute-start | bytes 6291464 | tf_op jit(solution)/shard_map/ppermute | solution.py:300
  129.9 15.8 %collective-permute-start.11 = (f32[8,128,128]{2,1,0:T(8,128)S(1)}, f32[8,128,128]{2,1,0:T(8,128)S(1)}, u32[]{:S(2)}, u32[]{:S(2)}) collective-permute-start(f32[8,128,128]{2,1,0:T(8,128)S(1)} %copy-done.5), channel_id=1, source_target_pairs={{0,64},{32,96},{64,0},{96,32},{1,65},{33,97},{65,1},{97,33},{2,66}... | collective-permute-start | bytes 1572872 | tf_op jit(solution)/shard_map/ppermute | solution.py:280
  145.7 1.9 collective-permute-start.12
  152.0 22.0 %copy-start.11 = (f32[4,8,8192]{2,1,0:T(8,128)S(1)}, f32[4,8,8192]{2,1,0:T(8,128)}, u32[]{:S(2)}) copy-start(f32[4,8,8192]{2,1,0:T(8,128)} %get-tuple-element.76) | copy-start | bytes 3145732
  152.0 23.2 %copy-start.10 = (f32[4,8,8192]{2,1,0:T(8,128)S(1)}, f32[4,8,8192]{2,1,0:T(8,128)}, u32[]{:S(2)}) copy-start(f32[4,8,8192]{2,1,0:T(8,128)} %get-tuple-element.78) | copy-start | bytes 3145732
  152.0 15.5 %collective-permute-start.13 = (f32[2,8,8192]{2,1,0:T(8,128)}, f32[2,8,8192]{2,1,0:T(8,128)S(1)}, u32[]{:S(2)}, u32[]{:S(2)}) collective-permute-start(f32[2,8,8192]{2,1,0:T(8,128)} %get-tuple-element.72), channel_id=1, source_target_pairs={{0,2},{1,3},{2,4},{3,5},{4,6},{5,7},{6,0},{7,1},{8,10},{9,11},{10,... | collective-permute-start | bytes 1572872 | tf_op jit(solution)/shard_map/ppermute | solution.py:256
  153.6 15.6 %collective-permute-start.15 = (f32[2,8,8192]{2,1,0:T(8,128)}, f32[2,8,8192]{2,1,0:T(8,128)S(1)}, u32[]{:S(2)}, u32[]{:S(2)}) collective-permute-start(f32[2,8,8192]{2,1,0:T(8,128)} %get-tuple-element.74), channel_id=1, source_target_pairs={{0,6},{1,7},{2,0},{3,1},{4,2},{5,3},{6,4},{7,5},{8,14},{9,15},{10,... | collective-permute-start | bytes 1572872 | tf_op jit(solution)/shard_map/ppermute | solution.py:256
  155.3 18.6 %collective-permute-start.20 = (f32[2,8,8192]{2,1,0:T(8,128)}, f32[2,8,8192]{2,1,0:T(8,128)S(1)}, u32[]{:S(2)}, u32[]{:S(2)}) collective-permute-start(f32[2,8,8192]{2,1,0:T(8,128)} %get-tuple-element.77), channel_id=1, source_target_pairs={{0,8},{1,9},{2,10},{3,11},{4,12},{5,13},{6,14},{7,15},{8,16},{9,17... | collective-permute-start | bytes 1572872 | tf_op jit(solution)/shard_map/ppermute | solution.py:257
  156.3 18.9 %collective-permute-start.22 = (f32[2,8,8192]{2,1,0:T(8,128)}, f32[2,8,8192]{2,1,0:T(8,128)S(1)}, u32[]{:S(2)}, u32[]{:S(2)}) collective-permute-start(f32[2,8,8192]{2,1,0:T(8,128)} %get-tuple-element.79), channel_id=1, source_target_pairs={{0,24},{1,25},{2,26},{3,27},{4,28},{5,29},{6,30},{7,31},{8,0},{9,1... | collective-permute-start | bytes 1572872 | tf_op jit(solution)/shard_map/ppermute | solution.py:257
  168.8 26.8 %copy-start.9 = (f32[4,8,8192]{2,1,0:T(8,128)S(1)}, f32[4,8,8192]{2,1,0:T(8,128)}, u32[]{:S(2)}) copy-start(f32[4,8,8192]{2,1,0:T(8,128)} %get-tuple-element.70) | copy-start | bytes 3145732
  168.9 25.7 %collective-permute-start.14 = (f32[4,8,8192]{2,1,0:T(8,128)S(1)}, f32[4,8,8192]{2,1,0:T(8,128)S(1)}, u32[]{:S(2)}, u32[]{:S(2)}) collective-permute-start(f32[4,8,8192]{2,1,0:T(8,128)S(1)} %pad_maximum_fusion), channel_id=1, source_target_pairs={{0,2},{1,3},{2,4},{3,5},{4,6},{5,7},{6,0},{7,1},{8,10},{9,11},{10,... | collective-permute-start | bytes 3145736 | tf_op jit(solution)/shard_map/ppermute | solution.py:266
  169.2 31.6 %copy-start.8 = (f32[4,8,8192]{2,1,0:T(8,128)S(1)}, f32[4,8,8192]{2,1,0:T(8,128)}, u32[]{:S(2)}) copy-start(f32[4,8,8192]{2,1,0:T(8,128)} %get-tuple-element.75) | copy-start | bytes 3145732
  170.7 24.9 %collective-permute-start.16 = (f32[4,8,8192]{2,1,0:T(8,128)S(1)}, f32[4,8,8192]{2,1,0:T(8,128)S(1)}, u32[]{:S(2)}, u32[]{:S(2)}) collective-permute-start(f32[4,8,8192]{2,1,0:T(8,128)S(1)} %pad_maximum_fusion.1), channel_id=1, source_target_pairs={{0,6},{1,7},{2,0},{3,1},{4,2},{5,3},{6,4},{7,5},{8,14},{9,15},{10,... | collective-permute-start | bytes 3145736 | tf_op jit(solution)/shard_map/ppermute | solution.py:266
  174.2 44.4 %copy-start.12 = (s32[128,1]{0,1:T(1,128)S(1)}, s32[128,1]{0,1:T(1,128)}, u32[]{:S(2)}) copy-start(s32[128,1]{0,1:T(1,128)} %param.9) | copy-start | bytes 1540
  174.2 44.4 %copy-start.13 = (s32[128]{0:T(128)S(1)}, s32[128]{0:T(128)}, u32[]{:S(2)}) copy-start(s32[128]{0:T(128)} %param.11) | copy-start | bytes 1540
  174.2 44.4 %copy-start.14 = (s32[128]{0:T(128)S(1)}, s32[128]{0:T(128)}, u32[]{:S(2)}) copy-start(s32[128]{0:T(128)} %param.10) | copy-start | bytes 1540
  174.2 26.6 %collective-permute-start.21 = (f32[4,8,8192]{2,1,0:T(8,128)S(1)}, f32[4,8,8192]{2,1,0:T(8,128)S(1)}, u32[]{:S(2)}, u32[]{:S(2)}) collective-permute-start(f32[4,8,8192]{2,1,0:T(8,128)S(1)} %pad_maximum_fusion.2), channel_id=1, source_target_pairs={{0,8},{1,9},{2,10},{3,11},{4,12},{5,13},{6,14},{7,15},{8,16},{9,17... | collective-permute-start | bytes 3145736 | tf_op jit(solution)/shard_map/ppermute | solution.py:267
  175.4 25.5 %collective-permute-start.23 = (f32[4,8,8192]{2,1,0:T(8,128)S(1)}, f32[4,8,8192]{2,1,0:T(8,128)S(1)}, u32[]{:S(2)}, u32[]{:S(2)}) collective-permute-start(f32[4,8,8192]{2,1,0:T(8,128)S(1)} %pad_maximum_fusion.3), channel_id=1, source_target_pairs={{0,24},{1,25},{2,26},{3,27},{4,28},{5,29},{6,30},{7,31},{8,0},{9,1... | collective-permute-start | bytes 3145736 | tf_op jit(solution)/shard_map/ppermute | solution.py:267
  195.7 14.8 %collective-permute-start.17 = (f32[8,8192]{1,0:T(8,128)S(1)}, f32[8,8192]{1,0:T(8,128)S(1)}, u32[]{:S(2)}, u32[]{:S(2)}) collective-permute-start(f32[8,8192]{1,0:T(8,128)S(1)} %get-tuple-element.81), channel_id=1, source_target_pairs={{0,8},{1,9},{2,10},{3,11},{4,12},{5,13},{6,14},{7,15},{8,16},{9,17... | collective-permute-start | bytes 786440 | tf_op jit(solution)/shard_map/ppermute | solution.py:270
  196.7 14.6 %collective-permute-start.18 = (f32[8,8192]{1,0:T(8,128)S(1)}, f32[8,8192]{1,0:T(8,128)S(1)}, u32[]{:S(2)}, u32[]{:S(2)}) collective-permute-start(f32[8,8192]{1,0:T(8,128)S(1)} %get-tuple-element.83), channel_id=1, source_target_pairs={{0,24},{1,25},{2,26},{3,27},{4,28},{5,29},{6,30},{7,31},{8,0},{9,1... | collective-permute-start | bytes 786440 | tf_op jit(solution)/shard_map/ppermute | solution.py:270
  199.0 12.2 %collective-permute-start.19 = (f32[8,8192]{1,0:T(8,128)S(1)}, f32[8,8192]{1,0:T(8,128)S(1)}, u32[]{:S(2)}, u32[]{:S(2)}) collective-permute-start(f32[8,8192]{1,0:T(8,128)S(1)} %get-tuple-element.82), channel_id=1, source_target_pairs={{0,16},{1,17},{2,18},{3,19},{4,20},{5,21},{6,22},{7,23},{8,24},{9,... | collective-permute-start | bytes 786440 | tf_op jit(solution)/shard_map/ppermute | solution.py:270
  200.9 10.4 %collective-permute-start.24 = (f32[8,8192]{1,0:T(8,128)S(1)}, f32[8,8192]{1,0:T(8,128)S(1)}, u32[]{:S(2)}, u32[]{:S(2)}) collective-permute-start(f32[8,8192]{1,0:T(8,128)S(1)} %get-tuple-element.84), channel_id=1, source_target_pairs={{0,2},{1,3},{2,4},{3,5},{4,6},{5,7},{6,0},{7,1},{8,10},{9,11},{10,... | collective-permute-start | bytes 786440 | tf_op jit(solution)/shard_map/ppermute | solution.py:271
  201.0 10.3 %collective-permute-start.25 = (f32[8,8192]{1,0:T(8,128)S(1)}, f32[8,8192]{1,0:T(8,128)S(1)}, u32[]{:S(2)}, u32[]{:S(2)}) collective-permute-start(f32[8,8192]{1,0:T(8,128)S(1)} %get-tuple-element.86), channel_id=1, source_target_pairs={{0,6},{1,7},{2,0},{3,1},{4,2},{5,3},{6,4},{7,5},{8,14},{9,15},{10,... | collective-permute-start | bytes 786440 | tf_op jit(solution)/shard_map/ppermute | solution.py:271
  210.5 7.9 %collective-permute-start.26 = (f32[8,8192]{1,0:T(8,128)S(1)}, f32[8,8192]{1,0:T(8,128)S(1)}, u32[]{:S(2)}, u32[]{:S(2)}) collective-permute-start(f32[8,8192]{1,0:T(8,128)S(1)} %get-tuple-element.85), channel_id=1, source_target_pairs={{0,4},{1,5},{2,6},{3,7},{4,0},{5,1},{6,2},{7,3},{8,12},{9,13},{10,... | collective-permute-start | bytes 786440 | tf_op jit(solution)/shard_map/ppermute | solution.py:271
  218.8 0.8 copy-start.7
Sparse Core Ops, SparseCore 0:
  9.5 74.0 all-gather.2
